TPU v7x, 32 devices: a whole 2x2x4 slice. The times are simulated.
32 devices in a mesh: section: 4 (over x, core), dp: 8 (over z, y).
Axes of the slice: x: 2, y: 2, z: 4, core: 2. Of those that a mesh axis runs over, the one named last changes fastest.
Arguments:
- inputs: float32 [65536, 256], P('dp'), may hold values from -6 to 6
- targets: float32 [4, 65536, 256], P('section', 'dp'), may hold values from -6 to 6
- lengths: int32 [65536], P('dp'), may hold values from 1 to 4, as said below
- lat_index: int32 [65536], P('dp'), may hold values from 0 to 127
- land: int32 [65536], P('dp'), may hold values from 0 to 1
- w_up: float32 [4, 2, 256, 256], P('section'), may hold values from -0.375 to 0.375
- w_down: float32 [4, 2, 256, 256], P('section'), may hold values from -0.375 to 0.375
- gains: float32 [4, 2, 256], P('section'), may hold values from 0.5 to 1.5
- m_up: float32 [4, 2, 256, 256], P('section'), may hold values from -7.6293945e-05 to 7.6293945e-05
- m_down: float32 [4, 2, 256, 256], P('section'), may hold values from -7.6293945e-05 to 7.6293945e-05
- m_gains: float32 [4, 2, 256], P('section'), may hold values from -0.00024414062 to 0.00024414062
- v_up: float32 [4, 2, 256, 256], P('section'), may hold values from 2.3795382e-12 to 9.518153e-12
- v_down: float32 [4, 2, 256, 256], P('section'), may hold values from 2.3795382e-12 to 9.518153e-12
- v_gains: float32 [4, 2, 256], P('section'), may hold values from 2.1415845e-11 to 8.566338e-11
Outputs:
- loss_sum: float32 [], replicated
- weight_sum: float32 [], replicated
- grad_norm: float32 [], replicated
- new_up: float32 [4, 2, 256, 256], P('section')
- new_down: float32 [4, 2, 256, 256], P('section')
- new_gains: float32 [4, 2, 256], P('section')
- new_m_up: float32 [4, 2, 256, 256], P('section')
- new_m_down: float32 [4, 2, 256, 256], P('section')
- new_m_gains: float32 [4, 2, 256], P('section')
- new_v_up: float32 [4, 2, 256, 256], P('section')
- new_v_down: float32 [4, 2, 256, 256], P('section')
- new_v_gains: float32 [4, 2, 256], P('section')
Inputs may be any that keep to these rules, and one draw needn't show every extreme that they name: `lengths`: some column has length 4.
All inputs are finite; a program needn't handle non-finite values.
Results may differ from a plain program's by a relative error of at most 0.0035.
Values sent between devices are 32-bit elements; how exact they have to be, the bound alone decides.
A program may use at most 128 MiB of HBM per device.

v0:
```python
import math

import jax
import jax.numpy as jnp
from jax import lax
from jax.sharding import PartitionSpec as P

MICRO = 8
NLAT = 128
STEP = 10


norm_eps = 1e-06
clip_limit = 0.05
beta_one = 0.9
beta_two = 0.999
adam_eps = 1e-08
learn_rate = 0.1
weight_decay = 0.01


def shifted(shard, axis, by):
    size = lax.axis_size(axis)
    pairs = [(i, i + by) for i in range(size) if 0 <= i + by < size]
    return lax.ppermute(shard, axis, pairs)


def area_weight(lat_index, land):
    latitude = (lat_index.astype(jnp.float32) + 0.5) * (math.pi / NLAT) - math.pi / 2
    return jnp.cos(latitude) * (1.0 + land.astype(jnp.float32))


def norm_part(state, gain_one):
    scale_inv = lax.rsqrt(jnp.mean(state * state, -1, keepdims=True) + norm_eps)
    return state * scale_inv * gain_one


def block_forward(state, up_one, down_one, gain_one):
    normed = norm_part(state, gain_one).astype(jnp.bfloat16)
    pre_act = jnp.dot(normed, up_one, preferred_element_type=jnp.float32)
    hidden = jax.nn.silu(pre_act).astype(jnp.bfloat16)
    branch = jnp.dot(hidden, down_one, preferred_element_type=jnp.float32)
    return (state + branch, normed, pre_act, hidden)


def block_backward(state, normed, pre_act, hidden, up_one, down_one, gain_one, cotangent):
    grad_low = cotangent.astype(jnp.bfloat16)
    grad_down = jnp.dot(hidden.T, grad_low, preferred_element_type=jnp.float32)
    grad_hidden = jnp.dot(grad_low, down_one.T, preferred_element_type=jnp.float32)
    sigmoid_pre = jax.nn.sigmoid(pre_act)
    grad_pre = (grad_hidden * sigmoid_pre * (1.0 + pre_act * (1.0 - sigmoid_pre))).astype(
        jnp.bfloat16
    )
    grad_up = jnp.dot(normed.T, grad_pre, preferred_element_type=jnp.float32)
    grad_normed = jnp.dot(grad_pre, up_one.T, preferred_element_type=jnp.float32)
    unused, norm_pull = jax.vjp(norm_part, state, gain_one)
    grad_state, grad_gain = norm_pull(grad_normed)
    return (cotangent + grad_state, grad_up, grad_down, grad_gain)


def adam_step(weights_old, gradient, moment_one, moment_two, decay_rate):
    moment_one = beta_one * moment_one + (1.0 - beta_one) * gradient
    moment_two = beta_two * moment_two + (1.0 - beta_two) * gradient * gradient
    first_hat = moment_one / (1.0 - beta_one**STEP)
    second_hat = moment_two / (1.0 - beta_two**STEP)
    new_weights = weights_old - learn_rate * (
        first_hat / (jnp.sqrt(second_hat) + adam_eps) + decay_rate * weights_old
    )
    return (new_weights, moment_one, moment_two)


def per_device(
    inputs,
    targets,
    lengths,
    lat_index,
    land,
    w_up,
    w_down,
    gains,
    m_up,
    m_down,
    m_gains,
    v_up,
    v_down,
    v_gains,
):
    section_id = lax.axis_index("section")
    section_count = lax.axis_size("section")
    micro_rows = inputs.shape[0] // MICRO
    loss_weight = area_weight(lat_index, land) * (section_id < lengths).astype(jnp.float32)
    target_all = targets[0]
    up_low = w_up[0].astype(jnp.bfloat16)
    down_low = w_down[0].astype(jnp.bfloat16)
    gain_all = gains[0]
    layer_count = up_low.shape[0]
    tick_count = MICRO + section_count - 1

    def take_rows(array, slot_id):
        return lax.dynamic_slice_in_dim(array, slot_id * micro_rows, micro_rows, 0)

    local_weight = jnp.sum(loss_weight)
    weight_sum = lax.psum(local_weight, ("section", "dp"))

    def forward_tick(time_step, state_carry):
        received, saved, accumulated = state_carry
        micro_id = time_step - section_id
        is_valid = (micro_id >= 0) & (micro_id < MICRO)
        slot_id = jnp.clip(micro_id, 0, MICRO - 1)
        state = jnp.where(section_id == 0, take_rows(inputs, slot_id), received)
        kept_in = jnp.where(is_valid, state, saved[slot_id])
        saved = lax.dynamic_update_index_in_dim(saved, kept_in, slot_id, 0)
        moved = state
        for layer_id in range(layer_count):
            moved = block_forward(moved, up_low[layer_id], down_low[layer_id], gain_all[layer_id])[
                0
            ]
        diff = moved - take_rows(target_all, slot_id)
        term = jnp.sum(take_rows(loss_weight, slot_id) * jnp.sum(diff * diff, -1))
        accumulated = accumulated + jnp.where(is_valid, term, 0.0)
        received = shifted(moved, "section", 1)
        return (received, saved, accumulated)

    start_carry = (
        jnp.zeros((micro_rows, inputs.shape[1]), jnp.float32),
        jnp.zeros((MICRO, micro_rows, inputs.shape[1]), jnp.float32),
        jnp.zeros((), jnp.float32),
    )
    received, saved, local_loss = lax.fori_loop(0, tick_count, forward_tick, start_carry)
    loss_sum = lax.psum(local_loss, ("section", "dp"))

    def backward_tick(time_step, state_carry):
        received, sum_up, sum_down, sum_gain = state_carry
        micro_id = time_step - (section_count - 1 - section_id)
        is_valid = (micro_id >= 0) & (micro_id < MICRO)
        slot_id = jnp.clip(micro_id, 0, MICRO - 1)
        state = saved[slot_id]
        kept_layers = []
        for layer_id in range(layer_count):
            next_state, normed, pre_act, hidden = block_forward(
                state, up_low[layer_id], down_low[layer_id], gain_all[layer_id]
            )
            kept_layers.append((state, normed, pre_act, hidden))
            state = next_state
        cotangent = (
            2.0
            * take_rows(loss_weight, slot_id)[:, None]
            * (state - take_rows(target_all, slot_id))
            / weight_sum
            + received
        )
        ups = [None] * layer_count
        downs = [None] * layer_count
        gains_list = [None] * layer_count
        for layer_id in reversed(range(layer_count)):
            layer_in, normed, pre_act, hidden = kept_layers[layer_id]
            cotangent, ups[layer_id], downs[layer_id], gains_list[layer_id] = block_backward(
                layer_in,
                normed,
                pre_act,
                hidden,
                up_low[layer_id],
                down_low[layer_id],
                gain_all[layer_id],
                cotangent,
            )
        cotangent, ups, downs, gains_here = (
            cotangent,
            jnp.stack(ups),
            jnp.stack(downs),
            jnp.stack(gains_list),
        )
        live_factor = is_valid.astype(jnp.float32)
        sum_up = sum_up + live_factor * ups
        sum_down = sum_down + live_factor * downs
        sum_gain = sum_gain + live_factor * gains_here
        received = shifted(cotangent, "section", -1)
        return (received, sum_up, sum_down, sum_gain)

    back_carry = (
        jnp.zeros((micro_rows, inputs.shape[1]), jnp.float32),
        jnp.zeros(w_up.shape[1:], jnp.float32),
        jnp.zeros(w_down.shape[1:], jnp.float32),
        jnp.zeros(gains.shape[1:], jnp.float32),
    )
    unused, grad_up, grad_down, grad_gain = lax.fori_loop(0, tick_count, backward_tick, back_carry)
    grad_up, grad_down, grad_gain = (grad_up[None], grad_down[None], grad_gain[None])
    grad_up, grad_down, grad_gain = lax.psum((grad_up, grad_down, grad_gain), "dp")
    local_squares = (
        jnp.sum(grad_up * grad_up) + jnp.sum(grad_down * grad_down) + jnp.sum(grad_gain * grad_gain)
    )
    grad_norm = jnp.sqrt(lax.psum(local_squares, "section"))
    clip_scale = jnp.minimum(1.0, clip_limit / grad_norm)
    new_up, new_m_up, new_v_up = adam_step(w_up, grad_up * clip_scale, m_up, v_up, weight_decay)
    new_down, new_m_down, new_v_down = adam_step(
        w_down, grad_down * clip_scale, m_down, v_down, weight_decay
    )
    new_gains, new_m_gains, new_v_gains = adam_step(
        gains, grad_gain * clip_scale, m_gains, v_gains, 0.0
    )
    return (
        loss_sum,
        weight_sum,
        grad_norm,
        new_up,
        new_down,
        new_gains,
        new_m_up,
        new_m_down,
        new_m_gains,
        new_v_up,
        new_v_down,
        new_v_gains,
    )


def solution(mesh):
    return jax.shard_map(
        per_device,
        mesh=mesh,
        in_specs=(
            P("dp", None),
            P("section", "dp", None),
            P("dp"),
            P("dp"),
            P("dp"),
            P("section", None, None, None),
            P("section", None, None, None),
            P("section", None, None),
            P("section", None, None, None),
            P("section", None, None, None),
            P("section", None, None),
            P("section", None, None, None),
            P("section", None, None, None),
            P("section", None, None),
        ),
        out_specs=(
            P(),
            P(),
            P(),
            P("section", None, None, None),
            P("section", None, None, None),
            P("section", None, None),
            P("section", None, None, None),
            P("section", None, None, None),
            P("section", None, None),
            P("section", None, None, None),
            P("section", None, None, None),
            P("section", None, None),
        ),
        check_vma=False,
    )
```

profile of v0, /device:TPU:0, one launch (start us, length us, event | category | flops | bytes accessed | tf_op | source)
XLA Modules:
  0.0 814.8 jit_solution(8372536558686232013)
XLA Ops:
  7.3 9.0 %copy.31 = f32[1,8192,256]{1,2,0:T(8,128)} copy(f32[1,8192,256]{2,1,0:T(8,128)} %param.19) | data formatting | bytes 16777216 | tf_op args[1]
  17.9 4.3 broadcast_in_dim.59
  23.2 279.5 %while.40 = (s32[]{:T(128)}, f32[1024,256]{0,1:T(8,128)}, f32[8,1024,256]{1,2,0:T(8,128)}, f32[]{:T(128)}, pred[]{:T(512)}, /*index=5*/s32[]{:T(128)}, f32[8192,...) while((s32[]{:T(128)}, f32[1024,256]{0,1:T(8,128)}, ...), condition=%wide.region_5.6_spmd, body=%wide.region_0.5_spmd.sunk | while | flops 543951872 | bytes 28887944 | solution.py:129
  31.4 3.6 collective-permute-start
  46.3 15.3 %collective-permute-start = (f32[1024,256]{0,1:T(8,128)S(1)}, f32[1024,256]{0,1:T(8,128)S(1)}, u32[]{:S(2)}, u32[]{:S(2)}) collective-permute-start(f32[1024,256]{0,1:T(8,128)S(1)} %get-tuple-element.854), channel_id=1, source_target_pairs={{0,8},{8,16},{16,24},{1,9},{9,17},{17,25},{2,10},{10,18},{18,26},{... | collective-permute-start | bytes 3145736 | tf_op jit(solution)/shard_map/while/body/eval_jaxpr/ppermute | solution.py:25
  73.0 15.1 %collective-permute-start = (f32[1024,256]{0,1:T(8,128)S(1)}, f32[1024,256]{0,1:T(8,128)S(1)}, u32[]{:S(2)}, u32[]{:S(2)}) collective-permute-start(f32[1024,256]{0,1:T(8,128)S(1)} %get-tuple-element.854), channel_id=1, source_target_pairs={{0,8},{8,16},{16,24},{1,9},{9,17},{17,25},{2,10},{10,18},{18,26},{... | collective-permute-start | bytes 3145736 | tf_op jit(solution)/shard_map/while/body/eval_jaxpr/ppermute | solution.py:25
  99.4 15.2 %collective-permute-start = (f32[1024,256]{0,1:T(8,128)S(1)}, f32[1024,256]{0,1:T(8,128)S(1)}, u32[]{:S(2)}, u32[]{:S(2)}) collective-permute-start(f32[1024,256]{0,1:T(8,128)S(1)} %get-tuple-element.854), channel_id=1, source_target_pairs={{0,8},{8,16},{16,24},{1,9},{9,17},{17,25},{2,10},{10,18},{18,26},{... | collective-permute-start | bytes 3145736 | tf_op jit(solution)/shard_map/while/body/eval_jaxpr/ppermute | solution.py:25
  126.0 15.0 %collective-permute-start = (f32[1024,256]{0,1:T(8,128)S(1)}, f32[1024,256]{0,1:T(8,128)S(1)}, u32[]{:S(2)}, u32[]{:S(2)}) collective-permute-start(f32[1024,256]{0,1:T(8,128)S(1)} %get-tuple-element.854), channel_id=1, source_target_pairs={{0,8},{8,16},{16,24},{1,9},{9,17},{17,25},{2,10},{10,18},{18,26},{... | collective-permute-start | bytes 3145736 | tf_op jit(solution)/shard_map/while/body/eval_jaxpr/ppermute | solution.py:25
  152.3 15.2 %collective-permute-start = (f32[1024,256]{0,1:T(8,128)S(1)}, f32[1024,256]{0,1:T(8,128)S(1)}, u32[]{:S(2)}, u32[]{:S(2)}) collective-permute-start(f32[1024,256]{0,1:T(8,128)S(1)} %get-tuple-element.854), channel_id=1, source_target_pairs={{0,8},{8,16},{16,24},{1,9},{9,17},{17,25},{2,10},{10,18},{18,26},{... | collective-permute-start | bytes 3145736 | tf_op jit(solution)/shard_map/while/body/eval_jaxpr/ppermute | solution.py:25
  178.8 15.0 %collective-permute-start = (f32[1024,256]{0,1:T(8,128)S(1)}, f32[1024,256]{0,1:T(8,128)S(1)}, u32[]{:S(2)}, u32[]{:S(2)}) collective-permute-start(f32[1024,256]{0,1:T(8,128)S(1)} %get-tuple-element.854), channel_id=1, source_target_pairs={{0,8},{8,16},{16,24},{1,9},{9,17},{17,25},{2,10},{10,18},{18,26},{... | collective-permute-start | bytes 3145736 | tf_op jit(solution)/shard_map/while/body/eval_jaxpr/ppermute | solution.py:25
  205.1 15.2 %collective-permute-start = (f32[1024,256]{0,1:T(8,128)S(1)}, f32[1024,256]{0,1:T(8,128)S(1)}, u32[]{:S(2)}, u32[]{:S(2)}) collective-permute-start(f32[1024,256]{0,1:T(8,128)S(1)} %get-tuple-element.854), channel_id=1, source_target_pairs={{0,8},{8,16},{16,24},{1,9},{9,17},{17,25},{2,10},{10,18},{18,26},{... | collective-permute-start | bytes 3145736 | tf_op jit(solution)/shard_map/while/body/eval_jaxpr/ppermute | solution.py:25
  231.6 15.1 %collective-permute-start = (f32[1024,256]{0,1:T(8,128)S(1)}, f32[1024,256]{0,1:T(8,128)S(1)}, u32[]{:S(2)}, u32[]{:S(2)}) collective-permute-start(f32[1024,256]{0,1:T(8,128)S(1)} %get-tuple-element.854), channel_id=1, source_target_pairs={{0,8},{8,16},{16,24},{1,9},{9,17},{17,25},{2,10},{10,18},{18,26},{... | collective-permute-start | bytes 3145736 | tf_op jit(solution)/shard_map/while/body/eval_jaxpr/ppermute | solution.py:25
  258.0 15.1 %collective-permute-start = (f32[1024,256]{0,1:T(8,128)S(1)}, f32[1024,256]{0,1:T(8,128)S(1)}, u32[]{:S(2)}, u32[]{:S(2)}) collective-permute-start(f32[1024,256]{0,1:T(8,128)S(1)} %get-tuple-element.854), channel_id=1, source_target_pairs={{0,8},{8,16},{16,24},{1,9},{9,17},{17,25},{2,10},{10,18},{18,26},{... | collective-permute-start | bytes 3145736 | tf_op jit(solution)/shard_map/while/body/eval_jaxpr/ppermute | solution.py:25
  284.4 15.1 %collective-permute-start = (f32[1024,256]{0,1:T(8,128)S(1)}, f32[1024,256]{0,1:T(8,128)S(1)}, u32[]{:S(2)}, u32[]{:S(2)}) collective-permute-start(f32[1024,256]{0,1:T(8,128)S(1)} %get-tuple-element.854), channel_id=1, source_target_pairs={{0,8},{8,16},{16,24},{1,9},{9,17},{17,25},{2,10},{10,18},{18,26},{... | collective-permute-start | bytes 3145736 | tf_op jit(solution)/shard_map/while/body/eval_jaxpr/ppermute | solution.py:25
  302.8 54.1 %all-reduce = (f32[]{:T(128)}, f32[]{:T(128)}) all-reduce(f32[]{:T(128)} %get-tuple-element.544, f32[]{:T(128)} %get-tuple-element.672), channel_id=1, replica_groups=mesh['section'=4,'dp'=8] {'section','dp'}, use_global_device_ids=true, to_apply=%region_6.7 | all-reduce | flops 2 | bytes 16 | tf_op jit(solution)/shard_map/psum | solution.py:130
  358.0 341.1 %while.41 = (s32[]{:T(128)}, f32[1024,256]{0,1:T(8,128)}, f32[2,256,256]{2,1,0:T(8,128)}, f32[2,256,256]{2,1,0:T(8,128)}, f32[2,256]{1,0:T(2,128)S(1)}, /*index=...) while((s32[]{:T(128)}, f32[1024,256]{0,1:T(8,128)}, ...), condition=%wide.region_16.17_spmd.clone, body=%wide.region_9.16_spmd.clone.sunk | while | flops 1634744832 | bytes 77726384 | solution.py:186
  406.6 4.1 collective-permute-done.1
  434.5 8.2 %collective-permute-done.1 = f32[1024,256]{0,1:T(8,128)} collective-permute-done((f32[1024,256]{0,1:T(8,128)}, f32[1024,256]{0,1:T(8,128)}, u32[]{:S(2)}, u32[]{:S(2)}) %collective-permute-start.1) | collective-permute-done | bytes 1048608 | tf_op jit(solution)/shard_map/while/body/eval_jaxpr/ppermute | solution.py:25
  466.6 8.2 %collective-permute-done.1 = f32[1024,256]{0,1:T(8,128)} collective-permute-done((f32[1024,256]{0,1:T(8,128)}, f32[1024,256]{0,1:T(8,128)}, u32[]{:S(2)}, u32[]{:S(2)}) %collective-permute-start.1) | collective-permute-done | bytes 1048608 | tf_op jit(solution)/shard_map/while/body/eval_jaxpr/ppermute | solution.py:25
  481.2 2.8 fusion.145
  498.6 8.2 %collective-permute-done.1 = f32[1024,256]{0,1:T(8,128)} collective-permute-done((f32[1024,256]{0,1:T(8,128)}, f32[1024,256]{0,1:T(8,128)}, u32[]{:S(2)}, u32[]{:S(2)}) %collective-permute-start.1) | collective-permute-done | bytes 1048608 | tf_op jit(solution)/shard_map/while/body/eval_jaxpr/ppermute | solution.py:25
  530.7 8.2 %collective-permute-done.1 = f32[1024,256]{0,1:T(8,128)} collective-permute-done((f32[1024,256]{0,1:T(8,128)}, f32[1024,256]{0,1:T(8,128)}, u32[]{:S(2)}, u32[]{:S(2)}) %collective-permute-start.1) | collective-permute-done | bytes 1048608 | tf_op jit(solution)/shard_map/while/body/eval_jaxpr/ppermute | solution.py:25
  562.7 8.2 %collective-permute-done.1 = f32[1024,256]{0,1:T(8,128)} collective-permute-done((f32[1024,256]{0,1:T(8,128)}, f32[1024,256]{0,1:T(8,128)}, u32[]{:S(2)}, u32[]{:S(2)}) %collective-permute-start.1) | collective-permute-done | bytes 1048608 | tf_op jit(solution)/shard_map/while/body/eval_jaxpr/ppermute | solution.py:25
  594.7 8.2 %collective-permute-done.1 = f32[1024,256]{0,1:T(8,128)} collective-permute-done((f32[1024,256]{0,1:T(8,128)}, f32[1024,256]{0,1:T(8,128)}, u32[]{:S(2)}, u32[]{:S(2)}) %collective-permute-start.1) | collective-permute-done | bytes 1048608 | tf_op jit(solution)/shard_map/while/body/eval_jaxpr/ppermute | solution.py:25
  626.8 8.2 %collective-permute-done.1 = f32[1024,256]{0,1:T(8,128)} collective-permute-done((f32[1024,256]{0,1:T(8,128)}, f32[1024,256]{0,1:T(8,128)}, u32[]{:S(2)}, u32[]{:S(2)}) %collective-permute-start.1) | collective-permute-done | bytes 1048608 | tf_op jit(solution)/shard_map/while/body/eval_jaxpr/ppermute | solution.py:25
  658.8 8.2 %collective-permute-done.1 = f32[1024,256]{0,1:T(8,128)} collective-permute-done((f32[1024,256]{0,1:T(8,128)}, f32[1024,256]{0,1:T(8,128)}, u32[]{:S(2)}, u32[]{:S(2)}) %collective-permute-start.1) | collective-permute-done | bytes 1048608 | tf_op jit(solution)/shard_map/while/body/eval_jaxpr/ppermute | solution.py:25
  690.9 8.2 %collective-permute-done.1 = f32[1024,256]{0,1:T(8,128)} collective-permute-done((f32[1024,256]{0,1:T(8,128)}, f32[1024,256]{0,1:T(8,128)}, u32[]{:S(2)}, u32[]{:S(2)}) %collective-permute-start.1) | collective-permute-done | bytes 1048608 | tf_op jit(solution)/shard_map/while/body/eval_jaxpr/ppermute | solution.py:25
  699.1 19.6 %psum.46 = f32[1,2,256]{2,1,0:T(2,128)S(1)} all-reduce(f32[1,2,256]{2,1,0:T(2,128)S(1)} %bitcast.182), channel_id=1, replica_groups=mesh['section'=4,'dp'=8] {'dp'}, use_global_device_ids=true, to_apply=%region_21.22 | all-reduce | flops 512 | bytes 4096 | tf_op jit(solution)/shard_map/psum | solution.py:188
  719.3 68.4 %all-reduce.4.cloned.1.call-done = (f32[1,2,256,256]{3,2,1,0:T(8,128)}, f32[1,2,256,256]{3,2,1,0:T(8,128)}) async-done(((f32[1,2,256,256]{3,2,1,0:T(8,128)}, f32[1,2,256,256]{3,2,1,0:T(8,128)}), (f32[1,2,256,256]{3,2,1,0:T(8,128)}, f32[1,2,256,256]{3,2,1,0:T(8,128)})) %all-reduce.4.cloned.1.call-update) | async-done | bytes 1048592 | tf_op jit(solution)/shard_map/psum | solution.py:188
  793.2 6.4 psum.47
  801.0 2.9 multiply_subtract_fusion
  803.9 2.9 multiply_subtract_fusion.1
  (689 shorter events, 382.4 us)
Async XLA Ops:
  7.2 780.6 %all-reduce.4.cloned.1.call-start = ((), (), s32[]{:S(2)}) async-start(), calls=%async_computation | async-start | bytes 2097152 | tf_op jit(solution)/shard_map/psum | solution.py:188
  7.3 9.1 %copy-start.10 = (f32[1,2,256,256]{3,2,1,0:T(8,128)S(1)}, f32[1,2,256,256]{3,2,1,0:T(8,128)}, u32[]{:S(2)}) copy-start(f32[1,2,256,256]{3,2,1,0:T(8,128)} %param.24) | copy-start | bytes 1572868
  7.3 9.1 %copy-start.11 = (f32[1,2,256,256]{3,2,1,0:T(8,128)S(1)}, f32[1,2,256,256]{3,2,1,0:T(8,128)}, u32[]{:S(2)}) copy-start(f32[1,2,256,256]{3,2,1,0:T(8,128)} %param.23) | copy-start | bytes 1572868
  7.3 9.8 %copy-start.15 = (s32[8192]{0:T(1024)S(1)}, s32[8192]{0:T(1024)}, u32[]{:S(2)}) copy-start(s32[8192]{0:T(1024)} %param.22) | copy-start | bytes 98308
  7.3 9.8 %copy-start.16 = (s32[8192]{0:T(1024)S(1)}, s32[8192]{0:T(1024)}, u32[]{:S(2)}) copy-start(s32[8192]{0:T(1024)} %param.21) | copy-start | bytes 98308
  7.3 9.8 %copy-start.17 = (s32[8192]{0:T(1024)S(1)}, s32[8192]{0:T(1024)}, u32[]{:S(2)}) copy-start(s32[8192]{0:T(1024)} %param.20) | copy-start | bytes 98308
  31.4 5.9 collective-permute-start
  46.3 17.6 %collective-permute-start = (f32[1024,256]{0,1:T(8,128)S(1)}, f32[1024,256]{0,1:T(8,128)S(1)}, u32[]{:S(2)}, u32[]{:S(2)}) collective-permute-start(f32[1024,256]{0,1:T(8,128)S(1)} %get-tuple-element.854), channel_id=1, source_target_pairs={{0,8},{8,16},{16,24},{1,9},{9,17},{17,25},{2,10},{10,18},{18,26},{... | collective-permute-start | bytes 3145736 | tf_op jit(solution)/shard_map/while/body/eval_jaxpr/ppermute | solution.py:25
  73.0 17.3 %collective-permute-start = (f32[1024,256]{0,1:T(8,128)S(1)}, f32[1024,256]{0,1:T(8,128)S(1)}, u32[]{:S(2)}, u32[]{:S(2)}) collective-permute-start(f32[1024,256]{0,1:T(8,128)S(1)} %get-tuple-element.854), channel_id=1, source_target_pairs={{0,8},{8,16},{16,24},{1,9},{9,17},{17,25},{2,10},{10,18},{18,26},{... | collective-permute-start | bytes 3145736 | tf_op jit(solution)/shard_map/while/body/eval_jaxpr/ppermute | solution.py:25
  99.4 17.4 %collective-permute-start = (f32[1024,256]{0,1:T(8,128)S(1)}, f32[1024,256]{0,1:T(8,128)S(1)}, u32[]{:S(2)}, u32[]{:S(2)}) collective-permute-start(f32[1024,256]{0,1:T(8,128)S(1)} %get-tuple-element.854), channel_id=1, source_target_pairs={{0,8},{8,16},{16,24},{1,9},{9,17},{17,25},{2,10},{10,18},{18,26},{... | collective-permute-start | bytes 3145736 | tf_op jit(solution)/shard_map/while/body/eval_jaxpr/ppermute | solution.py:25
  126.0 17.3 %collective-permute-start = (f32[1024,256]{0,1:T(8,128)S(1)}, f32[1024,256]{0,1:T(8,128)S(1)}, u32[]{:S(2)}, u32[]{:S(2)}) collective-permute-start(f32[1024,256]{0,1:T(8,128)S(1)} %get-tuple-element.854), channel_id=1, source_target_pairs={{0,8},{8,16},{16,24},{1,9},{9,17},{17,25},{2,10},{10,18},{18,26},{... | collective-permute-start | bytes 3145736 | tf_op jit(solution)/shard_map/while/body/eval_jaxpr/ppermute | solution.py:25
  152.3 17.4 %collective-permute-start = (f32[1024,256]{0,1:T(8,128)S(1)}, f32[1024,256]{0,1:T(8,128)S(1)}, u32[]{:S(2)}, u32[]{:S(2)}) collective-permute-start(f32[1024,256]{0,1:T(8,128)S(1)} %get-tuple-element.854), channel_id=1, source_target_pairs={{0,8},{8,16},{16,24},{1,9},{9,17},{17,25},{2,10},{10,18},{18,26},{... | collective-permute-start | bytes 3145736 | tf_op jit(solution)/shard_map/while/body/eval_jaxpr/ppermute | solution.py:25
  178.8 17.2 %collective-permute-start = (f32[1024,256]{0,1:T(8,128)S(1)}, f32[1024,256]{0,1:T(8,128)S(1)}, u32[]{:S(2)}, u32[]{:S(2)}) collective-permute-start(f32[1024,256]{0,1:T(8,128)S(1)} %get-tuple-element.854), channel_id=1, source_target_pairs={{0,8},{8,16},{16,24},{1,9},{9,17},{17,25},{2,10},{10,18},{18,26},{... | collective-permute-start | bytes 3145736 | tf_op jit(solution)/shard_map/while/body/eval_jaxpr/ppermute | solution.py:25
  205.1 17.4 %collective-permute-start = (f32[1024,256]{0,1:T(8,128)S(1)}, f32[1024,256]{0,1:T(8,128)S(1)}, u32[]{:S(2)}, u32[]{:S(2)}) collective-permute-start(f32[1024,256]{0,1:T(8,128)S(1)} %get-tuple-element.854), channel_id=1, source_target_pairs={{0,8},{8,16},{16,24},{1,9},{9,17},{17,25},{2,10},{10,18},{18,26},{... | collective-permute-start | bytes 3145736 | tf_op jit(solution)/shard_map/while/body/eval_jaxpr/ppermute | solution.py:25
  231.6 17.3 %collective-permute-start = (f32[1024,256]{0,1:T(8,128)S(1)}, f32[1024,256]{0,1:T(8,128)S(1)}, u32[]{:S(2)}, u32[]{:S(2)}) collective-permute-start(f32[1024,256]{0,1:T(8,128)S(1)} %get-tuple-element.854), channel_id=1, source_target_pairs={{0,8},{8,16},{16,24},{1,9},{9,17},{17,25},{2,10},{10,18},{18,26},{... | collective-permute-start | bytes 3145736 | tf_op jit(solution)/shard_map/while/body/eval_jaxpr/ppermute | solution.py:25
  258.0 17.3 %collective-permute-start = (f32[1024,256]{0,1:T(8,128)S(1)}, f32[1024,256]{0,1:T(8,128)S(1)}, u32[]{:S(2)}, u32[]{:S(2)}) collective-permute-start(f32[1024,256]{0,1:T(8,128)S(1)} %get-tuple-element.854), channel_id=1, source_target_pairs={{0,8},{8,16},{16,24},{1,9},{9,17},{17,25},{2,10},{10,18},{18,26},{... | collective-permute-start | bytes 3145736 | tf_op jit(solution)/shard_map/while/body/eval_jaxpr/ppermute | solution.py:25
  284.4 17.3 %collective-permute-start = (f32[1024,256]{0,1:T(8,128)S(1)}, f32[1024,256]{0,1:T(8,128)S(1)}, u32[]{:S(2)}, u32[]{:S(2)}) collective-permute-start(f32[1024,256]{0,1:T(8,128)S(1)} %get-tuple-element.854), channel_id=1, source_target_pairs={{0,8},{8,16},{16,24},{1,9},{9,17},{17,25},{2,10},{10,18},{18,26},{... | collective-permute-start | bytes 3145736 | tf_op jit(solution)/shard_map/while/body/eval_jaxpr/ppermute | solution.py:25
  358.0 442.4 %copy-start.18 = (f32[1,2,256]{2,1,0:T(2,128)S(1)}, f32[1,2,256]{2,1,0:T(2,128)}, u32[]{:S(2)}) copy-start(f32[1,2,256]{2,1,0:T(2,128)} %param.28) | copy-start | bytes 6148
  358.0 442.4 %copy-start.19 = (f32[1,2,256]{2,1,0:T(2,128)S(1)}, f32[1,2,256]{2,1,0:T(2,128)}, u32[]{:S(2)}) copy-start(f32[1,2,256]{2,1,0:T(2,128)} %param.31) | copy-start | bytes 6148
  373.6 8.2 %collective-permute-start.1 = (f32[1024,256]{0,1:T(8,128)}, f32[1024,256]{0,1:T(8,128)}, u32[]{:S(2)}, u32[]{:S(2)}) collective-permute-start(f32[1024,256]{0,1:T(8,128)} %fusion.149), channel_id=1, source_target_pairs={{8,0},{16,8},{24,16},{9,1},{17,9},{25,17},{10,2},{18,10},{26,18},{... | collective-permute-start | bytes 3145736 | tf_op jit(solution)/shard_map/while/body/eval_jaxpr/ppermute | solution.py:25
  398.4 12.3 %collective-permute-start.1 = (f32[1024,256]{0,1:T(8,128)}, f32[1024,256]{0,1:T(8,128)}, u32[]{:S(2)}, u32[]{:S(2)}) collective-permute-start(f32[1024,256]{0,1:T(8,128)} %fusion.149), channel_id=1, source_target_pairs={{8,0},{16,8},{24,16},{9,1},{17,9},{25,17},{10,2},{18,10},{26,18},{... | collective-permute-start | bytes 3145736 | tf_op jit(solution)/shard_map/while/body/eval_jaxpr/ppermute | solution.py:25
  426.3 16.4 %collective-permute-start.1 = (f32[1024,256]{0,1:T(8,128)}, f32[1024,256]{0,1:T(8,128)}, u32[]{:S(2)}, u32[]{:S(2)}) collective-permute-start(f32[1024,256]{0,1:T(8,128)} %fusion.149), channel_id=1, source_target_pairs={{8,0},{16,8},{24,16},{9,1},{17,9},{25,17},{10,2},{18,10},{26,18},{... | collective-permute-start | bytes 3145736 | tf_op jit(solution)/shard_map/while/body/eval_jaxpr/ppermute | solution.py:25
  434.5 8.2 %copy-start.7 = (f32[2,256,256]{2,1,0:T(8,128)}, f32[2,256,256]{2,1,0:T(8,128)S(1)}, u32[]{:S(2)}) copy-start(f32[2,256,256]{2,1,0:T(8,128)S(1)} %get-tuple-element.979) | copy-start | bytes 1572868 | tf_op jit(solution)/shard_map/while
  458.4 16.4 %collective-permute-start.1 = (f32[1024,256]{0,1:T(8,128)}, f32[1024,256]{0,1:T(8,128)}, u32[]{:S(2)}, u32[]{:S(2)}) collective-permute-start(f32[1024,256]{0,1:T(8,128)} %fusion.149), channel_id=1, source_target_pairs={{8,0},{16,8},{24,16},{9,1},{17,9},{25,17},{10,2},{18,10},{26,18},{... | collective-permute-start | bytes 3145736 | tf_op jit(solution)/shard_map/while/body/eval_jaxpr/ppermute | solution.py:25
  466.6 8.2 %copy-start.7 = (f32[2,256,256]{2,1,0:T(8,128)}, f32[2,256,256]{2,1,0:T(8,128)S(1)}, u32[]{:S(2)}) copy-start(f32[2,256,256]{2,1,0:T(8,128)S(1)} %get-tuple-element.979) | copy-start | bytes 1572868 | tf_op jit(solution)/shard_map/while
  490.4 16.4 %collective-permute-start.1 = (f32[1024,256]{0,1:T(8,128)}, f32[1024,256]{0,1:T(8,128)}, u32[]{:S(2)}, u32[]{:S(2)}) collective-permute-start(f32[1024,256]{0,1:T(8,128)} %fusion.149), channel_id=1, source_target_pairs={{8,0},{16,8},{24,16},{9,1},{17,9},{25,17},{10,2},{18,10},{26,18},{... | collective-permute-start | bytes 3145736 | tf_op jit(solution)/shard_map/while/body/eval_jaxpr/ppermute | solution.py:25
  522.4 16.4 %collective-permute-start.1 = (f32[1024,256]{0,1:T(8,128)}, f32[1024,256]{0,1:T(8,128)}, u32[]{:S(2)}, u32[]{:S(2)}) collective-permute-start(f32[1024,256]{0,1:T(8,128)} %fusion.149), channel_id=1, source_target_pairs={{8,0},{16,8},{24,16},{9,1},{17,9},{25,17},{10,2},{18,10},{26,18},{... | collective-permute-start | bytes 3145736 | tf_op jit(solution)/shard_map/while/body/eval_jaxpr/ppermute | solution.py:25
  554.5 16.4 %collective-permute-start.1 = (f32[1024,256]{0,1:T(8,128)}, f32[1024,256]{0,1:T(8,128)}, u32[]{:S(2)}, u32[]{:S(2)}) collective-permute-start(f32[1024,256]{0,1:T(8,128)} %fusion.149), channel_id=1, source_target_pairs={{8,0},{16,8},{24,16},{9,1},{17,9},{25,17},{10,2},{18,10},{26,18},{... | collective-permute-start | bytes 3145736 | tf_op jit(solution)/shard_map/while/body/eval_jaxpr/ppermute | solution.py:25
  586.5 16.4 %collective-permute-start.1 = (f32[1024,256]{0,1:T(8,128)}, f32[1024,256]{0,1:T(8,128)}, u32[]{:S(2)}, u32[]{:S(2)}) collective-permute-start(f32[1024,256]{0,1:T(8,128)} %fusion.149), channel_id=1, source_target_pairs={{8,0},{16,8},{24,16},{9,1},{17,9},{25,17},{10,2},{18,10},{26,18},{... | collective-permute-start | bytes 3145736 | tf_op jit(solution)/shard_map/while/body/eval_jaxpr/ppermute | solution.py:25
  618.6 16.4 %collective-permute-start.1 = (f32[1024,256]{0,1:T(8,128)}, f32[1024,256]{0,1:T(8,128)}, u32[]{:S(2)}, u32[]{:S(2)}) collective-permute-start(f32[1024,256]{0,1:T(8,128)} %fusion.149), channel_id=1, source_target_pairs={{8,0},{16,8},{24,16},{9,1},{17,9},{25,17},{10,2},{18,10},{26,18},{... | collective-permute-start | bytes 3145736 | tf_op jit(solution)/shard_map/while/body/eval_jaxpr/ppermute | solution.py:25
  650.6 16.4 %collective-permute-start.1 = (f32[1024,256]{0,1:T(8,128)}, f32[1024,256]{0,1:T(8,128)}, u32[]{:S(2)}, u32[]{:S(2)}) collective-permute-start(f32[1024,256]{0,1:T(8,128)} %fusion.149), channel_id=1, source_target_pairs={{8,0},{16,8},{24,16},{9,1},{17,9},{25,17},{10,2},{18,10},{26,18},{... | collective-permute-start | bytes 3145736 | tf_op jit(solution)/shard_map/while/body/eval_jaxpr/ppermute | solution.py:25
  682.7 16.4 %collective-permute-start.1 = (f32[1024,256]{0,1:T(8,128)}, f32[1024,256]{0,1:T(8,128)}, u32[]{:S(2)}, u32[]{:S(2)}) collective-permute-start(f32[1024,256]{0,1:T(8,128)} %fusion.149), channel_id=1, source_target_pairs={{8,0},{16,8},{24,16},{9,1},{17,9},{25,17},{10,2},{18,10},{26,18},{... | collective-permute-start | bytes 3145736 | tf_op jit(solution)/shard_map/while/body/eval_jaxpr/ppermute | solution.py:25
  (131 other events, 467.1 us)
Sparse Core Ops, SparseCore 0:
  699.2 88.4 all-reduce.3
where the time goes:
time: 822 us; the launch traced here: 815 us
  matrix products  221 us (27%)
  starting transfers between devices  169 us (21%)
  waiting for transfers between devices  157 us (19%)
  other arithmetic  85.6 us (10%)
  blocking collectives  80.1 us (10%)
  local copies, waits for them, and re-layouts  73.4 us (9%)
  between operations  18 us (2%)
  loops' own time  10.9 us (1%)
    ppermute x22, starting transfers between devices, shifted(): return lax.ppermute(shard, axis, pairs)  169 us
    dot_general x44, matrix products, block_forward(): branch = jnp.dot(hidden, down_one, preferred_element_type=jnp.float32)  91.4 us
    ppermute x22, waiting for transfers between devices, shifted(): return lax.ppermute(shard, axis, pairs)  88.2 us
    psum x1, waiting for transfers between devices, per_device(): lax.psum((grad_up, grad_down, grad_gain), 'dp')  68.4 us
    psum x1, blocking collectives, per_device(): loss_sum = lax.psum(local_loss, ('section', 'dp'))  54.1 us
    dot_general x22, matrix products, block_backward(): grad_down = jnp.dot(hidden.T, grad_low, preferred_element_type=jnp.float32)  41.1 us
    add x22, other arithmetic, block_backward(): return (cotangent + grad_state, grad_up, grad_down, grad_gain)  31.1 us
    dot_general x22, matrix products, block_backward(): grad_up = jnp.dot(normed.T, grad_pre, preferred_element_type=jnp.float32)  29.1 us
  transfers between devices with their start and end apart: 23, of which 22 were waited for; matrix products, arithmetic and copies ran while one was open for 10% of the time, Pallas kernels for 0%

commit v1 on v0

--- a/solution.py
+++ b/solution.py
@@ -1,14 +1,16 @@
+import functools
 import math
 
 import jax
 import jax.numpy as jnp
 from jax import lax
+from jax.experimental import pallas as pl
+from jax.experimental.pallas import tpu as pltpu
 from jax.sharding import PartitionSpec as P
 
 MICRO = 8
 NLAT = 128
 STEP = 10
-
 
 norm_eps = 1e-06
 clip_limit = 0.05
@@ -18,6 +20,532 @@
 learn_rate = 0.1
 weight_decay = 0.01
 
+f32, bf16 = jnp.float32, jnp.bfloat16
+MESH = pl.DeviceIdType.MESH
+LANES = 128
+ROWS = 512
+WINDOW = 1536
+RING = 11
+QRING = 8
+
+
+def dot(a, b):
+    return jnp.dot(a, b, preferred_element_type=f32)
+
+
+def dot_lhs_t(a, b):
+    return lax.dot_general(a, b, (((0,), (0,)), ((), ())), preferred_element_type=f32)
+
+
+def split_dot(product, onehot, values):
+    high = values.astype(bf16)
+    low = (values - high.astype(f32)).astype(bf16)
+    return product(onehot, high) + product(onehot, low)
+
+
+def rollout_kernel(
+    sections,
+    groups,
+    inputs_ref,
+    target_ref,
+    len_ref,
+    lat_ref,
+    land_ref,
+    up_ref,
+    down_ref,
+    gain_ref,
+    dup_ref,
+    ddown_ref,
+    dgain_ref,
+    stat_ref,
+    xin,
+    xout,
+    cin,
+    tgt,
+    packed,
+    save_x,
+    save_h,
+    save_d,
+    qring,
+    up_lo,
+    up_t,
+    down_lo,
+    down_t,
+    rank_ref,
+    q_ref,
+    scale_ref,
+    loss_acc,
+    gain_acc,
+    wbuf,
+    spread,
+    in_sem,
+    tgt_sem,
+    st_send,
+    st_recv,
+    ct_send,
+    ct_recv,
+    w_send,
+    w_recv,
+):
+    section = lax.axis_index("section")
+    dp = lax.axis_index("dp")
+    columns = xin.shape[0]
+    feats = xin.shape[1]
+    chunks = columns // ROWS
+    live_rows = ROWS * (sections - 2) // sections
+    prows = live_rows + 16
+    total_packed = chunks * prows
+    expand = live_rows + 512
+    natural = section < 2
+    last = sections - 1
+
+    barrier = pltpu.get_barrier_semaphore()
+
+    @pl.when(section > 0)
+    def _():
+        pl.semaphore_signal(barrier, inc=1, device_id=(section - 1, dp), device_id_type=MESH)
+
+    @pl.when(section < last)
+    def _():
+        pl.semaphore_signal(barrier, inc=1, device_id=(section + 1, dp), device_id_type=MESH)
+
+    for step in range(1, groups):
+        pl.semaphore_signal(
+            barrier, inc=1, device_id=(section, lax.rem(dp + step, groups)), device_id_type=MESH
+        )
+
+    def rows_at(index, size, align=16):
+        return pl.ds(pl.multiple_of(index, align), size)
+
+    def input_copy(i):
+        rows = rows_at(i * ROWS, ROWS)
+        return pltpu.make_async_copy(inputs_ref.at[rows], xin.at[rows], in_sem.at[i])
+
+    def target_copy(i):
+        rows = rows_at(i * ROWS, ROWS)
+        return pltpu.make_async_copy(target_ref.at[rows], tgt.at[rows], tgt_sem.at[i])
+
+    @pl.when(section == 0)
+    def _():
+        @pl.loop(0, chunks)
+        def _(i):
+            input_copy(i).start()
+
+    @pl.loop(0, chunks)
+    def _(i):
+        target_copy(i).start()
+
+    for layer in range(2):
+        up = up_ref[layer]
+        down = down_ref[layer]
+        up_lo[layer] = (0.5 * up).astype(bf16)
+        down_lo[layer] = down.astype(bf16)
+        up_t[layer] = up.T.astype(bf16)
+        down_t[layer] = (0.5 * down).T.astype(bf16)
+        dup_ref[layer] = jnp.zeros((feats, feats), f32)
+        ddown_ref[layer] = jnp.zeros((feats, feats), f32)
+        gain_acc[layer] = jnp.zeros((8, feats), f32)
+    loss_acc[...] = jnp.zeros_like(loss_acc)
+
+    grid_rows = columns // LANES
+    length = len_ref[...]
+    latitude = (lat_ref[...].astype(f32) + 0.5) * (math.pi / NLAT) - math.pi / 2
+    area = jnp.cos(latitude) * (1.0 + land_ref[...].astype(f32))
+    q_ref[...] = area * (section < length).astype(f32)
+    local_weight = jnp.sum(
+        area * jnp.minimum(length, sections).astype(f32), axis=(0, 1), keepdims=True
+    )
+    beyond = length > 2
+    flag = beyond.astype(bf16)
+    lane_a = lax.broadcasted_iota(jnp.int32, (LANES, LANES), 0)
+    lane_b = lax.broadcasted_iota(jnp.int32, (LANES, LANES), 1)
+    within = dot(flag, (lane_a < lane_b).astype(bf16))
+    row_total = jnp.sum(flag.astype(f32), axis=1, keepdims=True)
+    row_a = lax.broadcasted_iota(jnp.int32, (grid_rows, grid_rows), 0)
+    row_b = lax.broadcasted_iota(jnp.int32, (grid_rows, grid_rows), 1)
+    before = dot(
+        (row_b < row_a).astype(bf16), jnp.broadcast_to(row_total, (grid_rows, LANES)).astype(bf16)
+    )
+    rank = jnp.where(beyond, within + before, -1e6)
+    rank_ref[...] = rank
+
+    def window_start(j):
+        first = (j * (prows * sections) // (sections - 2) - 448) // LANES * LANES
+        return jnp.clip(first, 0, columns - WINDOW)
+
+    def expand_start(k):
+        return jnp.clip(live_rows * k - 256, 0, total_packed - expand)
+
+    place = (
+        lax.broadcasted_iota(jnp.int32, (grid_rows, LANES), 0) * LANES
+        + lax.broadcasted_iota(jnp.int32, (grid_rows, LANES), 1)
+    )
+    rank_i = rank.astype(jnp.int32)
+    missed = beyond & (rank_i >= total_packed)
+    for j in range(chunks):
+        start = min(
+            max((j * (prows * sections) // (sections - 2) - 448) // LANES * LANES, 0),
+            columns - WINDOW,
+        )
+        member = (rank_i >= j * prows) & (rank_i < (j + 1) * prows)
+        missed |= member & ((place < start) | (place >= start + WINDOW))
+    row_chunk = lax.broadcasted_iota(jnp.int32, (grid_rows, LANES), 0) // (ROWS // LANES)
+    row_start = jnp.clip(live_rows * row_chunk - 256, 0, total_packed - expand)
+    missed |= beyond & ((rank_i < row_start) | (rank_i >= row_start + expand))
+    misses = jnp.sum(missed.astype(f32), axis=(0, 1), keepdims=True)
+    tile_row = lax.broadcasted_iota(jnp.int32, (8, LANES), 0)
+    wbuf[dp] = jnp.where(tile_row < 4, local_weight, misses)
+
+    chain = jnp.where((section > 0) & (section < last), 2, 1)
+    pl.semaphore_wait(barrier, groups - 1 + chain)
+
+    def weight_copy(step):
+        return pltpu.make_async_remote_copy(
+            src_ref=wbuf.at[dp],
+            dst_ref=wbuf.at[dp],
+            send_sem=w_send.at[step],
+            recv_sem=w_recv.at[step],
+            device_id=(section, lax.rem(dp + step, groups)),
+            device_id_type=MESH,
+        )
+
+    for step in range(1, groups):
+        weight_copy(step).start()
+
+    def finish_weights():
+        for step in range(1, groups):
+            weight_copy(step).wait_recv()
+        total = wbuf[0]
+        for peer in range(1, groups):
+            total = total + wbuf[peer]
+        stat_ref[...] = total
+        scale_ref[...] = 2.0 / jnp.broadcast_to(total[0:1], (8, LANES))
+
+    def pack_matrix(j):
+        start = window_start(j)
+        base = (j * prows).astype(f32)
+        target_row = lax.broadcasted_iota(jnp.int32, (prows, LANES), 0).astype(f32)
+        first = start // LANES
+        hits = []
+        for i in range(WINDOW // LANES):
+            hits.append(target_row == rank_ref[pl.ds(first + i, 1), :] - base)
+        return start, first, hits
+
+    def as_onehot(hits):
+        return jnp.concatenate([jnp.where(hit, 1.0, 0.0).astype(bf16) for hit in hits], axis=1)
+
+    def unpack_rows(k):
+        start = expand_start(k)
+        base = start.astype(f32)
+        source_row = lax.broadcasted_iota(jnp.int32, (expand, LANES), 0).astype(f32)
+        hits = []
+        for i in range(ROWS // LANES):
+            hits.append(source_row == rank_ref[pl.ds(k * (ROWS // LANES) + i, 1), :] - base)
+        return split_dot(dot_lhs_t, as_onehot(hits), cin[rows_at(start, expand), :])
+
+    def forward(size, rows, saved):
+        x = xin[rows, :]
+        for layer in range(2):
+            if layer == 1:
+                save_x[saved, :] = x
+            r = lax.rsqrt(jnp.mean(x * x, -1, keepdims=True) + norm_eps)
+            normed = (x * r * gain_ref[layer : layer + 1]).astype(bf16)
+            half = dot(normed, up_lo[layer])
+            t = jnp.tanh(half)
+            a = 1.0 + t
+            h = half * a
+            hidden = h.astype(bf16)
+            save_h[layer, saved, :] = hidden
+            save_d[layer, saved, :] = (a + h * (1.0 - t)).astype(bf16)
+            x = x + dot(hidden, down_lo[layer])
+        xout[rows, :] = x
+
+    def loss_part(size, diff, weight):
+        weighted = jnp.concatenate(
+            [diff[:, :LANES] * weight, diff[:, LANES:] * weight], axis=1
+        )
+        loss_acc[...] += jnp.sum((weighted * diff).reshape(size // 8, 8, feats), 0)
+        return weighted * scale_ref[0:1, 0:1]
+
+    def backward(size, rows, saved, g):
+        for layer in (1, 0):
+            low = g.astype(bf16)
+            ddown_ref[layer] += dot_lhs_t(save_h[layer, saved, :], low)
+            pull = dot(low, down_t[layer])
+            g_pre = (pull * save_d[layer, saved, :].astype(f32)).astype(bf16)
+            x = save_x[saved, :] if layer == 1 else xin[rows, :]
+            r = lax.rsqrt(jnp.mean(x * x, -1, keepdims=True) + norm_eps)
+            gain = gain_ref[layer : layer + 1]
+            xr = x * r
+            normed = (xr * gain).astype(bf16)
+            dup_ref[layer] += dot_lhs_t(normed, g_pre)
+            g_normed = dot(g_pre, up_t[layer])
+            prod = g_normed * xr
+            gain_acc[layer] += jnp.sum(prod.reshape(size // 8, 8, feats), 0)
+            mean = jnp.mean(prod * gain, -1, keepdims=True)
+            g = g + r * (gain * g_normed - xr * mean)
+        xin[rows, :] = g
+
+    def state_copy(source, size, i):
+        rows = rows_at(i * size, size)
+        return pltpu.make_async_remote_copy(
+            src_ref=source.at[rows],
+            dst_ref=xin.at[rows],
+            send_sem=st_send.at[i],
+            recv_sem=st_recv.at[i],
+            device_id=(jnp.minimum(section + 1, last), dp),
+            device_id_type=MESH,
+        )
+
+    def cot_copy(size, i):
+        rows = rows_at(i * size, size)
+        return pltpu.make_async_remote_copy(
+            src_ref=xin.at[rows],
+            dst_ref=cin.at[rows],
+            send_sem=ct_send.at[i],
+            recv_sem=ct_recv.at[i],
+            device_id=(jnp.maximum(section - 1, 0), dp),
+            device_id_type=MESH,
+        )
+
+    @pl.when(natural)
+    def _():
+        lag = jnp.where(section == 0, RING - 1, RING - 3)
+
+        @pl.loop(0, chunks + RING - 1)
+        def _(t):
+            @pl.when(t < chunks)
+            def _():
+                @pl.when(section == 0)
+                def _():
+                    input_copy(t).wait()
+
+                @pl.when(section > 0)
+                def _():
+                    state_copy(xout, ROWS, t).wait_recv()
+
+                rows = rows_at(t * ROWS, ROWS)
+                saved = rows_at(lax.rem(t, RING) * ROWS, ROWS)
+                forward(ROWS, rows, saved)
+
+                @pl.when(section == 0)
+                def _():
+                    state_copy(xout, ROWS, t).start()
+
+            @pl.when((section == 1) & (t >= 2) & (t < chunks + 2))
+            def _():
+                j = t - 2
+                start, _, hits = pack_matrix(j)
+                packed[rows_at(j * prows, prows), :] = split_dot(
+                    dot, as_onehot(hits), xout[rows_at(start, WINDOW), :]
+                )
+                state_copy(packed, prows, j).start()
+
+            k = t - lag
+
+            @pl.when((k >= 0) & (k < chunks))
+            def _():
+                @pl.when(k == 0)
+                def _():
+                    finish_weights()
+
+                @pl.when(section == 0)
+                def _():
+                    cot_copy(ROWS, k).wait_recv()
+
+                @pl.when((section == 1) & (k == 0))
+                def _():
+                    cot_copy(prows, k).wait_recv()
+                    cot_copy(prows, k + 1).wait_recv()
+                    cot_copy(prows, k + 2).wait_recv()
+
+                @pl.when((section == 1) & (k >= 2) & (k + 1 < chunks))
+                def _():
+                    cot_copy(prows, k + 1).wait_recv()
+
+                target_copy(k).wait()
+                rows = rows_at(k * ROWS, ROWS)
+                saved = rows_at(lax.rem(k, RING) * ROWS, ROWS)
+
+                @pl.when(section == 1)
+                def _():
+                    cin_rows = unpack_rows(k)
+                    spread[...] = cin_rows
+
+                @pl.when(section == 0)
+                def _():
+                    spread[...] = cin[rows, :]
+
+                weight = jnp.concatenate(
+                    [
+                        jnp.broadcast_to(
+                            q_ref[pl.ds(k * (ROWS // LANES) + i, 1), :], (LANES, LANES)
+                        ).T
+                        for i in range(ROWS // LANES)
+                    ],
+                    axis=0,
+                )
+                diff = xout[rows, :] - tgt[rows, :]
+                g = loss_part(ROWS, diff, weight) + spread[...]
+                backward(ROWS, rows, saved, g)
+
+                @pl.when(section == 1)
+                def _():
+                    cot_copy(ROWS, k).start()
+
+        @pl.when(section == 0)
+        def _():
+            @pl.loop(0, chunks)
+            def _(i):
+                state_copy(xout, ROWS, i).wait_send()
+
+        @pl.when(section == 1)
+        def _():
+            @pl.loop(0, chunks)
+            def _(i):
+                state_copy(packed, prows, i).wait_send()
+                cot_copy(ROWS, i).wait_send()
+
+    @pl.when(jnp.logical_not(natural))
+    def _():
+        lag = last - section
+
+        @pl.loop(0, chunks + lag)
+        def _(t):
+            @pl.when(t < chunks)
+            def _():
+                @pl.when(t == 0)
+                def _():
+                    target_copy(0).wait()
+                    target_copy(1).wait()
+
+                @pl.when(t + 2 < chunks)
+                def _():
+                    target_copy(t + 2).wait()
+
+                start, first, hits = pack_matrix(t)
+                rows = rows_at(t * prows, prows)
+                packed[rows, :] = split_dot(dot, as_onehot(hits), tgt[rows_at(start, WINDOW), :])
+                weight = jnp.zeros((prows, LANES), f32)
+                for i, hit in enumerate(hits):
+                    weight += jnp.where(hit, q_ref[pl.ds(first + i, 1), :], 0.0)
+                qring[lax.rem(t, QRING)] = jnp.broadcast_to(
+                    jnp.sum(weight, -1, keepdims=True), (prows, LANES)
+                )
+                state_copy(xout, prows, t).wait_recv()
+                saved = rows_at(lax.rem(t, RING) * ROWS, prows)
+                forward(prows, rows, saved)
+
+                @pl.when(section < last)
+                def _():
+                    state_copy(xout, prows, t).start()
+
+            k = t - lag
+
+            @pl.when(k >= 0)
+            def _():
+                @pl.when(k == 0)
+                def _():
+                    finish_weights()
+
+                rows = rows_at(k * prows, prows)
+                saved = rows_at(lax.rem(k, RING) * ROWS, prows)
+                diff = xout[rows, :] - packed[rows, :]
+                spread[0:prows, :] = loss_part(prows, diff, qring[lax.rem(k, QRING)])
+
+                @pl.when(section < last)
+                def _():
+                    cot_copy(prows, k).wait_recv()
+                    spread[0:prows, :] += cin[rows, :]
+
+                backward(prows, rows, saved, spread[0:prows, :])
+                cot_copy(prows, k).start()
+
+        @pl.loop(0, chunks)
+        def _(i):
+            cot_copy(prows, i).wait_send()
+
+        @pl.when(section < last)
+        def _():
+            @pl.loop(0, chunks)
+            def _(i):
+                state_copy(xout, prows, i).wait_send()
+
+    for step in range(1, groups):
+        weight_copy(step).wait_send()
+    for layer in range(2):
+        dgain_ref[layer : layer + 1, :] = jnp.sum(gain_acc[layer], 0, keepdims=True)
+    loss = jnp.sum(loss_acc[...], axis=(0, 1), keepdims=True)
+    stat_ref[...] = jnp.where(tile_row < 2, loss, stat_ref[...])
+
+
+def rollout(inputs, target, lengths, lat_index, land, w_up, w_down, gains, sections, groups):
+    columns, feats = inputs.shape
+    chunks = columns // ROWS
+    prows = ROWS * (sections - 2) // sections + 16
+    grid_rows = columns // LANES
+    hbm = pl.BlockSpec(memory_space=pl.ANY)
+    vmem = pl.BlockSpec(memory_space=pltpu.VMEM)
+    square = jax.ShapeDtypeStruct((2, feats, feats), f32)
+    dma = pltpu.SemaphoreType.DMA
+    wide = pltpu.VMEM((columns, feats), f32)
+    lows = pltpu.VMEM((2, feats, feats), bf16)
+    flat = lambda array: array.reshape(grid_rows, LANES)
+    return pl.pallas_call(
+        functools.partial(rollout_kernel, sections, groups),
+        out_shape=(
+            square,
+            square,
+            jax.ShapeDtypeStruct((2, feats), f32),
+            jax.ShapeDtypeStruct((8, LANES), f32),
+        ),
+        in_specs=[hbm, hbm] + [vmem] * 6,
+        out_specs=(vmem,) * 4,
+        scratch_shapes=[
+            wide,
+            wide,
+            wide,
+            wide,
+            pltpu.VMEM((chunks * prows, feats), f32),
+            pltpu.VMEM((RING * ROWS, feats), f32),
+            pltpu.VMEM((2, RING * ROWS, feats), bf16),
+            pltpu.VMEM((2, RING * ROWS, feats), bf16),
+            pltpu.VMEM((QRING, prows, LANES), f32),
+            lows,
+            lows,
+            lows,
+            lows,
+            pltpu.VMEM((grid_rows, LANES), f32),
+            pltpu.VMEM((grid_rows, LANES), f32),
+            pltpu.VMEM((8, LANES), f32),
+            pltpu.VMEM((8, feats), f32),
+            pltpu.VMEM((2, 8, feats), f32),
+            pltpu.VMEM((groups, 8, LANES), f32),
+            pltpu.VMEM((ROWS, feats), f32),
+            dma((chunks,)),
+            dma((chunks,)),
+            dma((chunks,)),
+            dma((chunks,)),
+            dma((chunks,)),
+            dma((chunks,)),
+            dma((groups,)),
+            dma((groups,)),
+        ],
+        compiler_params=pltpu.CompilerParams(
+            collective_id=0, has_side_effects=True, vmem_limit_bytes=63 * 1024 * 1024
+        ),
+        name="rollout",
+    )(
+        inputs,
+        target,
+        flat(lengths),
+        flat(lat_index),
+        flat(land),
+        w_up,
+        w_down,
+        gains,
+    )
+
 
 def shifted(shard, axis, by):
     size = lax.axis_size(axis)
@@ -58,49 +586,15 @@
     return (cotangent + grad_state, grad_up, grad_down, grad_gain)
 
 
-def adam_step(weights_old, gradient, moment_one, moment_two, decay_rate):
-    moment_one = beta_one * moment_one + (1.0 - beta_one) * gradient
-    moment_two = beta_two * moment_two + (1.0 - beta_two) * gradient * gradient
-    first_hat = moment_one / (1.0 - beta_one**STEP)
-    second_hat = moment_two / (1.0 - beta_two**STEP)
-    new_weights = weights_old - learn_rate * (
-        first_hat / (jnp.sqrt(second_hat) + adam_eps) + decay_rate * weights_old
-    )
-    return (new_weights, moment_one, moment_two)
-
-
-def per_device(
-    inputs,
-    targets,
-    lengths,
-    lat_index,
-    land,
-    w_up,
-    w_down,
-    gains,
-    m_up,
-    m_down,
-    m_gains,
-    v_up,
-    v_down,
-    v_gains,
-):
+def plain_gradients(inputs, target_all, loss_weight, weight_sum, up_low, down_low, gain_all):
     section_id = lax.axis_index("section")
     section_count = lax.axis_size("section")
     micro_rows = inputs.shape[0] // MICRO
-    loss_weight = area_weight(lat_index, land) * (section_id < lengths).astype(jnp.float32)
-    target_all = targets[0]
-    up_low = w_up[0].astype(jnp.bfloat16)
-    down_low = w_down[0].astype(jnp.bfloat16)
-    gain_all = gains[0]
     layer_count = up_low.shape[0]
     tick_count = MICRO + section_count - 1
 
     def take_rows(array, slot_id):
         return lax.dynamic_slice_in_dim(array, slot_id * micro_rows, micro_rows, 0)
-
-    local_weight = jnp.sum(loss_weight)
-    weight_sum = lax.psum(local_weight, ("section", "dp"))
 
     def forward_tick(time_step, state_carry):
         received, saved, accumulated = state_carry
@@ -127,7 +621,6 @@
         jnp.zeros((), jnp.float32),
     )
     received, saved, local_loss = lax.fori_loop(0, tick_count, forward_tick, start_carry)
-    loss_sum = lax.psum(local_loss, ("section", "dp"))
 
     def backward_tick(time_step, state_carry):
         received, sum_up, sum_down, sum_gain = state_carry
@@ -179,11 +672,73 @@
 
     back_carry = (
         jnp.zeros((micro_rows, inputs.shape[1]), jnp.float32),
-        jnp.zeros(w_up.shape[1:], jnp.float32),
-        jnp.zeros(w_down.shape[1:], jnp.float32),
-        jnp.zeros(gains.shape[1:], jnp.float32),
+        jnp.zeros(up_low.shape, jnp.float32),
+        jnp.zeros(down_low.shape, jnp.float32),
+        jnp.zeros(gain_all.shape, jnp.float32),
     )
     unused, grad_up, grad_down, grad_gain = lax.fori_loop(0, tick_count, backward_tick, back_carry)
+    return grad_up, grad_down, grad_gain, local_loss
+
+
+def adam_step(weights_old, gradient, moment_one, moment_two, decay_rate):
+    moment_one = beta_one * moment_one + (1.0 - beta_one) * gradient
+    moment_two = beta_two * moment_two + (1.0 - beta_two) * gradient * gradient
+    first_hat = moment_one / (1.0 - beta_one**STEP)
+    second_hat = moment_two / (1.0 - beta_two**STEP)
+    new_weights = weights_old - learn_rate * (
+        first_hat / (jnp.sqrt(second_hat) + adam_eps) + decay_rate * weights_old
+    )
+    return (new_weights, moment_one, moment_two)
+
+
+def per_device(
+    inputs,
+    targets,
+    lengths,
+    lat_index,
+    land,
+    w_up,
+    w_down,
+    gains,
+    m_up,
+    m_down,
+    m_gains,
+    v_up,
+    v_down,
+    v_gains,
+):
+    section_id = lax.axis_index("section")
+    sections, groups = lax.axis_size("section"), lax.axis_size("dp")
+    fast_up, fast_down, fast_gain, stats = rollout(
+        inputs,
+        targets[0],
+        lengths,
+        lat_index,
+        land,
+        w_up[0],
+        w_down[0],
+        gains[0],
+        sections,
+        groups,
+    )
+    weight_sum = stats[2, 0]
+
+    def slow_path():
+        loss_weight = area_weight(lat_index, land) * (section_id < lengths).astype(jnp.float32)
+        return plain_gradients(
+            inputs,
+            targets[0],
+            loss_weight,
+            weight_sum,
+            w_up[0].astype(bf16),
+            w_down[0].astype(bf16),
+            gains[0],
+        )
+
+    grad_up, grad_down, grad_gain, local_loss = lax.cond(
+        stats[4, 0] > 0.0, slow_path, lambda: (fast_up, fast_down, fast_gain, stats[0, 0])
+    )
+    loss_sum = lax.psum(local_loss, ("section", "dp"))
     grad_up, grad_down, grad_gain = (grad_up[None], grad_down[None], grad_gain[None])
     grad_up, grad_down, grad_gain = lax.psum((grad_up, grad_down, grad_gain), "dp")
     local_squares = (

time: 822 us -> 242 us (0.29)
  matrix products: 221 us -> 0 us
  starting transfers between devices: 169 us -> 0.04 us
  waiting for transfers between devices: 157 us -> 56.4 us
  Pallas kernels: 0 us -> 91.5 us
  other arithmetic: 85.6 us -> 9.09 us
  local copies, waits for them, and re-layouts: 73.4 us -> 1.07 us
  blocking collectives: 80.1 us -> 64.7 us
  loops' own time: 10.9 us -> 0.01 us
    dot_general x154 -> x0, matrix products: 221 us -> none  [the longest x44 91.4 us: block_forward(): branch = jnp.dot(hidden, down_one, preferred_element_type=jnp.float32)]
    ppermute x22 -> x0, starting transfers between devices: 169 us -> none  [shifted(): return lax.ppermute(shard, axis, pairs)]
    pallas_call x0 -> x1, Pallas kernels: none -> 91.5 us  [rollout(): pl.pallas_call(functools.partial(rollout_kernel, sections, groups), out_s...]
    ppermute x22 -> x0, waiting for transfers between devices: 88.2 us -> none  [shifted(): return lax.ppermute(shard, axis, pairs)]
    add x44 -> x0, other arithmetic: 36 us -> none  [the longest x22 31.1 us: block_backward(): return (cotangent + grad_state, grad_up, grad_down, grad_gain)]
    dynamic_slice x33 -> x0, local copies, waits for them, and re-layouts: 32.2 us -> none  [the longest x22 17.9 us: take_rows(): return lax.dynamic_slice_in_dim(array, slot_id * micro_rows, micro_rows, 0)]
    while x264 -> x0, local copies, waits for them, and re-layouts: 25.6 us -> none
    reduce_sum x34 -> x0, other arithmetic: 23.5 us -> none  [the longest x22 16.1 us: norm_part(): scale_inv = lax.rsqrt(jnp.mean(state * state, -1, keepdims=True) + norm_eps)]
  transfers between devices with their start and end apart: 23 -> 1, of which waited for: 22 -> 1; matrix products, arithmetic and copies ran while one was open for 10% -> 0% of each run, Pallas kernels for 0% -> 0%
where the time goes in v1:
time: 242 us; the launch traced here: 241 us
  Pallas kernels  91.5 us (38%)
  blocking collectives  64.7 us (27%)
  waiting for transfers between devices  56.4 us (23%)
  between operations  18.6 us (8%)
  other arithmetic  9.09 us (4%)
    pallas_call x1, Pallas kernels, rollout(): pl.pallas_call(functools.partial(rollout_kernel, sections, groups), out_s...  91.5 us
    psum x1, waiting for transfers between devices, per_device(): lax.psum((grad_up, grad_down, grad_gain), 'dp')  56.4 us
    psum x1, blocking collectives, per_device(): loss_sum = lax.psum(local_loss, ('section', 'dp'))  39.9 us
    psum x1, blocking collectives, per_device(): lax.psum((grad_up, grad_down, grad_gain), 'dp')  18.5 us
    psum x1, blocking collectives, per_device(): grad_norm = jnp.sqrt(lax.psum(local_squares, 'section'))  6.33 us
    sub x2, other arithmetic, adam_step(): weights_old - learn_rate * (first_hat / (jnp.sqrt(second_hat) + adam_eps)...  4.93 us
  transfers between devices with their start and end apart: 1, of which 1 were waited for; matrix products, arithmetic and copies ran while one was open for 0% of the time, Pallas kernels for 0%

profile of v1, /device:TPU:0, one launch (start us, length us, event | category | flops | bytes accessed | tf_op | source)
XLA Modules:
  0.0 241.5 jit_solution(14681040939593919594)
XLA Ops:
  7.2 0.0 all-reduce.3.cloned.1.call-start
  7.2 0.0 copy-start.6
  7.2 0.0 copy-start.7
  7.2 0.0 copy-start.10
  7.3 0.0 copy-start.11
  7.3 0.0 copy-start.12
  7.3 91.5 %rollout.1 = (f32[2,256,256]{2,1,0:T(8,128)}, f32[2,256,256]{2,1,0:T(8,128)}, f32[2,256]{1,0:T(2,128)}, f32[8,128]{1,0:T(8,128)S(1)}) custom-call(f32[8192,256]{1,0:T(8,128)} %inputs_ref.1, f32[8192,256]{1,0:T(8,128)} %bitcast.177, s32[64,128]{1,0:T(8,128)} %bitcast.191, s32[64,128]{1,0:T(8,128)} %bitcast.192, s32[64,128]{1,0:T(8,128)} %bitcast.193, ...), custom_call_target="tpu_custom_call" | custom-call | tf_op jit(solution)/shard_map/rollout/pallas_call | solution.py:494
  98.8 0.5 fusion.87
  100.0 0.0 copy-done.6
  100.0 0.0 copy-done.7
  100.0 0.0 copy-done.10
  100.0 0.0 copy-done.11
  100.0 0.0 copy-done.12
  100.1 0.0 copy-start.13
  100.1 0.0 copy-start.14
  100.1 0.5 conditional.1
  100.1 0.5 slice.102
  100.6 0.0 all-reduce.3.cloned.1.call-update
  100.6 18.5 %psum.38 = f32[1,2,256]{2,1,0:T(2,128)S(1)} all-reduce(f32[1,2,256]{2,1,0:T(2,128)} %bitcast.24), channel_id=1, replica_groups=mesh['section'=4,'dp'=8] {'dp'}, use_global_device_ids=true, to_apply=%region_21.22 | all-reduce | flops 512 | bytes 4096 | tf_op jit(solution)/shard_map/psum | solution.py:743
  119.1 0.6 multiply_reduce_fusion.10
  119.7 56.4 %all-reduce.3.cloned.1.call-done = (f32[1,2,256,256]{3,2,1,0:T(8,128)}, f32[1,2,256,256]{3,2,1,0:T(8,128)}) async-done(((f32[1,2,256,256]{3,2,1,0:T(8,128)}, f32[1,2,256,256]{3,2,1,0:T(8,128)}), (f32[1,2,256,256]{3,2,1,0:T(8,128)}, f32[1,2,256,256]{3,2,1,0:T(8,128)})) %all-reduce.3.cloned.1.call-update) | async-done | bytes 1048592 | tf_op jit(solution)/shard_map/psum | solution.py:743
  176.1 1.8 multiply_reduce_fusion.8
  177.8 1.8 multiply_reduce_fusion.9
  181.6 39.9 %psum.35 = f32[]{:T(128)} all-reduce(f32[]{:T(128)} %get-tuple-element.598), channel_id=1, replica_groups=mesh['section'=4,'dp'=8] {'section','dp'}, use_global_device_ids=true, to_apply=%region_16.17 | all-reduce | flops 1 | bytes 8 | tf_op jit(solution)/shard_map/psum | solution.py:741
  221.5 6.3 %psum.39 = f32[]{:T(128)} all-reduce(f32[]{:T(128)S(6)} %add.347), channel_id=1, replica_groups=mesh['section'=4,'dp'=8] {'section'}, use_global_device_ids=true, to_apply=%region_23.24 | all-reduce | flops 1 | bytes 8 | tf_op jit(solution)/shard_map/psum | solution.py:747
  228.5 0.0 copy-done.13
  228.5 0.0 copy-done.14
  228.6 0.6 multiply_subtract_fusion.2
  229.2 4.3 %multiply_subtract_fusion = (f32[1,2,256,256]{3,2,1,0:T(8,128)}, f32[1,2,256,256]{3,2,1,0:T(8,128)}, f32[1,2,256,256]{3,2,1,0:T(8,128)}, f32[1,2,256,256]{3,2,1,...) fusion(f32[1,2,256,256]{3,2,1,0:T(8,128)} %param.26, f32[1,2,256,256]{3,2,1,0:T(8,128)} %get-tuple-element.709, ...), kind=kLoop, calls=%fused_computation.123 | loop fusion | flops 4194304 | bytes 7340036 | tf_op jit(solution)/shard_map/sub | solution.py:688
Async XLA Ops:
  7.2 168.9 %all-reduce.3.cloned.1.call-start = ((), (), s32[]{:S(2)}) async-start(), calls=%async_computation | async-start | bytes 2097152 | tf_op jit(solution)/shard_map/psum | solution.py:743
  7.2 92.8 %copy-start.6 = (f32[1,2,256,256]{3,2,1,0:T(8,128)S(1)}, f32[1,2,256,256]{3,2,1,0:T(8,128)}, u32[]{:S(2)}) copy-start(f32[1,2,256,256]{3,2,1,0:T(8,128)} %param.25) | copy-start | bytes 1572868
  7.2 92.8 %copy-start.7 = (f32[1,2,256]{2,1,0:T(2,128)S(1)}, f32[1,2,256]{2,1,0:T(2,128)}, u32[]{:S(2)}) copy-start(f32[1,2,256]{2,1,0:T(2,128)} %param.27) | copy-start | bytes 6148
  7.2 92.8 %copy-start.10 = (s32[8192]{0:T(1024)S(1)}, s32[8192]{0:T(1024)}, u32[]{:S(2)}) copy-start(s32[8192]{0:T(1024)} %param.22) | copy-start | bytes 98308
  7.3 92.8 %copy-start.11 = (s32[8192]{0:T(1024)S(1)}, s32[8192]{0:T(1024)}, u32[]{:S(2)}) copy-start(s32[8192]{0:T(1024)} %param.23) | copy-start | bytes 98308
  7.3 92.8 %copy-start.12 = (s32[8192]{0:T(1024)S(1)}, s32[8192]{0:T(1024)}, u32[]{:S(2)}) copy-start(s32[8192]{0:T(1024)} %param.24) | copy-start | bytes 98308
  100.1 128.5 %copy-start.13 = (f32[1,2,256]{2,1,0:T(2,128)S(1)}, f32[1,2,256]{2,1,0:T(2,128)}, u32[]{:S(2)}) copy-start(f32[1,2,256]{2,1,0:T(2,128)} %param.30) | copy-start | bytes 6148
  100.1 128.5 %copy-start.14 = (f32[1,2,256]{2,1,0:T(2,128)S(1)}, f32[1,2,256]{2,1,0:T(2,128)}, u32[]{:S(2)}) copy-start(f32[1,2,256]{2,1,0:T(2,128)} %param.33) | copy-start | bytes 6148
Sparse Core Ops, SparseCore 0:
  100.7 75.2 all-reduce.2

commit v2 on v1

v2 whole, which is shorter than its diff:
```python
import functools
import math

import jax
import jax.numpy as jnp
from jax import lax
from jax.experimental import pallas as pl
from jax.experimental.pallas import tpu as pltpu
from jax.sharding import PartitionSpec as P

NLAT = 128
STEP = 10

norm_eps = 1e-06
clip_limit = 0.05
beta_one = 0.9
beta_two = 0.999
adam_eps = 1e-08
learn_rate = 0.1
weight_decay = 0.01

f32, bf16 = jnp.float32, jnp.bfloat16
MESH = pl.DeviceIdType.MESH
LANES = 128
ROWS = 512
WINDOW = 1536
SAVE_BYTES = 21 * 1024 * 1024


def dot(a, b):
    return jnp.dot(a, b, preferred_element_type=f32)


def dot_lhs_t(a, b):
    return lax.dot_general(a, b, (((0,), (0,)), ((), ())), preferred_element_type=f32)


def split_dot(product, onehot, values):
    high = values.astype(bf16)
    low = (values - high.astype(f32)).astype(bf16)
    return product(onehot, high) + product(onehot, low)


def rollout_kernel(
    sections,
    groups,
    packing,
    inputs_ref,
    target_ref,
    len_ref,
    lat_ref,
    land_ref,
    up_ref,
    down_ref,
    gain_ref,
    grads_ref,
    dgain_ref,
    stat_ref,
    xin,
    xout,
    cin,
    tgt,
    packed,
    save_x,
    save_h,
    save_d,
    qring,
    up_lo,
    up_t,
    down_lo,
    down_t,
    rank_ref,
    q_ref,
    scale_ref,
    loss_acc,
    gain_acc,
    wbuf,
    spread,
    acc,
    final,
    ybuf,
    zbuf,
    small,
    tiny,
    in_sem,
    tgt_sem,
    st_send,
    st_recv,
    ct_send,
    ct_recv,
    w_send,
    w_recv,
    y_send,
    y_recv,
    z_send,
    z_recv,
    za_send,
    za_recv,
    ya_send,
    ya_recv,
    small_send,
    small_recv,
    tiny_send,
    tiny_recv,
    out_sem,
):
    section = lax.axis_index("section")
    dp = lax.axis_index("dp")
    columns = xin.shape[0]
    feats = xin.shape[1]
    chunks = columns // ROWS
    live_rows = ROWS * (sections - 2) // sections
    prows = live_rows + 16
    total_packed = chunks * prows
    expand = live_rows + 512
    last = sections - 1
    ring = save_x.shape[0] // ROWS
    natural = section < (2 if packing else sections)
    plain_next = (section == 0) if packing else (section < last)
    packs = (section == 1) if packing else (section < 0)

    def peer(step):
        return (section, lax.rem(dp + step, groups))

    barrier = pltpu.get_barrier_semaphore()
    for step in range(1, sections):
        other = lax.rem(section + step, sections)
        pl.semaphore_signal(barrier, inc=1, device_id=(other, dp), device_id_type=MESH)
    for step in range(1, groups):
        pl.semaphore_signal(barrier, inc=1, device_id=peer(step), device_id_type=MESH)

    def rows_at(index, size, align=16):
        return pl.ds(pl.multiple_of(index, align), size)

    def input_copy(i):
        rows = rows_at(i * ROWS, ROWS)
        return pltpu.make_async_copy(inputs_ref.at[rows], xin.at[rows], in_sem.at[i])

    def target_copy(i):
        rows = rows_at(i * ROWS, ROWS)
        return pltpu.make_async_copy(target_ref.at[rows], tgt.at[rows], tgt_sem.at[i])

    @pl.when(section == 0)
    def _():
        @pl.loop(0, chunks)
        def _(i):
            input_copy(i).start()

    @pl.loop(0, chunks)
    def _(i):
        target_copy(i).start()

    for layer in range(2):
        up_lo[layer] = (0.5 * up_ref[layer]).astype(bf16)
        down_lo[layer] = down_ref[layer].astype(bf16)

    def prepare_backward():
        for layer in range(2):
            up_t[layer] = up_ref[layer].T.astype(bf16)
            down_t[layer] = (0.5 * down_ref[layer]).T.astype(bf16)
            gain_acc[layer] = jnp.zeros((8, feats), f32)
        for i in range(4):
            acc[i] = jnp.zeros((feats, feats), f32)
        loss_acc[...] = jnp.zeros_like(loss_acc)

    grid_rows = columns // LANES
    tile_row = lax.broadcasted_iota(jnp.int32, (8, LANES), 0)

    def window_start(j):
        shift = jnp.where(j < 7, 0, jnp.where(j < 11, 256, 384))
        return jnp.clip(ROWS * (j - 1) + shift, 0, columns - WINDOW)

    def expand_start(k):
        return jnp.clip(live_rows * k - 256, 0, total_packed - expand)

    def weight_copy(step):
        return pltpu.make_async_remote_copy(
            src_ref=wbuf.at[dp],
            dst_ref=wbuf.at[dp],
            send_sem=w_send.at[step],
            recv_sem=w_recv.at[step],
            device_id=peer(step),
            device_id_type=MESH,
        )

    def prepare_columns():
        length = len_ref[...]
        latitude = (lat_ref[...].astype(f32) + 0.5) * (math.pi / NLAT) - math.pi / 2
        area = jnp.cos(latitude) * (1.0 + land_ref[...].astype(f32))
        q_ref[...] = area * (section < length).astype(f32)
        local_weight = jnp.sum(
            area * jnp.minimum(length, sections).astype(f32), axis=(0, 1), keepdims=True
        )
        misses = jnp.zeros((1, 1), f32)
        if packing:
            beyond = length > 2
            flag = beyond.astype(bf16)
            lane_a = lax.broadcasted_iota(jnp.int32, (LANES, LANES), 0)
            lane_b = lax.broadcasted_iota(jnp.int32, (LANES, LANES), 1)
            within = dot(flag, (lane_a < lane_b).astype(bf16))
            row_total = jnp.sum(flag.astype(f32), axis=1, keepdims=True)
            row_a = lax.broadcasted_iota(jnp.int32, (grid_rows, grid_rows), 0)
            row_b = lax.broadcasted_iota(jnp.int32, (grid_rows, grid_rows), 1)
            before = dot(
                (row_b < row_a).astype(bf16),
                jnp.broadcast_to(row_total, (grid_rows, LANES)).astype(bf16),
            )
            rank = jnp.where(beyond, within + before, -1e6)
            rank_ref[...] = rank
            place = (
                lax.broadcasted_iota(jnp.int32, (grid_rows, LANES), 0) * LANES
                + lax.broadcasted_iota(jnp.int32, (grid_rows, LANES), 1)
            )
            rank_i = rank.astype(jnp.int32)
            missed = beyond & (rank_i >= total_packed)
            for j in range(chunks):
                shift = 0 if j < 7 else 256 if j < 11 else 384
                start = min(max(ROWS * (j - 1) + shift, 0), columns - WINDOW)
                member = (rank_i >= j * prows) & (rank_i < (j + 1) * prows)
                ready = ROWS * (j + 2 if j < 7 else j + 3)
                missed |= member & ((place < start) | (place >= min(start + WINDOW, ready)))
            row_chunk = lax.broadcasted_iota(jnp.int32, (grid_rows, LANES), 0) // (ROWS // LANES)
            row_start = jnp.clip(live_rows * row_chunk - 256, 0, total_packed - expand)
            missed |= beyond & ((rank_i < row_start) | (rank_i >= row_start + expand))
            misses = jnp.sum(missed.astype(f32), axis=(0, 1), keepdims=True)
        wbuf[dp] = jnp.where(tile_row < 4, local_weight, misses)
        for step in range(1, groups):
            weight_copy(step).start()

    def finish_weights():
        for step in range(1, groups):
            weight_copy(step).wait_recv()
        total = wbuf[0]
        for other in range(1, groups):
            total = total + wbuf[other]
        stat_ref[...] = total
        scale_ref[...] = 2.0 / jnp.broadcast_to(total[0:1], (8, LANES))

    pl.semaphore_wait(barrier, sections - 1 + groups - 1)

    def pack_matrix(j):
        start = window_start(j)
        base = (j * prows).astype(f32)
        target_row = lax.broadcasted_iota(jnp.int32, (prows, LANES), 0).astype(f32)
        first = start // LANES
        hits = []
        for i in range(WINDOW // LANES):
            hits.append(target_row == rank_ref[pl.ds(first + i, 1), :] - base)
        return start, first, hits

    def as_onehot(hits):
        return jnp.concatenate([jnp.where(hit, 1.0, 0.0).astype(bf16) for hit in hits], axis=1)

    def unpack_rows(k):
        start = expand_start(k)
        base = start.astype(f32)
        source_row = lax.broadcasted_iota(jnp.int32, (expand, LANES), 0).astype(f32)
        hits = []
        for i in range(ROWS // LANES):
            hits.append(source_row == rank_ref[pl.ds(k * (ROWS // LANES) + i, 1), :] - base)
        return split_dot(dot_lhs_t, as_onehot(hits), cin[rows_at(start, expand), :])

    def forward(rows, saved):
        x = xin[rows, :]
        for layer in range(2):
            if layer == 1:
                save_x[saved, :] = x
            r = lax.rsqrt(jnp.mean(x * x, -1, keepdims=True) + norm_eps)
            normed = (x * r * gain_ref[layer : layer + 1]).astype(bf16)
            half = dot(normed, up_lo[layer])
            t = jnp.tanh(half)
            a = 1.0 + t
            h = half * a
            hidden = h.astype(bf16)
            save_h[layer, saved, :] = hidden
            save_d[layer, saved, :] = (a + h * (1.0 - t)).astype(bf16)
            x = x + dot(hidden, down_lo[layer])
        xout[rows, :] = x

    def loss_part(size, diff, weight):
        weighted = jnp.concatenate(
            [diff[:, :LANES] * weight, diff[:, LANES:] * weight], axis=1
        )
        loss_acc[...] += jnp.sum((weighted * diff).reshape(size // 8, 8, feats), 0)
        return weighted * scale_ref[0:1, 0:1]

    def backward(size, rows, saved, g):
        for layer in (1, 0):
            low = g.astype(bf16)
            acc[2 + layer] += dot_lhs_t(save_h[layer, saved, :], low)
            pull = dot(low, down_t[layer])
            g_pre = (pull * save_d[layer, saved, :].astype(f32)).astype(bf16)
            x = save_x[saved, :] if layer == 1 else xin[rows, :]
            r = lax.rsqrt(jnp.mean(x * x, -1, keepdims=True) + norm_eps)
            gain = gain_ref[layer : layer + 1]
            xr = x * r
            normed = (xr * gain).astype(bf16)
            acc[layer] += dot_lhs_t(normed, g_pre)
            g_normed = dot(g_pre, up_t[layer])
            prod = g_normed * xr
            gain_acc[layer] += jnp.sum(prod.reshape(size // 8, 8, feats), 0)
            mean = jnp.mean(prod * gain, -1, keepdims=True)
            g = g + r * (gain * g_normed - xr * mean)
        xin[rows, :] = g

    def state_copy(source, size, i):
        rows = rows_at(i * size, size)
        return pltpu.make_async_remote_copy(
            src_ref=source.at[rows],
            dst_ref=xin.at[rows],
            send_sem=st_send.at[i],
            recv_sem=st_recv.at[i],
            device_id=(lax.rem(section + 1, sections), dp),
            device_id_type=MESH,
        )

    def cot_copy(size, i):
        rows = rows_at(i * size, size)
        return pltpu.make_async_remote_copy(
            src_ref=xin.at[rows],
            dst_ref=cin.at[rows],
            send_sem=ct_send.at[i],
            recv_sem=ct_recv.at[i],
            device_id=(lax.rem(section + sections - 1, sections), dp),
            device_id_type=MESH,
        )

    @pl.when(natural)
    def _():
        if packing:
            lag = jnp.where(section == 0, ring - 1, ring - 3)
        else:
            lag = jnp.minimum(ring - 1, 3 * (last - section))

        @pl.when(section > 0)
        def _():
            prepare_columns()
            prepare_backward()
            if packing:
                xout[2 * ROWS : WINDOW, :] = jnp.zeros((WINDOW - 2 * ROWS, feats), f32)

        @pl.loop(0, chunks + lag)
        def _(t):
            @pl.when(t < chunks)
            def _():
                @pl.when(section == 0)
                def _():
                    input_copy(t).wait()

                @pl.when(section > 0)
                def _():
                    state_copy(xout, ROWS, t).wait_recv()

                rows = rows_at(t * ROWS, ROWS)
                saved = rows_at(lax.rem(t, ring) * ROWS, ROWS)
                forward(rows, saved)

                @pl.when(plain_next)
                def _():
                    state_copy(xout, ROWS, t).start()

            if packing:

                j = jnp.where(t < 8, t - 1, t - 2)

                @pl.when(packs & (t >= 1) & (t != 8) & (j < chunks))
                def _():
                    start, _, hits = pack_matrix(j)
                    packed[rows_at(j * prows, prows), :] = split_dot(
                        dot, as_onehot(hits), xout[rows_at(start, WINDOW), :]
                    )
                    state_copy(packed, prows, j).start()

            @pl.when((section == 0) & (t == 3))
            def _():
                prepare_columns()
                prepare_backward()

            k = t - lag

            @pl.when((k >= 0) & (k < chunks))
            def _():
                @pl.when(k == 0)
                def _():
                    finish_weights()

                target_copy(k).wait()
                rows = rows_at(k * ROWS, ROWS)
                saved = rows_at(lax.rem(k, ring) * ROWS, ROWS)

                @pl.when(plain_next)
                def _():
                    cot_copy(ROWS, k).wait_recv()
                    spread[...] = cin[rows, :]

                if packing:

                    @pl.when(packs)
                    def _():
                        @pl.when(k == 0)
                        def _():
                            for i in range(3):
                                cot_copy(prows, i).wait_recv()

                        @pl.when((k >= 2) & (k + 1 < chunks))
                        def _():
                            cot_copy(prows, k + 1).wait_recv()

                        spread[...] = unpack_rows(k)

                else:

                    @pl.when(section == last)
                    def _():
                        spread[...] = jnp.zeros_like(spread)

                weight = jnp.concatenate(
                    [
                        jnp.broadcast_to(
                            q_ref[pl.ds(k * (ROWS // LANES) + i, 1), :], (LANES, LANES)
                        ).T
                        for i in range(ROWS // LANES)
                    ],
                    axis=0,
                )
                diff = xout[rows, :] - tgt[rows, :]
                g = loss_part(ROWS, diff, weight) + spread[...]
                backward(ROWS, rows, saved, g)

                @pl.when(section > 0)
                def _():
                    cot_copy(ROWS, k).start()

        @pl.loop(0, chunks)
        def _(i):
            @pl.when(plain_next)
            def _():
                state_copy(xout, ROWS, i).wait_send()

            if packing:

                @pl.when(packs)
                def _():
                    state_copy(packed, prows, i).wait_send()

            @pl.when(section > 0)
            def _():
                cot_copy(ROWS, i).wait_send()

    if packing:

        @pl.when(jnp.logical_not(natural))
        def _():
            lag = last - section
            prepare_columns()
            prepare_backward()

            @pl.loop(0, chunks + lag)
            def _(t):
                @pl.when(t < chunks)
                def _():
                    @pl.when(t == 0)
                    def _():
                        target_copy(0).wait()
                        target_copy(1).wait()

                    @pl.when(t + 2 < chunks)
                    def _():
                        target_copy(t + 2).wait()

                    start, first, hits = pack_matrix(t)
                    rows = rows_at(t * prows, prows)
                    packed[rows, :] = split_dot(
                        dot, as_onehot(hits), tgt[rows_at(start, WINDOW), :]
                    )
                    weight = jnp.zeros((prows, LANES), f32)
                    for i, hit in enumerate(hits):
                        weight += jnp.where(hit, q_ref[pl.ds(first + i, 1), :], 0.0)
                    qring[lax.rem(t, sections)] = jnp.broadcast_to(
                        jnp.sum(weight, -1, keepdims=True), (prows, LANES)
                    )
                    state_copy(xout, prows, t).wait_recv()
                    saved = rows_at(lax.rem(t, ring) * ROWS, prows)
                    forward(rows, saved)

                    @pl.when(section < last)
                    def _():
                        state_copy(xout, prows, t).start()

                k = t - lag

                @pl.when(k >= 0)
                def _():
                    @pl.when(k == 0)
                    def _():
                        finish_weights()

                    rows = rows_at(k * prows, prows)
                    saved = rows_at(lax.rem(k, ring) * ROWS, prows)
                    diff = xout[rows, :] - packed[rows, :]
                    spread[0:prows, :] = loss_part(prows, diff, qring[lax.rem(k, sections)])

                    @pl.when(section < last)
                    def _():
                        cot_copy(prows, k).wait_recv()
                        spread[0:prows, :] += cin[rows, :]

                    backward(prows, rows, saved, spread[0:prows, :])
                    cot_copy(prows, k).start()

            @pl.loop(0, chunks)
            def _(i):
                cot_copy(prows, i).wait_send()

                @pl.when(section < last)
                def _():
                    state_copy(xout, prows, i).wait_send()

    depth = min(4, groups)
    width = groups // depth
    y, z = lax.rem(dp, width), dp // width
    ypart, zpart = feats // width, feats // groups
    order = (3, 1, 2, 0)
    ysum = save_x

    def y_copy(p, step):
        to = lax.rem(y + step, width)
        i = p * width + step
        return pltpu.make_async_remote_copy(
            src_ref=acc.at[order[p], rows_at(to * ypart, ypart)],
            dst_ref=ybuf.at[p * (width - 1) + step - 1],
            send_sem=y_send.at[i],
            recv_sem=y_recv.at[i],
            device_id=(section, z * width + to),
            device_id_type=MESH,
        )

    def z_copy(p, step):
        to = lax.rem(z + step, depth)
        i = p * depth + step
        return pltpu.make_async_remote_copy(
            src_ref=ysum.at[rows_at(p * ypart + to * zpart, zpart)],
            dst_ref=zbuf.at[p * (depth - 1) + step - 1],
            send_sem=z_send.at[i],
            recv_sem=z_recv.at[i],
            device_id=(section, to * width + y),
            device_id_type=MESH,
        )

    def z_back(p, step):
        to = lax.rem(z + step, depth)
        i = p * depth + step
        rows = rows_at(y * ypart + z * zpart, zpart)
        return pltpu.make_async_remote_copy(
            src_ref=final.at[order[p], rows],
            dst_ref=final.at[order[p], rows],
            send_sem=za_send.at[i],
            recv_sem=za_recv.at[i],
            device_id=(section, to * width + y),
            device_id_type=MESH,
        )

    def y_back(p, step):
        to = lax.rem(y + step, width)
        i = p * width + step
        rows = rows_at(y * ypart, ypart)
        return pltpu.make_async_remote_copy(
            src_ref=final.at[order[p], rows],
            dst_ref=final.at[order[p], rows],
            send_sem=ya_send.at[i],
            recv_sem=ya_recv.at[i],
            device_id=(section, z * width + to),
            device_id_type=MESH,
        )

    def small_copy(step):
        return pltpu.make_async_remote_copy(
            src_ref=small.at[dp],
            dst_ref=small.at[dp],
            send_sem=small_send.at[step],
            recv_sem=small_recv.at[step],
            device_id=peer(step),
            device_id_type=MESH,
        )

    def tiny_copy(step):
        return pltpu.make_async_remote_copy(
            src_ref=tiny.at[section],
            dst_ref=tiny.at[section],
            send_sem=tiny_send.at[step],
            recv_sem=tiny_recv.at[step],
            device_id=(lax.rem(section + step, sections), dp),
            device_id_type=MESH,
        )

    def out_copy(p):
        return pltpu.make_async_copy(final.at[order[p]], grads_ref.at[order[p]], out_sem.at[p])

    pieces = range(4)
    for p in pieces:
        for step in range(1, width):
            y_copy(p, step).start()
    for p in pieces:
        own = acc[order[p], rows_at(y * ypart, ypart), :]
        for step in range(1, width):
            y_copy(p, step).wait_recv()
            own = own + ybuf[p * (width - 1) + step - 1]
        ysum[p * ypart : (p + 1) * ypart, :] = own
        for step in range(1, depth):
            z_copy(p, step).start()
    squares = jnp.zeros((1, 1), f32)
    for p in pieces:
        own = ysum[rows_at(p * ypart + z * zpart, zpart), :]
        for step in range(1, depth):
            z_copy(p, step).wait_recv()
            own = own + zbuf[p * (depth - 1) + step - 1]
        final[order[p], rows_at(y * ypart + z * zpart, zpart), :] = own
        squares = squares + jnp.sum(own * own, axis=(0, 1), keepdims=True)
        for step in range(1, depth):
            z_back(p, step).start()
    loss = jnp.sum(loss_acc[...], axis=(0, 1), keepdims=True)
    wide_row = lax.broadcasted_iota(jnp.int32, (8, feats), 0)
    small[dp] = jnp.where(
        wide_row == 0,
        jnp.sum(gain_acc[0], 0, keepdims=True),
        jnp.where(
            wide_row == 1,
            jnp.sum(gain_acc[1], 0, keepdims=True),
            jnp.where(wide_row < 4, loss, squares),
        ),
    )
    for step in range(1, groups):
        small_copy(step).start()
    for p in pieces:
        for step in range(1, depth):
            z_back(p, step).wait_recv()
        for step in range(1, width):
            y_back(p, step).start()
    for step in range(1, groups):
        small_copy(step).wait_recv()
    total = small[0]
    for other in range(1, groups):
        total = total + small[other]
    dgain_ref[...] = total[0:2]
    gain_squares = jnp.sum(total[0:2] * total[0:2], axis=(0, 1), keepdims=True)
    tiny[section] = jnp.where(tile_row < 4, total[2:3, 0:1], total[4:5, 0:1] + gain_squares)
    for step in range(1, sections):
        tiny_copy(step).start()
    for p in pieces:
        for step in range(1, width):
            y_back(p, step).wait_recv()
        out_copy(p).start()
    for step in range(1, sections):
        tiny_copy(step).wait_recv()
    whole = tiny[0]
    for other in range(1, sections):
        whole = whole + tiny[other]
    norm = jnp.sqrt(whole[4:5])
    scale = jnp.minimum(1.0, clip_limit / norm)
    stats = stat_ref[...]
    stat_ref[...] = jnp.where(
        tile_row == 0,
        whole[0:1],
        jnp.where(tile_row == 1, norm, jnp.where(tile_row == 2, scale, stats)),
    )

    for step in range(1, groups):
        weight_copy(step).wait_send()
        small_copy(step).wait_send()
    for step in range(1, sections):
        tiny_copy(step).wait_send()
    for p in pieces:
        out_copy(p).wait()
        for step in range(1, width):
            y_copy(p, step).wait_send()
            y_back(p, step).wait_send()
        for step in range(1, depth):
            z_copy(p, step).wait_send()
            z_back(p, step).wait_send()


def rollout(packing, sections, groups, inputs, target, lengths, lat_index, land, w_up, w_down, gains):
    columns, feats = inputs.shape
    chunks = columns // ROWS
    prows = ROWS * (sections - 2) // sections + 16
    grid_rows = columns // LANES
    packed_bytes = 4 * chunks * prows * feats
    ring = (SAVE_BYTES - packed_bytes) // (12 * ROWS * feats)
    depth = min(4, groups)
    width = groups // depth
    hbm = pl.BlockSpec(memory_space=pl.ANY)
    vmem = pl.BlockSpec(memory_space=pltpu.VMEM)
    dma = pltpu.SemaphoreType.DMA
    wide = pltpu.VMEM((columns, feats), f32)
    lows = pltpu.VMEM((2, feats, feats), bf16)
    grads = pltpu.VMEM((4, feats, feats), f32)
    flat = lambda array: array.reshape(grid_rows, LANES)
    return pl.pallas_call(
        functools.partial(rollout_kernel, sections, groups, packing),
        out_shape=(
            jax.ShapeDtypeStruct((4, feats, feats), f32),
            jax.ShapeDtypeStruct((2, feats), f32),
            jax.ShapeDtypeStruct((8, LANES), f32),
        ),
        in_specs=[hbm, hbm] + [vmem] * 6,
        out_specs=(hbm, vmem, vmem),
        scratch_shapes=[
            wide,
            wide,
            wide,
            wide,
            pltpu.VMEM((chunks * prows if packing else 8, feats), f32),
            pltpu.VMEM((ring * ROWS, feats), f32),
            pltpu.VMEM((2, ring * ROWS, feats), bf16),
            pltpu.VMEM((2, ring * ROWS, feats), bf16),
            pltpu.VMEM((sections, prows, LANES), f32),
            lows,
            lows,
            lows,
            lows,
            pltpu.VMEM((grid_rows, LANES), f32),
            pltpu.VMEM((grid_rows, LANES), f32),
            pltpu.VMEM((8, LANES), f32),
            pltpu.VMEM((8, feats), f32),
            pltpu.VMEM((2, 8, feats), f32),
            pltpu.VMEM((groups, 8, LANES), f32),
            pltpu.VMEM((ROWS, feats), f32),
            grads,
            grads,
            pltpu.VMEM((max(4 * (width - 1), 1), feats // width, feats), f32),
            pltpu.VMEM((4 * (depth - 1), feats // groups, feats), f32),
            pltpu.VMEM((groups, 8, feats), f32),
            pltpu.VMEM((sections, 8, LANES), f32),
            dma((chunks,)),
            dma((chunks,)),
            dma((chunks,)),
            dma((chunks,)),
            dma((chunks,)),
            dma((chunks,)),
            dma((groups,)),
            dma((groups,)),
            dma((4 * width,)),
            dma((4 * width,)),
            dma((4 * depth,)),
            dma((4 * depth,)),
            dma((4 * depth,)),
            dma((4 * depth,)),
            dma((4 * width,)),
            dma((4 * width,)),
            dma((groups,)),
            dma((groups,)),
            dma((sections,)),
            dma((sections,)),
            dma((4,)),
        ],
        compiler_params=pltpu.CompilerParams(
            collective_id=0 if packing else 1,
            has_side_effects=True,
            vmem_limit_bytes=63 * 1024 * 1024,
        ),
        name="rollout_packed" if packing else "rollout_all",
    )(
        inputs,
        target,
        flat(lengths),
        flat(lat_index),
        flat(land),
        w_up,
        w_down,
        gains,
    )


def adam_step(weights_old, gradient, moment_one, moment_two, decay_rate):
    moment_one = beta_one * moment_one + (1.0 - beta_one) * gradient
    moment_two = beta_two * moment_two + (1.0 - beta_two) * gradient * gradient
    first_hat = moment_one / (1.0 - beta_one**STEP)
    second_hat = moment_two / (1.0 - beta_two**STEP)
    new_weights = weights_old - learn_rate * (
        first_hat / (jnp.sqrt(second_hat) + adam_eps) + decay_rate * weights_old
    )
    return (new_weights, moment_one, moment_two)


def per_device(
    inputs,
    targets,
    lengths,
    lat_index,
    land,
    w_up,
    w_down,
    gains,
    m_up,
    m_down,
    m_gains,
    v_up,
    v_down,
    v_gains,
):
    sections, groups = lax.axis_size("section"), lax.axis_size("dp")
    operands = (inputs, targets[0], lengths, lat_index, land, w_up[0], w_down[0], gains[0])
    packed = rollout(True, sections, groups, *operands)

    grads, grad_gain, stats = lax.cond(
        packed[2][4, 0] > 0.0,
        lambda: rollout(False, sections, groups, *operands),
        lambda: packed,
    )
    loss_sum, grad_norm, clip_scale, weight_sum = (stats[i, 0] for i in range(4))
    grad_up, grad_down, grad_gain = grads[None, 0:2], grads[None, 2:4], grad_gain[None]
    new_up, new_m_up, new_v_up = adam_step(w_up, grad_up * clip_scale, m_up, v_up, weight_decay)
    new_down, new_m_down, new_v_down = adam_step(
        w_down, grad_down * clip_scale, m_down, v_down, weight_decay
    )
    new_gains, new_m_gains, new_v_gains = adam_step(
        gains, grad_gain * clip_scale, m_gains, v_gains, 0.0
    )
    return (
        loss_sum,
        weight_sum,
        grad_norm,
        new_up,
        new_down,
        new_gains,
        new_m_up,
        new_m_down,
        new_m_gains,
        new_v_up,
        new_v_down,
        new_v_gains,
    )


def solution(mesh):
    return jax.shard_map(
        per_device,
        mesh=mesh,
        in_specs=(
            P("dp", None),
            P("section", "dp", None),
            P("dp"),
            P("dp"),
            P("dp"),
            P("section", None, None, None),
            P("section", None, None, None),
            P("section", None, None),
            P("section", None, None, None),
            P("section", None, None, None),
            P("section", None, None),
            P("section", None, None, None),
            P("section", None, None, None),
            P("section", None, None),
        ),
        out_specs=(
            P(),
            P(),
            P(),
            P("section", None, None, None),
            P("section", None, None, None),
            P("section", None, None),
            P("section", None, None, None),
            P("section", None, None, None),
            P("section", None, None),
            P("section", None, None, None),
            P("section", None, None, None),
            P("section", None, None),
        ),
        check_vma=False,
    )
```

time: 242 us -> 135 us (0.56)
  blocking collectives: 64.7 us -> 0 us
  waiting for transfers between devices: 56.4 us -> 0 us
  Pallas kernels: 91.5 us -> 126 us
  between operations: 18.6 us -> 1.41 us
  other arithmetic: 9.09 us -> 6.15 us
    psum x3 -> x0, blocking collectives: 64.7 us -> none  [the longest x1 39.9 us: per_device(): loss_sum = lax.psum(local_loss, ('section', 'dp'))]
    psum x1 -> x0, waiting for transfers between devices: 56.4 us -> none  [per_device(): lax.psum((grad_up, grad_down, grad_gain), 'dp')]
    pallas_call x1, Pallas kernels: 91.5 us -> 126 us  [rollout(): pl.pallas_call(functools.partial(rollout_kernel, sections, groups, packin...]
    reduce_sum x3 -> x0, other arithmetic: 4.16 us -> none  [the longest x1 1.78 us: per_device(): jnp.sum(grad_down * grad_down)]
  transfers between devices with their start and end apart: 1 -> 0, of which waited for: 1 -> 0; matrix products, arithmetic and copies ran while one was open for 0% -> 0% of each run, Pallas kernels for 0% -> 0%
where the time goes in v2:
time: 135 us
  Pallas kernels  126 us (93%)
  other arithmetic  6.15 us (5%)
  between operations  1.41 us (1%)
    pallas_call x1, Pallas kernels, rollout(): pl.pallas_call(functools.partial(rollout_kernel, sections, groups, packin...  126 us
    sub x2, other arithmetic, adam_step(): weights_old - learn_rate * (first_hat / (jnp.sqrt(second_hat) + adam_eps)...  6.15 us

profile of v2, /device:TPU:0, one launch (start us, length us, event | category | flops | bytes accessed | tf_op | source)
XLA Modules:
  0.0 134.5 jit_solution(16525764476342100410)
XLA Ops:
  0.6 0.0 copy-start
  0.7 0.0 copy-start.1
  0.7 0.0 copy-start.2
  0.7 0.0 copy-start.3
  0.7 0.0 copy-start.4
  0.7 125.6 %rollout_packed.1 = (f32[4,256,256]{2,1,0:T(8,128)}, f32[2,256]{1,0:T(2,128)S(1)}, f32[8,128]{1,0:T(8,128)S(1)}) custom-call(f32[8192,256]{1,0:T(8,128)} %inputs_ref.1, f32[8192,256]{1,0:T(8,128)} %bitcast.42, s32[64,128]{1,0:T(8,128)} %bitcast.48, s32[64,128]{1,0:T(8,128)} %bitcast.50, s32[64,128]{1,0:T(8,128)} %bitcast.52, f32[2,256,256]{2,1,0:T(8,128)} %bitcast.44, ...), custom_call_target="tpu_custom_call" | custom-call | tf_op jit(solution)/shard_map/rollout_packed/pallas_call | solution.py:698
  126.3 0.5 slice.61
  127.5 0.0 copy-done
  127.5 0.0 copy-done.1
  127.5 0.0 copy-done.2
  127.5 0.0 copy-done.3
  127.5 0.0 copy-done.4
  127.5 0.0 copy-start.5
  127.5 0.0 copy-start.6
  127.6 0.2 conditional.1
  127.8 0.6 fusion.9
  128.4 4.9 %multiply_subtract_fusion = (f32[1,2,256,256]{3,2,1,0:T(8,128)}, f32[1,2,256,256]{3,2,1,0:T(8,128)}, f32[1,2,256,256]{3,2,1,0:T(8,128)}, f32[1,2,256,256]{3,2,1,...) fusion(f32[1,2,256,256]{3,2,1,0:T(8,128)} %param.22, f32[]{:T(128)} %bitcast.11, ...), kind=kLoop, calls=%fused_computation.8 | loop fusion | flops 4194304 | bytes 7340036 | tf_op jit(solution)/shard_map/sub | solution.py:779
  133.2 0.0 copy-done.5
  133.2 0.0 copy-done.6
  133.2 1.3 multiply_subtract_fusion.2
Async XLA Ops:
  0.6 126.8 %copy-start = (f32[1,2,256,256]{3,2,1,0:T(8,128)S(1)}, f32[1,2,256,256]{3,2,1,0:T(8,128)}, u32[]{:S(2)}) copy-start(f32[1,2,256,256]{3,2,1,0:T(8,128)} %param.21) | copy-start | bytes 1572868
  0.7 126.8 %copy-start.1 = (s32[8192]{0:T(1024)S(1)}, s32[8192]{0:T(1024)}, u32[]{:S(2)}) copy-start(s32[8192]{0:T(1024)} %param.18) | copy-start | bytes 98308
  0.7 126.8 %copy-start.2 = (s32[8192]{0:T(1024)S(1)}, s32[8192]{0:T(1024)}, u32[]{:S(2)}) copy-start(s32[8192]{0:T(1024)} %param.19) | copy-start | bytes 98308
  0.7 126.8 %copy-start.3 = (s32[8192]{0:T(1024)S(1)}, s32[8192]{0:T(1024)}, u32[]{:S(2)}) copy-start(s32[8192]{0:T(1024)} %param.20) | copy-start | bytes 98308
  0.7 126.8 %copy-start.4 = (f32[1,2,256]{2,1,0:T(2,128)S(1)}, f32[1,2,256]{2,1,0:T(2,128)}, u32[]{:S(2)}) copy-start(f32[1,2,256]{2,1,0:T(2,128)} %param.23) | copy-start | bytes 6148
  127.5 5.7 %copy-start.5 = (f32[1,2,256]{2,1,0:T(2,128)S(1)}, f32[1,2,256]{2,1,0:T(2,128)}, u32[]{:S(2)}) copy-start(f32[1,2,256]{2,1,0:T(2,128)} %param.26) | copy-start | bytes 6148
  127.5 5.7 %copy-start.6 = (f32[1,2,256]{2,1,0:T(2,128)S(1)}, f32[1,2,256]{2,1,0:T(2,128)}, u32[]{:S(2)}) copy-start(f32[1,2,256]{2,1,0:T(2,128)} %param.29) | copy-start | bytes 6148

commit v3 on v2

--- a/solution.py
+++ b/solution.py
@@ -22,7 +22,9 @@
 f32, bf16 = jnp.float32, jnp.bfloat16
 MESH = pl.DeviceIdType.MESH
 LANES = 128
+PIECE = 128
 ROWS = 512
+SPARE = 80
 WINDOW = 1536
 SAVE_BYTES = 21 * 1024 * 1024
 
@@ -50,8 +52,8 @@
     len_ref,
     lat_ref,
     land_ref,
-    up_ref,
-    down_ref,
+    up_hbm,
+    down_hbm,
     gain_ref,
     grads_ref,
     dgain_ref,
@@ -76,6 +78,8 @@
     gain_acc,
     wbuf,
     spread,
+    up_ref,
+    down_ref,
     acc,
     final,
     ybuf,
@@ -103,6 +107,7 @@
     tiny_send,
     tiny_recv,
     out_sem,
+    weight_sem,
 ):
     section = lax.axis_index("section")
     dp = lax.axis_index("dp")
@@ -122,6 +127,11 @@
     def peer(step):
         return (section, lax.rem(dp + step, groups))
 
+    up_copy = pltpu.make_async_copy(up_hbm, up_ref, weight_sem.at[0])
+    down_copy = pltpu.make_async_copy(down_hbm, down_ref, weight_sem.at[1])
+    up_copy.start()
+    down_copy.start()
+
     barrier = pltpu.get_barrier_semaphore()
     for step in range(1, sections):
         other = lax.rem(section + step, sections)
@@ -149,10 +159,6 @@
     @pl.loop(0, chunks)
     def _(i):
         target_copy(i).start()
-
-    for layer in range(2):
-        up_lo[layer] = (0.5 * up_ref[layer]).astype(bf16)
-        down_lo[layer] = down_ref[layer].astype(bf16)
 
     def prepare_backward():
         for layer in range(2):
@@ -171,7 +177,10 @@
         return jnp.clip(ROWS * (j - 1) + shift, 0, columns - WINDOW)
 
     def expand_start(k):
-        return jnp.clip(live_rows * k - 256, 0, total_packed - expand)
+        return jnp.clip(live_rows * k - 272, 0, total_packed - expand)
+
+    def chunks_for(k):
+        return (expand_start(k) + expand - 1) // prows
 
     def weight_copy(step):
         return pltpu.make_async_remote_copy(
@@ -212,7 +221,7 @@
                 + lax.broadcasted_iota(jnp.int32, (grid_rows, LANES), 1)
             )
             rank_i = rank.astype(jnp.int32)
-            missed = beyond & (rank_i >= total_packed)
+            missed = beyond & (rank_i >= total_packed - SPARE)
             for j in range(chunks):
                 shift = 0 if j < 7 else 256 if j < 11 else 384
                 start = min(max(ROWS * (j - 1) + shift, 0), columns - WINDOW)
@@ -220,7 +229,7 @@
                 ready = ROWS * (j + 2 if j < 7 else j + 3)
                 missed |= member & ((place < start) | (place >= min(start + WINDOW, ready)))
             row_chunk = lax.broadcasted_iota(jnp.int32, (grid_rows, LANES), 0) // (ROWS // LANES)
-            row_start = jnp.clip(live_rows * row_chunk - 256, 0, total_packed - expand)
+            row_start = jnp.clip(live_rows * row_chunk - 272, 0, total_packed - expand)
             missed |= beyond & ((rank_i < row_start) | (rank_i >= row_start + expand))
             misses = jnp.sum(missed.astype(f32), axis=(0, 1), keepdims=True)
         wbuf[dp] = jnp.where(tile_row < 4, local_weight, misses)
@@ -236,6 +245,11 @@
         stat_ref[...] = total
         scale_ref[...] = 2.0 / jnp.broadcast_to(total[0:1], (8, LANES))
 
+    up_copy.wait()
+    down_copy.wait()
+    for layer in range(2):
+        up_lo[layer] = (0.5 * up_ref[layer]).astype(bf16)
+        down_lo[layer] = down_ref[layer].astype(bf16)
     pl.semaphore_wait(barrier, sections - 1 + groups - 1)
 
     def pack_matrix(j):
@@ -258,7 +272,7 @@
         hits = []
         for i in range(ROWS // LANES):
             hits.append(source_row == rank_ref[pl.ds(k * (ROWS // LANES) + i, 1), :] - base)
-        return split_dot(dot_lhs_t, as_onehot(hits), cin[rows_at(start, expand), :])
+        return dot_lhs_t(as_onehot(hits), cin[rows_at(start, expand), :].astype(bf16))
 
     def forward(rows, saved):
         x = xin[rows, :]
@@ -303,8 +317,8 @@
             g = g + r * (gain * g_normed - xr * mean)
         xin[rows, :] = g
 
-    def state_copy(source, size, i):
-        rows = rows_at(i * size, size)
+    def state_copy(source, size, i, count=None):
+        rows = rows_at(i * size, size if count is None else count)
         return pltpu.make_async_remote_copy(
             src_ref=source.at[rows],
             dst_ref=xin.at[rows],
@@ -314,8 +328,8 @@
             device_id_type=MESH,
         )
 
-    def cot_copy(size, i):
-        rows = rows_at(i * size, size)
+    def cot_copy(size, i, count=None):
+        rows = rows_at(i * size, size if count is None else count)
         return pltpu.make_async_remote_copy(
             src_ref=xin.at[rows],
             dst_ref=cin.at[rows],
@@ -325,6 +339,42 @@
             device_id_type=MESH,
         )
 
+    def shorter(copy, size, i, action):
+        @pl.when(i < chunks - 1)
+        def _():
+            action(copy(size, i, size))
+
+        @pl.when(i == chunks - 1)
+        def _():
+            action(copy(size, i, size - SPARE))
+
+    def packed_state(size, i, count):
+        return state_copy(packed, size, i, count)
+
+    def packed_receive(size, i):
+        @pl.when(section == 2)
+        def _():
+            shorter(packed_state, size, i, lambda copy: copy.wait_recv())
+
+        @pl.when(section > 2)
+        def _():
+            state_copy(xout, size, i).wait_recv()
+
+    def cot_part(size, i, count):
+        return cot_copy(size, i, count)
+
+    def cot_wait(size, i):
+        shorter(cot_part, size, i, lambda copy: copy.wait_recv())
+
+    def cot_do(size, i, action):
+        @pl.when(section == 2)
+        def _():
+            shorter(cot_part, size, i, action)
+
+        @pl.when(section > 2)
+        def _():
+            action(cot_copy(size, i))
+
     @pl.when(natural)
     def _():
         if packing:
@@ -338,6 +388,7 @@
             prepare_backward()
             if packing:
                 xout[2 * ROWS : WINDOW, :] = jnp.zeros((WINDOW - 2 * ROWS, feats), f32)
+                cin[total_packed - SPARE : total_packed, :] = jnp.zeros((SPARE, feats), f32)
 
         @pl.loop(0, chunks + lag)
         def _(t):
@@ -369,7 +420,7 @@
                     packed[rows_at(j * prows, prows), :] = split_dot(
                         dot, as_onehot(hits), xout[rows_at(start, WINDOW), :]
                     )
-                    state_copy(packed, prows, j).start()
+                    shorter(packed_state, prows, j, lambda copy: copy.start())
 
             @pl.when((section == 0) & (t == 3))
             def _():
@@ -397,14 +448,12 @@
 
                     @pl.when(packs)
                     def _():
-                        @pl.when(k == 0)
-                        def _():
-                            for i in range(3):
-                                cot_copy(prows, i).wait_recv()
-
-                        @pl.when((k >= 2) & (k + 1 < chunks))
-                        def _():
-                            cot_copy(prows, k + 1).wait_recv()
+                        had = jnp.where(k == 0, -1, chunks_for(jnp.maximum(k - 1, 0)))
+                        for i in range(3):
+
+                            @pl.when(had + 1 + i <= chunks_for(k))
+                            def _():
+                                cot_wait(prows, had + 1 + i)
 
                         spread[...] = unpack_rows(k)
 
@@ -441,7 +490,7 @@
 
                 @pl.when(packs)
                 def _():
-                    state_copy(packed, prows, i).wait_send()
+                    shorter(packed_state, prows, i, lambda copy: copy.wait_send())
 
             @pl.when(section > 0)
             def _():
@@ -454,6 +503,11 @@
             lag = last - section
             prepare_columns()
             prepare_backward()
+
+            @pl.when(section == 2)
+            def _():
+                xin[total_packed - SPARE : total_packed, :] = jnp.zeros((SPARE, feats), f32)
+
 
             @pl.loop(0, chunks + lag)
             def _(t):
@@ -479,7 +533,7 @@
                     qring[lax.rem(t, sections)] = jnp.broadcast_to(
                         jnp.sum(weight, -1, keepdims=True), (prows, LANES)
                     )
-                    state_copy(xout, prows, t).wait_recv()
+                    packed_receive(prows, t)
                     saved = rows_at(lax.rem(t, ring) * ROWS, prows)
                     forward(rows, saved)
 
@@ -506,11 +560,11 @@
                         spread[0:prows, :] += cin[rows, :]
 
                     backward(prows, rows, saved, spread[0:prows, :])
-                    cot_copy(prows, k).start()
+                    cot_do(prows, k, lambda copy: copy.start())
 
             @pl.loop(0, chunks)
             def _(i):
-                cot_copy(prows, i).wait_send()
+                cot_do(prows, i, lambda copy: copy.wait_send())
 
                 @pl.when(section < last)
                 def _():
@@ -519,15 +573,18 @@
     depth = min(4, groups)
     width = groups // depth
     y, z = lax.rem(dp, width), dp // width
-    ypart, zpart = feats // width, feats // groups
-    order = (3, 1, 2, 0)
+    ypart, zpart = PIECE // width, PIECE // groups
+    halves = feats // PIECE
+    pieces = range(4 * halves)
+    matrix = [m for m in (3, 1, 2, 0) for _ in range(halves)]
+    first = [PIECE * (p % halves) for p in pieces]
     ysum = save_x
 
     def y_copy(p, step):
         to = lax.rem(y + step, width)
         i = p * width + step
         return pltpu.make_async_remote_copy(
-            src_ref=acc.at[order[p], rows_at(to * ypart, ypart)],
+            src_ref=acc.at[matrix[p], rows_at(first[p] + to * ypart, ypart)],
             dst_ref=ybuf.at[p * (width - 1) + step - 1],
             send_sem=y_send.at[i],
             recv_sem=y_recv.at[i],
@@ -550,10 +607,10 @@
     def z_back(p, step):
         to = lax.rem(z + step, depth)
         i = p * depth + step
-        rows = rows_at(y * ypart + z * zpart, zpart)
+        rows = rows_at(first[p] + y * ypart + z * zpart, zpart)
         return pltpu.make_async_remote_copy(
-            src_ref=final.at[order[p], rows],
-            dst_ref=final.at[order[p], rows],
+            src_ref=final.at[matrix[p], rows],
+            dst_ref=final.at[matrix[p], rows],
             send_sem=za_send.at[i],
             recv_sem=za_recv.at[i],
             device_id=(section, to * width + y),
@@ -563,10 +620,10 @@
     def y_back(p, step):
         to = lax.rem(y + step, width)
         i = p * width + step
-        rows = rows_at(y * ypart, ypart)
+        rows = rows_at(first[p] + y * ypart, ypart)
         return pltpu.make_async_remote_copy(
-            src_ref=final.at[order[p], rows],
-            dst_ref=final.at[order[p], rows],
+            src_ref=final.at[matrix[p], rows],
+            dst_ref=final.at[matrix[p], rows],
             send_sem=ya_send.at[i],
             recv_sem=ya_recv.at[i],
             device_id=(section, z * width + to),
@@ -594,14 +651,16 @@
         )
 
     def out_copy(p):
-        return pltpu.make_async_copy(final.at[order[p]], grads_ref.at[order[p]], out_sem.at[p])
-
-    pieces = range(4)
+        rows = pl.ds(first[p], PIECE)
+        return pltpu.make_async_copy(
+            final.at[matrix[p], rows], grads_ref.at[matrix[p], rows], out_sem.at[p]
+        )
+
     for p in pieces:
         for step in range(1, width):
             y_copy(p, step).start()
     for p in pieces:
-        own = acc[order[p], rows_at(y * ypart, ypart), :]
+        own = acc[matrix[p], rows_at(first[p] + y * ypart, ypart), :]
         for step in range(1, width):
             y_copy(p, step).wait_recv()
             own = own + ybuf[p * (width - 1) + step - 1]
@@ -614,7 +673,7 @@
         for step in range(1, depth):
             z_copy(p, step).wait_recv()
             own = own + zbuf[p * (depth - 1) + step - 1]
-        final[order[p], rows_at(y * ypart + z * zpart, zpart), :] = own
+        final[matrix[p], rows_at(first[p] + y * ypart + z * zpart, zpart), :] = own
         squares = squares + jnp.sum(own * own, axis=(0, 1), keepdims=True)
         for step in range(1, depth):
             z_back(p, step).start()
@@ -688,12 +747,14 @@
     ring = (SAVE_BYTES - packed_bytes) // (12 * ROWS * feats)
     depth = min(4, groups)
     width = groups // depth
+    pieces = 4 * feats // PIECE
     hbm = pl.BlockSpec(memory_space=pl.ANY)
     vmem = pl.BlockSpec(memory_space=pltpu.VMEM)
     dma = pltpu.SemaphoreType.DMA
     wide = pltpu.VMEM((columns, feats), f32)
     lows = pltpu.VMEM((2, feats, feats), bf16)
     grads = pltpu.VMEM((4, feats, feats), f32)
+    square = pltpu.VMEM((2, feats, feats), f32)
     flat = lambda array: array.reshape(grid_rows, LANES)
     return pl.pallas_call(
         functools.partial(rollout_kernel, sections, groups, packing),
@@ -702,7 +763,7 @@
             jax.ShapeDtypeStruct((2, feats), f32),
             jax.ShapeDtypeStruct((8, LANES), f32),
         ),
-        in_specs=[hbm, hbm] + [vmem] * 6,
+        in_specs=[hbm, hbm, vmem, vmem, vmem, hbm, hbm, vmem],
         out_specs=(hbm, vmem, vmem),
         scratch_shapes=[
             wide,
@@ -725,10 +786,12 @@
             pltpu.VMEM((2, 8, feats), f32),
             pltpu.VMEM((groups, 8, LANES), f32),
             pltpu.VMEM((ROWS, feats), f32),
+            square,
+            square,
             grads,
             grads,
-            pltpu.VMEM((max(4 * (width - 1), 1), feats // width, feats), f32),
-            pltpu.VMEM((4 * (depth - 1), feats // groups, feats), f32),
+            pltpu.VMEM((max(pieces * (width - 1), 1), PIECE // width, feats), f32),
+            pltpu.VMEM((pieces * (depth - 1), PIECE // groups, feats), f32),
             pltpu.VMEM((groups, 8, feats), f32),
             pltpu.VMEM((sections, 8, LANES), f32),
             dma((chunks,)),
@@ -739,19 +802,20 @@
             dma((chunks,)),
             dma((groups,)),
             dma((groups,)),
-            dma((4 * width,)),
-            dma((4 * width,)),
-            dma((4 * depth,)),
-            dma((4 * depth,)),
-            dma((4 * depth,)),
-            dma((4 * depth,)),
-            dma((4 * width,)),
-            dma((4 * width,)),
+            dma((pieces * width,)),
+            dma((pieces * width,)),
+            dma((pieces * depth,)),
+            dma((pieces * depth,)),
+            dma((pieces * depth,)),
+            dma((pieces * depth,)),
+            dma((pieces * width,)),
+            dma((pieces * width,)),
             dma((groups,)),
             dma((groups,)),
             dma((sections,)),
             dma((sections,)),
-            dma((4,)),
+            dma((pieces,)),
+            dma((2,)),
         ],
         compiler_params=pltpu.CompilerParams(
             collective_id=0 if packing else 1,
@@ -780,6 +844,61 @@
         first_hat / (jnp.sqrt(second_hat) + adam_eps) + decay_rate * weights_old
     )
     return (new_weights, moment_one, moment_two)
+
+
+def update_kernel(
+    grads_ref,
+    dgain_ref,
+    stat_ref,
+    w_up,
+    w_down,
+    gains,
+    m_up,
+    m_down,
+    m_gains,
+    v_up,
+    v_down,
+    v_gains,
+    *outs,
+):
+    clip = stat_ref[2:3, 0:1]
+    matrices = ((0, w_up, m_up, v_up), (1, w_down, m_down, v_down))
+    for i, weight, one, two in matrices:
+        new = adam_step(weight[0], grads_ref[i, 0] * clip, one[0], two[0], weight_decay)
+        for part in range(3):
+            outs[3 * part + i][0] = new[part]
+
+    @pl.when(pl.program_id(0) == 0)
+    def _():
+        new = adam_step(gains[...], dgain_ref[...] * clip, m_gains[...], v_gains[...], 0.0)
+        for part in range(3):
+            outs[3 * part + 2][...] = new[part]
+
+
+def update(grads, grad_gain, stats, *state):
+    layers, feats = grad_gain.shape
+    halves = 2
+    rows = feats // halves
+    grads = grads.reshape(2, layers, feats, feats)
+    matrix = pl.BlockSpec((1, rows, feats), lambda i: (i // halves, i % halves, 0))
+    small = pl.BlockSpec((layers, feats), lambda i: (0, 0))
+    specs = [matrix, matrix, small] * 3
+    shapes = [jax.ShapeDtypeStruct(a.shape[1:], f32) for a in state]
+    new = pl.pallas_call(
+        update_kernel,
+        grid=(layers * halves,),
+        in_specs=[
+            pl.BlockSpec((2, 1, rows, feats), lambda i: (0, i // halves, i % halves, 0)),
+            small,
+            pl.BlockSpec((8, LANES), lambda i: (0, 0)),
+        ]
+        + specs,
+        out_specs=specs,
+        out_shape=shapes,
+        compiler_params=pltpu.CompilerParams(vmem_limit_bytes=32 * 1024 * 1024),
+        name="update",
+    )(grads, grad_gain, stats, *(a[0] for a in state))
+    return tuple(a[None] for a in new)
 
 
 def per_device(
@@ -807,29 +926,21 @@
         lambda: rollout(False, sections, groups, *operands),
         lambda: packed,
     )
-    loss_sum, grad_norm, clip_scale, weight_sum = (stats[i, 0] for i in range(4))
-    grad_up, grad_down, grad_gain = grads[None, 0:2], grads[None, 2:4], grad_gain[None]
-    new_up, new_m_up, new_v_up = adam_step(w_up, grad_up * clip_scale, m_up, v_up, weight_decay)
-    new_down, new_m_down, new_v_down = adam_step(
-        w_down, grad_down * clip_scale, m_down, v_down, weight_decay
+    new = update(
+        grads,
+        grad_gain,
+        stats,
+        w_up,
+        w_down,
+        gains,
+        m_up,
+        m_down,
+        m_gains,
+        v_up,
+        v_down,
+        v_gains,
     )
-    new_gains, new_m_gains, new_v_gains = adam_step(
-        gains, grad_gain * clip_scale, m_gains, v_gains, 0.0
-    )
-    return (
-        loss_sum,
-        weight_sum,
-        grad_norm,
-        new_up,
-        new_down,
-        new_gains,
-        new_m_up,
-        new_m_down,
-        new_m_gains,
-        new_v_up,
-        new_v_down,
-        new_v_gains,
-    )
+    return (stats[0, 0], stats[3, 0], stats[1, 0]) + new
 
 
 def solution(mesh):

time: 135 us -> 135 us (level)
  other arithmetic: 6.15 us -> 0 us
  local copies, waits for them, and re-layouts: 1.14 us -> 5.61 us
    sub x2 -> x0, other arithmetic: 6.15 us -> none  [adam_step(): weights_old - learn_rate * (first_hat / (jnp.sqrt(second_hat) + adam_eps)...]
    pallas_call x0 -> x1, Pallas kernels: none -> 4.63 us  [update(): pl.pallas_call(update_kernel, grid=(layers * halves,), in_specs=[pl.Block...]
    unnamed x14 -> x20, local copies, waits for them, and re-layouts: 0.03 us -> 3.15 us
    pallas_call x1, Pallas kernels: 126 us -> 123 us  [rollout(): pl.pallas_call(functools.partial(rollout_kernel, sections, groups, packin...]
where the time goes in v3:
time: 135 us; the launch traced here: 134 us
  Pallas kernels  127 us (94%)
  local copies, waits for them, and re-layouts  5.61 us (4%)
  between operations  1.58 us (1%)
    pallas_call x1, Pallas kernels, rollout(): pl.pallas_call(functools.partial(rollout_kernel, sections, groups, packin...  123 us
    pallas_call x1, Pallas kernels, update(): pl.pallas_call(update_kernel, grid=(layers * halves,), in_specs=[pl.Block...  4.63 us
    unnamed x20, local copies, waits for them, and re-layouts  3.15 us

profile of v3, /device:TPU:0, one launch (start us, length us, event | category | flops | bytes accessed | tf_op | source)
XLA Modules:
  0.0 134.4 jit_solution(9823426536826889600)
XLA Ops:
  0.6 0.0 copy-start.6
  0.7 0.0 copy-start.7
  0.7 0.0 copy-start.8
  0.7 0.0 copy-start.9
  0.7 122.5 %rollout_packed.1 = (f32[4,256,256]{2,1,0:T(8,128)}, f32[2,256]{1,0:T(2,128)S(1)}, f32[8,128]{1,0:T(8,128)}) custom-call(f32[8192,256]{1,0:T(8,128)} %inputs_ref.1, f32[8192,256]{1,0:T(8,128)} %bitcast.40, s32[64,128]{1,0:T(8,128)} %bitcast.50, s32[64,128]{1,0:T(8,128)} %bitcast.52, s32[64,128]{1,0:T(8,128)} %bitcast.54, f32[2,256,256]{2,1,0:T(8,128)} %bitcast.42, ...), custom_call_target="tpu_custom_call" | custom-call | tf_op jit(solution)/shard_map/rollout_packed/pallas_call | solution.py:759
  123.2 1.2 slice.30
  125.1 0.0 copy-done.6
  125.1 0.0 copy-done.7
  125.1 0.0 copy-done.8
  125.1 0.0 copy-done.9
  125.1 0.0 copy-start
  125.1 0.0 copy-start.4
  125.1 0.0 copy-start.5
  125.2 1.3 conditional.1
  125.2 1.3 fusion
  126.4 0.0 copy-done
  126.4 0.0 copy-done.4
  126.4 0.0 copy-done.5
  126.5 0.0 copy-start.1
  126.5 1.0 copy-done.1
  127.5 0.0 copy-start.2
  127.5 1.0 copy-done.2
  128.5 0.0 copy-start.3
  128.5 1.0 copy-done.3
  129.6 4.6 %update.1 = (f32[2,256,256]{2,1,0:T(8,128)}, f32[2,256,256]{2,1,0:T(8,128)}, f32[2,256]{1,0:T(2,128)}, f32[2,256,256]{2,1,0:T(8,128)}, f32[2,256,256]{2,1,0:T(8,...) custom-call(f32[2,2,256,256]{3,2,1,0:T(8,128)} %get-tuple-element.106.grads_ref, ...), custom_call_target="tpu_custom_call" | custom-call | tf_op jit(solution)/shard_map/update/pallas_call | solution.py:887
Async XLA Ops:
  0.6 124.4 %copy-start.6 = (s32[8192]{0:T(1024)S(1)}, s32[8192]{0:T(1024)}, u32[]{:S(2)}) copy-start(s32[8192]{0:T(1024)} %param.18) | copy-start | bytes 98308
  0.7 124.4 %copy-start.7 = (s32[8192]{0:T(1024)S(1)}, s32[8192]{0:T(1024)}, u32[]{:S(2)}) copy-start(s32[8192]{0:T(1024)} %param.19) | copy-start | bytes 98308
  0.7 124.4 %copy-start.8 = (s32[8192]{0:T(1024)S(1)}, s32[8192]{0:T(1024)}, u32[]{:S(2)}) copy-start(s32[8192]{0:T(1024)} %param.20) | copy-start | bytes 98308
  0.7 124.4 %copy-start.9 = (f32[1,2,256]{2,1,0:T(2,128)S(1)}, f32[1,2,256]{2,1,0:T(2,128)}, u32[]{:S(2)}) copy-start(f32[1,2,256]{2,1,0:T(2,128)} %param.23) | copy-start | bytes 6148
  125.1 1.3 copy-start
  125.1 1.3 copy-start.4
  125.1 1.3 copy-start.5
  126.5 1.0 copy-start.1
  127.5 1.0 copy-start.2
  128.5 1.0 copy-start.3

commit v4 on v3

--- a/solution.py
+++ b/solution.py
@@ -49,15 +49,15 @@
     packing,
     inputs_ref,
     target_ref,
-    len_ref,
-    lat_ref,
-    land_ref,
+    len_hbm,
+    lat_hbm,
+    land_hbm,
     up_hbm,
     down_hbm,
-    gain_ref,
+    gain_hbm,
     grads_ref,
-    dgain_ref,
     stat_ref,
+    miss_ref,
     xin,
     xout,
     cin,
@@ -74,10 +74,15 @@
     rank_ref,
     q_ref,
     scale_ref,
+    weight_ref,
     loss_acc,
     gain_acc,
     wbuf,
     spread,
+    len_ref,
+    lat_ref,
+    land_ref,
+    gain_ref,
     up_ref,
     down_ref,
     acc,
@@ -127,10 +132,14 @@
     def peer(step):
         return (section, lax.rem(dp + step, groups))
 
-    up_copy = pltpu.make_async_copy(up_hbm, up_ref, weight_sem.at[0])
-    down_copy = pltpu.make_async_copy(down_hbm, down_ref, weight_sem.at[1])
-    up_copy.start()
-    down_copy.start()
+    sources = (up_hbm, down_hbm, gain_hbm, len_hbm, lat_hbm, land_hbm)
+    places = (up_ref, down_ref, gain_ref, len_ref, lat_ref, land_ref)
+    fetches = [
+        pltpu.make_async_copy(source, place, weight_sem.at[i])
+        for i, (source, place) in enumerate(zip(sources, places))
+    ]
+    for fetch in fetches:
+        fetch.start()
 
     barrier = pltpu.get_barrier_semaphore()
     for step in range(1, sections):
@@ -242,11 +251,12 @@
         total = wbuf[0]
         for other in range(1, groups):
             total = total + wbuf[other]
-        stat_ref[...] = total
+        weight_ref[...] = total
+        miss_ref[...] = (total[4:5, 0:1] > 0.0).astype(jnp.int32)
         scale_ref[...] = 2.0 / jnp.broadcast_to(total[0:1], (8, LANES))
 
-    up_copy.wait()
-    down_copy.wait()
+    for fetch in fetches:
+        fetch.wait()
     for layer in range(2):
         up_lo[layer] = (0.5 * up_ref[layer]).astype(bf16)
         down_lo[layer] = down_ref[layer].astype(bf16)
@@ -700,7 +710,6 @@
     total = small[0]
     for other in range(1, groups):
         total = total + small[other]
-    dgain_ref[...] = total[0:2]
     gain_squares = jnp.sum(total[0:2] * total[0:2], axis=(0, 1), keepdims=True)
     tiny[section] = jnp.where(tile_row < 4, total[2:3, 0:1], total[4:5, 0:1] + gain_squares)
     for step in range(1, sections):
@@ -714,14 +723,12 @@
     whole = tiny[0]
     for other in range(1, sections):
         whole = whole + tiny[other]
-    norm = jnp.sqrt(whole[4:5])
-    scale = jnp.minimum(1.0, clip_limit / norm)
-    stats = stat_ref[...]
-    stat_ref[...] = jnp.where(
-        tile_row == 0,
-        whole[0:1],
-        jnp.where(tile_row == 1, norm, jnp.where(tile_row == 2, scale, stats)),
-    )
+    norm = jnp.sqrt(whole[4:5, 0:1])
+    clip = jnp.minimum(1.0, clip_limit / norm)
+    stats = total
+    for row, number in ((2, clip), (3, whole[0:1, 0:1]), (4, weight_ref[0:1, 0:1]), (5, norm)):
+        stats = jnp.where(wide_row == row, number, stats)
+    stat_ref[...] = stats
 
     for step in range(1, groups):
         weight_copy(step).wait_send()
@@ -760,10 +767,10 @@
         functools.partial(rollout_kernel, sections, groups, packing),
         out_shape=(
             jax.ShapeDtypeStruct((4, feats, feats), f32),
-            jax.ShapeDtypeStruct((2, feats), f32),
-            jax.ShapeDtypeStruct((8, LANES), f32),
+            jax.ShapeDtypeStruct((8, feats), f32),
+            jax.ShapeDtypeStruct((1, 1), jnp.int32),
         ),
-        in_specs=[hbm, hbm, vmem, vmem, vmem, hbm, hbm, vmem],
+        in_specs=[hbm] * 8,
         out_specs=(hbm, vmem, vmem),
         scratch_shapes=[
             wide,
@@ -782,10 +789,15 @@
             pltpu.VMEM((grid_rows, LANES), f32),
             pltpu.VMEM((grid_rows, LANES), f32),
             pltpu.VMEM((8, LANES), f32),
+            pltpu.VMEM((8, LANES), f32),
             pltpu.VMEM((8, feats), f32),
             pltpu.VMEM((2, 8, feats), f32),
             pltpu.VMEM((groups, 8, LANES), f32),
             pltpu.VMEM((ROWS, feats), f32),
+            pltpu.VMEM((grid_rows, LANES), jnp.int32),
+            pltpu.VMEM((grid_rows, LANES), jnp.int32),
+            pltpu.VMEM((grid_rows, LANES), jnp.int32),
+            pltpu.VMEM((2, feats), f32),
             square,
             square,
             grads,
@@ -815,7 +827,7 @@
             dma((sections,)),
             dma((sections,)),
             dma((pieces,)),
-            dma((2,)),
+            dma((6,)),
         ],
         compiler_params=pltpu.CompilerParams(
             collective_id=0 if packing else 1,
@@ -838,18 +850,17 @@
 def adam_step(weights_old, gradient, moment_one, moment_two, decay_rate):
     moment_one = beta_one * moment_one + (1.0 - beta_one) * gradient
     moment_two = beta_two * moment_two + (1.0 - beta_two) * gradient * gradient
-    first_hat = moment_one / (1.0 - beta_one**STEP)
-    second_hat = moment_two / (1.0 - beta_two**STEP)
-    new_weights = weights_old - learn_rate * (
-        first_hat / (jnp.sqrt(second_hat) + adam_eps) + decay_rate * weights_old
-    )
+    second_hat = moment_two * (1.0 / (1.0 - beta_two**STEP))
+    root = second_hat * lax.rsqrt(second_hat)
+    pace = moment_one * (learn_rate / (1.0 - beta_one**STEP))
+    step = pace * pl.reciprocal(root + adam_eps)
+    new_weights = weights_old * (1.0 - learn_rate * decay_rate) - step
     return (new_weights, moment_one, moment_two)
 
 
 def update_kernel(
     grads_ref,
-    dgain_ref,
-    stat_ref,
+    stat_hbm,
     w_up,
     w_down,
     gains,
@@ -859,46 +870,94 @@
     v_up,
     v_down,
     v_gains,
-    *outs,
+    loss_out,
+    total_out,
+    norm_out,
+    new_up,
+    new_down,
+    new_gains,
+    new_m_up,
+    new_m_down,
+    new_m_gains,
+    new_v_up,
+    new_v_down,
+    new_v_gains,
+    held,
+    stat_ref,
+    gain_ref,
+    in_sem,
+    out_sem,
+    small_in,
+    small_out,
 ):
+    old = ((grads_ref, grads_ref), (w_up, w_down), (m_up, m_down), (v_up, v_down))
+    new = ((new_up, new_down), (new_m_up, new_m_down), (new_v_up, new_v_down))
+
+    def fetch(i, part):
+        source = old[part][i // 2].at[i if part == 0 else i % 2]
+        return pltpu.make_async_copy(source, held.at[part, i], in_sem.at[part, i])
+
+    def store(i, part):
+        return pltpu.make_async_copy(
+            held.at[part + 1, i], new[part][i // 2].at[i % 2], out_sem.at[part, i]
+        )
+
+    small_fetch = [pltpu.make_async_copy(stat_hbm, stat_ref, small_in.at[3])]
+    small_store = []
+    for part, (source, out) in enumerate(
+        ((gains, new_gains), (m_gains, new_m_gains), (v_gains, new_v_gains))
+    ):
+        small_fetch.append(pltpu.make_async_copy(source, gain_ref.at[part], small_in.at[part]))
+        small_store.append(pltpu.make_async_copy(gain_ref.at[part], out, small_out.at[part]))
+    for copy in small_fetch:
+        copy.start()
+    for i in range(4):
+        for part in range(4):
+            fetch(i, part).start()
+    for copy in small_fetch:
+        copy.wait()
     clip = stat_ref[2:3, 0:1]
-    matrices = ((0, w_up, m_up, v_up), (1, w_down, m_down, v_down))
-    for i, weight, one, two in matrices:
-        new = adam_step(weight[0], grads_ref[i, 0] * clip, one[0], two[0], weight_decay)
+    for row, out in ((3, loss_out), (4, total_out), (5, norm_out)):
+        out[...] = stat_ref[row : row + 1, 0:1]
+    fresh = adam_step(gain_ref[0], stat_ref[0:2] * clip, gain_ref[1], gain_ref[2], 0.0)
+    for part in range(3):
+        gain_ref[part] = fresh[part]
+        small_store[part].start()
+    for i in range(4):
+        for part in range(4):
+            fetch(i, part).wait()
+        fresh = adam_step(held[1, i], held[0, i] * clip, held[2, i], held[3, i], weight_decay)
         for part in range(3):
-            outs[3 * part + i][0] = new[part]
-
-    @pl.when(pl.program_id(0) == 0)
-    def _():
-        new = adam_step(gains[...], dgain_ref[...] * clip, m_gains[...], v_gains[...], 0.0)
+            held[part + 1, i] = fresh[part]
+            store(i, part).start()
+    for i in range(4):
         for part in range(3):
-            outs[3 * part + 2][...] = new[part]
-
-
-def update(grads, grad_gain, stats, *state):
-    layers, feats = grad_gain.shape
-    halves = 2
-    rows = feats // halves
-    grads = grads.reshape(2, layers, feats, feats)
-    matrix = pl.BlockSpec((1, rows, feats), lambda i: (i // halves, i % halves, 0))
-    small = pl.BlockSpec((layers, feats), lambda i: (0, 0))
-    specs = [matrix, matrix, small] * 3
-    shapes = [jax.ShapeDtypeStruct(a.shape[1:], f32) for a in state]
-    new = pl.pallas_call(
+            store(i, part).wait()
+    for copy in small_store:
+        copy.wait()
+
+
+def update(grads, stats, *state):
+    hbm = pl.BlockSpec(memory_space=pl.ANY)
+    vmem = pl.BlockSpec(memory_space=pltpu.VMEM)
+    return pl.pallas_call(
         update_kernel,
-        grid=(layers * halves,),
-        in_specs=[
-            pl.BlockSpec((2, 1, rows, feats), lambda i: (0, i // halves, i % halves, 0)),
-            small,
-            pl.BlockSpec((8, LANES), lambda i: (0, 0)),
-        ]
-        + specs,
-        out_specs=specs,
-        out_shape=shapes,
-        compiler_params=pltpu.CompilerParams(vmem_limit_bytes=32 * 1024 * 1024),
+        in_specs=[hbm] * 11,
+        out_specs=(vmem,) * 3 + (hbm,) * 9,
+        out_shape=(jax.ShapeDtypeStruct((1, 1), f32),) * 3
+        + tuple(jax.ShapeDtypeStruct(a.shape, f32) for a in state),
+        scratch_shapes=[
+            pltpu.VMEM((4,) + grads.shape, f32),
+            pltpu.VMEM(stats.shape, f32),
+            pltpu.VMEM((3,) + state[2].shape, f32),
+            pltpu.SemaphoreType.DMA((4, 4)),
+            pltpu.SemaphoreType.DMA((3, 4)),
+            pltpu.SemaphoreType.DMA((4,)),
+            pltpu.SemaphoreType.DMA((3,)),
+        ],
+        compiler_params=pltpu.CompilerParams(vmem_limit_bytes=63 * 1024 * 1024),
         name="update",
-    )(grads, grad_gain, stats, *(a[0] for a in state))
-    return tuple(a[None] for a in new)
+    )(grads, stats, *state)
 
 
 def per_device(
@@ -918,29 +977,19 @@
     v_gains,
 ):
     sections, groups = lax.axis_size("section"), lax.axis_size("dp")
-    operands = (inputs, targets[0], lengths, lat_index, land, w_up[0], w_down[0], gains[0])
+    state = tuple(
+        a[0] for a in (w_up, w_down, gains, m_up, m_down, m_gains, v_up, v_down, v_gains)
+    )
+    operands = (inputs, targets[0], lengths, lat_index, land) + state[:3]
     packed = rollout(True, sections, groups, *operands)
 
-    grads, grad_gain, stats = lax.cond(
-        packed[2][4, 0] > 0.0,
+    grads, stats, unused = lax.cond(
+        packed[2].reshape(()) > 0,
         lambda: rollout(False, sections, groups, *operands),
         lambda: packed,
     )
-    new = update(
-        grads,
-        grad_gain,
-        stats,
-        w_up,
-        w_down,
-        gains,
-        m_up,
-        m_down,
-        m_gains,
-        v_up,
-        v_down,
-        v_gains,
-    )
-    return (stats[0, 0], stats[3, 0], stats[1, 0]) + new
+    new = update(grads, stats, *state)
+    return tuple(a.reshape(()) for a in new[:3]) + tuple(a[None] for a in new[3:])
 
 
 def solution(mesh):

time: 135 us -> 128 us (0.948)
  local copies, waits for them, and re-layouts: 5.61 us -> 0.02 us
    unnamed x20 -> x10, local copies, waits for them, and re-layouts: 3.15 us -> 0.02 us
    slice x2 -> x0, local copies, waits for them, and re-layouts: 2.46 us -> none  [the longest x1 1.27 us: per_device(): return (stats[0, 0], stats[3, 0], stats[1, 0]) + new]
where the time goes in v4:
time: 128 us
  Pallas kernels  126 us (98%)
  between operations  1.55 us (1%)
    pallas_call x1, Pallas kernels, rollout(): pl.pallas_call(functools.partial(rollout_kernel, sections, groups, packin...  122 us
    pallas_call x1, Pallas kernels, update(): pl.pallas_call(update_kernel, in_specs=[hbm] * 11, out_specs=(vmem,) * 3...  3.92 us

profile of v4, /device:TPU:0, one launch (start us, length us, event | category | flops | bytes accessed | tf_op | source)
XLA Modules:
  0.0 127.9 jit_solution(3479408846376219790)
XLA Ops:
  0.6 0.0 copy-start
  0.7 0.0 copy-start.1
  0.7 0.0 copy-start.2
  0.7 0.0 copy-start.3
  0.7 0.0 copy-start.4
  0.7 122.1 %rollout_packed.1 = (f32[4,256,256]{2,1,0:T(8,128)}, f32[8,256]{1,0:T(8,128)S(1)}, s32[1,1]{1,0:T(1,128)}) custom-call(f32[8192,256]{1,0:T(8,128)} %inputs_ref.1, f32[8192,256]{1,0:T(8,128)} %bitcast.29, s32[64,128]{1,0:T(8,128)} %bitcast.41, s32[64,128]{1,0:T(8,128)} %bitcast.43, s32[64,128]{1,0:T(8,128)} %bitcast.45, f32[2,256,256]{2,1,0:T(8,128)} %bitcast.31, ...), custom_call_target="tpu_custom_call" | custom-call | tf_op jit(solution)/shard_map/rollout_packed/pallas_call | solution.py:766
  123.5 0.0 copy-done
  123.5 0.0 copy-done.1
  123.5 0.0 copy-done.2
  123.5 0.0 copy-done.3
  123.5 0.0 copy-done.4
  123.5 0.2 conditional.1
  123.8 3.9 %update.1 = (f32[1,1]{1,0:T(1,128)}, f32[1,1]{1,0:T(1,128)}, f32[1,1]{1,0:T(1,128)}, f32[2,256,256]{2,1,0:T(8,128)}, f32[2,256,256]{2,1,0:T(8,128)}, /*index=5*/...) custom-call(f32[4,256,256]{2,1,0:T(8,128)} %get-tuple-element.62.gra, ...), custom_call_target="tpu_custom_call" | custom-call | tf_op jit(solution)/shard_map/update/pallas_call | solution.py:943
Async XLA Ops:
  0.6 122.8 %copy-start = (f32[1,2,256,256]{3,2,1,0:T(8,128)S(1)}, f32[1,2,256,256]{3,2,1,0:T(8,128)}, u32[]{:S(2)}) copy-start(f32[1,2,256,256]{3,2,1,0:T(8,128)} %param.21) | copy-start | bytes 1572868
  0.7 122.8 %copy-start.1 = (s32[8192]{0:T(1024)S(1)}, s32[8192]{0:T(1024)}, u32[]{:S(2)}) copy-start(s32[8192]{0:T(1024)} %param.18) | copy-start | bytes 98308
  0.7 122.8 %copy-start.2 = (s32[8192]{0:T(1024)S(1)}, s32[8192]{0:T(1024)}, u32[]{:S(2)}) copy-start(s32[8192]{0:T(1024)} %param.19) | copy-start | bytes 98308
  0.7 122.8 %copy-start.3 = (s32[8192]{0:T(1024)S(1)}, s32[8192]{0:T(1024)}, u32[]{:S(2)}) copy-start(s32[8192]{0:T(1024)} %param.20) | copy-start | bytes 98308
  0.7 122.8 %copy-start.4 = (f32[1,2,256]{2,1,0:T(2,128)S(1)}, f32[1,2,256]{2,1,0:T(2,128)}, u32[]{:S(2)}) copy-start(f32[1,2,256]{2,1,0:T(2,128)} %param.23) | copy-start | bytes 6148

commit v5 on v4

--- a/solution.py
+++ b/solution.py
@@ -26,7 +26,8 @@
 ROWS = 512
 SPARE = 80
 WINDOW = 1536
-SAVE_BYTES = 21 * 1024 * 1024
+SAVE_BYTES = 19 * 1024 * 1024
+NEAR = 4
 
 
 def dot(a, b):
@@ -63,7 +64,7 @@
     cin,
     tgt,
     packed,
-    save_x,
+    near,
     save_h,
     save_d,
     qring,
@@ -124,7 +125,8 @@
     total_packed = chunks * prows
     expand = live_rows + 512
     last = sections - 1
-    ring = save_x.shape[0] // ROWS
+    ring = save_h.shape[1] // ROWS
+    ring_packed = near.shape[0] // prows
     natural = section < (2 if packing else sections)
     plain_next = (section == 0) if packing else (section < last)
     packs = (section == 1) if packing else (section < 0)
@@ -159,15 +161,29 @@
         rows = rows_at(i * ROWS, ROWS)
         return pltpu.make_async_copy(target_ref.at[rows], tgt.at[rows], tgt_sem.at[i])
 
+    def near_copy(i):
+        place = rows_at(lax.rem(i, NEAR) * ROWS, ROWS)
+        return pltpu.make_async_copy(
+            target_ref.at[rows_at(i * ROWS, ROWS)], near.at[place], tgt_sem.at[i]
+        )
+
     @pl.when(section == 0)
     def _():
         @pl.loop(0, chunks)
         def _(i):
             input_copy(i).start()
 
-    @pl.loop(0, chunks)
-    def _(i):
-        target_copy(i).start()
+    @pl.when(natural)
+    def _():
+        @pl.loop(0, NEAR)
+        def _(i):
+            near_copy(i).start()
+
+    @pl.when(jnp.logical_not(natural))
+    def _():
+        @pl.loop(0, chunks)
+        def _(i):
+            target_copy(i).start()
 
     def prepare_backward():
         for layer in range(2):
@@ -284,11 +300,11 @@
             hits.append(source_row == rank_ref[pl.ds(k * (ROWS // LANES) + i, 1), :] - base)
         return dot_lhs_t(as_onehot(hits), cin[rows_at(start, expand), :].astype(bf16))
 
-    def forward(rows, saved):
+    def forward(rows, saved, keep):
         x = xin[rows, :]
         for layer in range(2):
             if layer == 1:
-                save_x[saved, :] = x
+                keep[...] = x
             r = lax.rsqrt(jnp.mean(x * x, -1, keepdims=True) + norm_eps)
             normed = (x * r * gain_ref[layer : layer + 1]).astype(bf16)
             half = dot(normed, up_lo[layer])
@@ -308,13 +324,13 @@
         loss_acc[...] += jnp.sum((weighted * diff).reshape(size // 8, 8, feats), 0)
         return weighted * scale_ref[0:1, 0:1]
 
-    def backward(size, rows, saved, g):
+    def backward(size, rows, saved, keep, g):
         for layer in (1, 0):
             low = g.astype(bf16)
             acc[2 + layer] += dot_lhs_t(save_h[layer, saved, :], low)
             pull = dot(low, down_t[layer])
             g_pre = (pull * save_d[layer, saved, :].astype(f32)).astype(bf16)
-            x = save_x[saved, :] if layer == 1 else xin[rows, :]
+            x = keep[...] if layer == 1 else xin[rows, :]
             r = lax.rsqrt(jnp.mean(x * x, -1, keepdims=True) + norm_eps)
             gain = gain_ref[layer : layer + 1]
             xr = x * r
@@ -414,7 +430,7 @@
 
                 rows = rows_at(t * ROWS, ROWS)
                 saved = rows_at(lax.rem(t, ring) * ROWS, ROWS)
-                forward(rows, saved)
+                forward(rows, saved, tgt.at[saved])
 
                 @pl.when(plain_next)
                 def _():
@@ -445,8 +461,9 @@
                 def _():
                     finish_weights()
 
-                target_copy(k).wait()
+                near_copy(k).wait()
                 rows = rows_at(k * ROWS, ROWS)
+                place = rows_at(lax.rem(k, NEAR) * ROWS, ROWS)
                 saved = rows_at(lax.rem(k, ring) * ROWS, ROWS)
 
                 @pl.when(plain_next)
@@ -482,9 +499,14 @@
                     ],
                     axis=0,
                 )
-                diff = xout[rows, :] - tgt[rows, :]
-                g = loss_part(ROWS, diff, weight) + spread[...]
-                backward(ROWS, rows, saved, g)
+                diff = xout[rows, :] - near[place, :]
+                spread[...] += loss_part(ROWS, diff, weight)
+
+                @pl.when(k + NEAR < chunks)
+                def _():
+                    near_copy(k + NEAR).start()
+
+                backward(ROWS, rows, saved, tgt.at[saved], spread[...])
 
                 @pl.when(section > 0)
                 def _():
@@ -510,7 +532,7 @@
 
         @pl.when(jnp.logical_not(natural))
         def _():
-            lag = last - section
+            lag = jnp.minimum(2 * (last - section), min(ring_packed, qring.shape[0]) - 1)
             prepare_columns()
             prepare_backward()
 
@@ -545,7 +567,8 @@
                     )
                     packed_receive(prows, t)
                     saved = rows_at(lax.rem(t, ring) * ROWS, prows)
-                    forward(rows, saved)
+                    kept = rows_at(lax.rem(t, ring_packed) * prows, prows)
+                    forward(rows, saved, near.at[kept])
 
                     @pl.when(section < last)
                     def _():
@@ -569,7 +592,8 @@
                         cot_copy(prows, k).wait_recv()
                         spread[0:prows, :] += cin[rows, :]
 
-                    backward(prows, rows, saved, spread[0:prows, :])
+                    kept = rows_at(lax.rem(k, ring_packed) * prows, prows)
+                    backward(prows, rows, saved, near.at[kept], spread[0:prows, :])
                     cot_do(prows, k, lambda copy: copy.start())
 
             @pl.loop(0, chunks)
@@ -588,7 +612,7 @@
     pieces = range(4 * halves)
     matrix = [m for m in (3, 1, 2, 0) for _ in range(halves)]
     first = [PIECE * (p % halves) for p in pieces]
-    ysum = save_x
+    ysum = near
 
     def y_copy(p, step):
         to = lax.rem(y + step, width)
@@ -751,7 +775,7 @@
     prows = ROWS * (sections - 2) // sections + 16
     grid_rows = columns // LANES
     packed_bytes = 4 * chunks * prows * feats
-    ring = (SAVE_BYTES - packed_bytes) // (12 * ROWS * feats)
+    ring = min((SAVE_BYTES - packed_bytes) // (8 * ROWS * feats), chunks)
     depth = min(4, groups)
     width = groups // depth
     pieces = 4 * feats // PIECE
@@ -778,7 +802,7 @@
             wide,
             wide,
             pltpu.VMEM((chunks * prows if packing else 8, feats), f32),
-            pltpu.VMEM((ring * ROWS, feats), f32),
+            pltpu.VMEM((NEAR * ROWS, feats), f32),
             pltpu.VMEM((2, ring * ROWS, feats), bf16),
             pltpu.VMEM((2, ring * ROWS, feats), bf16),
             pltpu.VMEM((sections, prows, LANES), f32),

time: 128 us -> 122 us (0.953)
  Pallas kernels: 126 us -> 120 us
    pallas_call x1, Pallas kernels: 122 us -> 116 us  [rollout(): pl.pallas_call(functools.partial(rollout_kernel, sections, groups, packin...]
where the time goes in v5:
time: 122 us; the launch traced here: 121 us
  Pallas kernels  120 us (98%)
  between operations  1.55 us (1%)
    pallas_call x1, Pallas kernels, rollout(): pl.pallas_call(functools.partial(rollout_kernel, sections, groups, packin...  116 us
    pallas_call x1, Pallas kernels, update(): pl.pallas_call(update_kernel, in_specs=[hbm] * 11, out_specs=(vmem,) * 3...  3.92 us

profile of v5, /device:TPU:0, one launch (start us, length us, event | category | flops | bytes accessed | tf_op | source)
XLA Modules:
  0.0 121.3 jit_solution(1549451320842497063)
XLA Ops:
  0.6 0.0 copy-start
  0.7 0.0 copy-start.1
  0.7 0.0 copy-start.2
  0.7 0.0 copy-start.3
  0.7 0.0 copy-start.4
  0.7 115.6 %rollout_packed.1 = (f32[4,256,256]{2,1,0:T(8,128)}, f32[8,256]{1,0:T(8,128)S(1)}, s32[1,1]{1,0:T(1,128)}) custom-call(f32[8192,256]{1,0:T(8,128)} %inputs_ref.1, f32[8192,256]{1,0:T(8,128)} %bitcast.29, s32[64,128]{1,0:T(8,128)} %bitcast.41, s32[64,128]{1,0:T(8,128)} %bitcast.43, s32[64,128]{1,0:T(8,128)} %bitcast.45, f32[2,256,256]{2,1,0:T(8,128)} %bitcast.31, ...), custom_call_target="tpu_custom_call" | custom-call | tf_op jit(solution)/shard_map/rollout_packed/pallas_call | solution.py:790
  116.9 0.0 copy-done
  116.9 0.0 copy-done.1
  117.0 0.0 copy-done.2
  117.0 0.0 copy-done.3
  117.0 0.0 copy-done.4
  117.0 0.2 conditional.1
  117.2 3.9 %update.1 = (f32[1,1]{1,0:T(1,128)}, f32[1,1]{1,0:T(1,128)}, f32[1,1]{1,0:T(1,128)}, f32[2,256,256]{2,1,0:T(8,128)}, f32[2,256,256]{2,1,0:T(8,128)}, /*index=5*/...) custom-call(f32[4,256,256]{2,1,0:T(8,128)} %get-tuple-element.62.gra, ...), custom_call_target="tpu_custom_call" | custom-call | tf_op jit(solution)/shard_map/update/pallas_call | solution.py:967
Async XLA Ops:
  0.6 116.3 %copy-start = (f32[1,2,256,256]{3,2,1,0:T(8,128)S(1)}, f32[1,2,256,256]{3,2,1,0:T(8,128)}, u32[]{:S(2)}) copy-start(f32[1,2,256,256]{3,2,1,0:T(8,128)} %param.21) | copy-start | bytes 1572868
  0.7 116.3 %copy-start.1 = (s32[8192]{0:T(1024)S(1)}, s32[8192]{0:T(1024)}, u32[]{:S(2)}) copy-start(s32[8192]{0:T(1024)} %param.18) | copy-start | bytes 98308
  0.7 116.3 %copy-start.2 = (s32[8192]{0:T(1024)S(1)}, s32[8192]{0:T(1024)}, u32[]{:S(2)}) copy-start(s32[8192]{0:T(1024)} %param.19) | copy-start | bytes 98308
  0.7 116.3 %copy-start.3 = (s32[8192]{0:T(1024)S(1)}, s32[8192]{0:T(1024)}, u32[]{:S(2)}) copy-start(s32[8192]{0:T(1024)} %param.20) | copy-start | bytes 98308
  0.7 116.3 %copy-start.4 = (f32[1,2,256]{2,1,0:T(2,128)S(1)}, f32[1,2,256]{2,1,0:T(2,128)}, u32[]{:S(2)}) copy-start(f32[1,2,256]{2,1,0:T(2,128)} %param.23) | copy-start | bytes 6148

commit v6 on v5

--- a/solution.py
+++ b/solution.py
@@ -26,7 +26,7 @@
 ROWS = 512
 SPARE = 80
 WINDOW = 1536
-SAVE_BYTES = 19 * 1024 * 1024
+SAVE_BYTES = 18 * 1024 * 1024
 NEAR = 4
 
 
@@ -84,12 +84,9 @@
     lat_ref,
     land_ref,
     gain_ref,
-    up_ref,
-    down_ref,
     acc,
-    final,
-    ybuf,
-    zbuf,
+    gain_land,
+    land,
     small,
     tiny,
     in_sem,
@@ -100,20 +97,20 @@
     ct_recv,
     w_send,
     w_recv,
-    y_send,
-    y_recv,
-    z_send,
-    z_recv,
-    za_send,
-    za_recv,
-    ya_send,
-    ya_recv,
+    rs_send,
+    rs_recv,
+    ag_send,
+    ag_recv,
     small_send,
     small_recv,
     tiny_send,
     tiny_recv,
     out_sem,
     weight_sem,
+    mate_send,
+    mate_recv,
+    pair_send,
+    pair_recv,
 ):
     section = lax.axis_index("section")
     dp = lax.axis_index("dp")
@@ -125,8 +122,11 @@
     total_packed = chunks * prows
     expand = live_rows + 512
     last = sections - 1
+    core = lax.rem(section, 2)
+    mate = section + 1 - 2 * core
+    final = acc.at[pl.ds(4, 4)]
+    up_ref, down_ref = acc.at[pl.ds(0, 2)], acc.at[pl.ds(2, 2)]
     ring = save_h.shape[1] // ROWS
-    ring_packed = near.shape[0] // prows
     natural = section < (2 if packing else sections)
     plain_next = (section == 0) if packing else (section < last)
     packs = (section == 1) if packing else (section < 0)
@@ -135,7 +135,7 @@
         return (section, lax.rem(dp + step, groups))
 
     sources = (up_hbm, down_hbm, gain_hbm, len_hbm, lat_hbm, land_hbm)
-    places = (up_ref, down_ref, gain_ref, len_ref, lat_ref, land_ref)
+    places = (up_ref, down_ref, gain_ref.at[0], len_ref, lat_ref, land_ref)
     fetches = [
         pltpu.make_async_copy(source, place, weight_sem.at[i])
         for i, (source, place) in enumerate(zip(sources, places))
@@ -169,7 +169,7 @@
 
     @pl.when(section == 0)
     def _():
-        @pl.loop(0, chunks)
+        @pl.loop(0, NEAR)
         def _(i):
             input_copy(i).start()
 
@@ -189,10 +189,63 @@
         for layer in range(2):
             up_t[layer] = up_ref[layer].T.astype(bf16)
             down_t[layer] = (0.5 * down_ref[layer]).T.astype(bf16)
-            gain_acc[layer] = jnp.zeros((8, feats), f32)
+        gain_acc[...] = jnp.zeros_like(gain_acc)
+        loss_acc[...] = jnp.zeros_like(loss_acc)
         for i in range(4):
             acc[i] = jnp.zeros((feats, feats), f32)
-        loss_acc[...] = jnp.zeros_like(loss_acc)
+
+    def mate_weight(i):
+        source = gain_ref.at[0] if i == 4 else acc.at[i]
+        place = gain_ref.at[1] if i == 4 else acc.at[4 + i]
+        return pltpu.make_async_remote_copy(
+            src_ref=source,
+            dst_ref=place,
+            send_sem=mate_send.at[i],
+            recv_sem=mate_recv.at[i],
+            device_id=(mate, dp),
+            device_id_type=MESH,
+        )
+
+    def prepare_mate():
+        for i in range(5):
+            mate_weight(i).wait_recv()
+        for layer in range(2):
+            up = acc[4 + layer]
+            down = acc[6 + layer]
+            up_lo[2 + layer] = (0.5 * up).astype(bf16)
+            down_lo[2 + layer] = down.astype(bf16)
+            up_t[2 + layer] = up.T.astype(bf16)
+            down_t[2 + layer] = (0.5 * down).T.astype(bf16)
+        for i in range(4, 8):
+            acc[i] = jnp.zeros((feats, feats), f32)
+
+    def mate_gradient(i):
+        if i < 4:
+            source = acc.at[4 + i]
+            place = xin.at[pl.ds(columns - (4 - i) * feats, feats)]
+        else:
+            source, place = gain_acc.at[pl.ds(2, 2)], gain_land
+        return pltpu.make_async_remote_copy(
+            src_ref=source,
+            dst_ref=place,
+            send_sem=mate_send.at[5 + i],
+            recv_sem=mate_recv.at[5 + i],
+            device_id=(mate, dp),
+            device_id_type=MESH,
+        )
+
+    def pair_copy(j):
+        return pltpu.make_async_remote_copy(
+            src_ref=packed.at[rows_at(j * prows, prows)],
+            dst_ref=cin.at[rows_at(swapped(j) * prows, prows)],
+            send_sem=pair_send.at[j],
+            recv_sem=pair_recv.at[j],
+            device_id=(mate, dp),
+            device_id_type=MESH,
+        )
+
+    def swapped(j):
+        return j + 1 - 2 * lax.rem(j, 2)
 
     grid_rows = columns // LANES
     tile_row = lax.broadcasted_iota(jnp.int32, (8, LANES), 0)
@@ -221,7 +274,8 @@
         length = len_ref[...]
         latitude = (lat_ref[...].astype(f32) + 0.5) * (math.pi / NLAT) - math.pi / 2
         area = jnp.cos(latitude) * (1.0 + land_ref[...].astype(f32))
-        q_ref[...] = area * (section < length).astype(f32)
+        q_ref[0] = area * (section < length).astype(f32)
+        q_ref[1] = area * (mate < length).astype(f32)
         local_weight = jnp.sum(
             area * jnp.minimum(length, sections).astype(f32), axis=(0, 1), keepdims=True
         )
@@ -300,22 +354,22 @@
             hits.append(source_row == rank_ref[pl.ds(k * (ROWS // LANES) + i, 1), :] - base)
         return dot_lhs_t(as_onehot(hits), cin[rows_at(start, expand), :].astype(bf16))
 
-    def forward(rows, saved, keep):
-        x = xin[rows, :]
+    def forward(source, place, owner, saved, keep):
+        x = source[...]
         for layer in range(2):
             if layer == 1:
                 keep[...] = x
             r = lax.rsqrt(jnp.mean(x * x, -1, keepdims=True) + norm_eps)
-            normed = (x * r * gain_ref[layer : layer + 1]).astype(bf16)
-            half = dot(normed, up_lo[layer])
+            normed = (x * r * gain_ref[owner, layer : layer + 1]).astype(bf16)
+            half = dot(normed, up_lo[2 * owner + layer])
             t = jnp.tanh(half)
             a = 1.0 + t
             h = half * a
             hidden = h.astype(bf16)
             save_h[layer, saved, :] = hidden
             save_d[layer, saved, :] = (a + h * (1.0 - t)).astype(bf16)
-            x = x + dot(hidden, down_lo[layer])
-        xout[rows, :] = x
+            x = x + dot(hidden, down_lo[2 * owner + layer])
+        place[...] = x
 
     def loss_part(size, diff, weight):
         weighted = jnp.concatenate(
@@ -324,46 +378,51 @@
         loss_acc[...] += jnp.sum((weighted * diff).reshape(size // 8, 8, feats), 0)
         return weighted * scale_ref[0:1, 0:1]
 
-    def backward(size, rows, saved, keep, g):
+    def backward(size, source, place, owner, saved, keep, g):
         for layer in (1, 0):
             low = g.astype(bf16)
-            acc[2 + layer] += dot_lhs_t(save_h[layer, saved, :], low)
-            pull = dot(low, down_t[layer])
+            acc[4 * owner + 2 + layer] += dot_lhs_t(save_h[layer, saved, :], low)
+            pull = dot(low, down_t[2 * owner + layer])
             g_pre = (pull * save_d[layer, saved, :].astype(f32)).astype(bf16)
-            x = keep[...] if layer == 1 else xin[rows, :]
+            x = keep[...] if layer == 1 else source[...]
             r = lax.rsqrt(jnp.mean(x * x, -1, keepdims=True) + norm_eps)
-            gain = gain_ref[layer : layer + 1]
+            gain = gain_ref[owner, layer : layer + 1]
             xr = x * r
             normed = (xr * gain).astype(bf16)
-            acc[layer] += dot_lhs_t(normed, g_pre)
-            g_normed = dot(g_pre, up_t[layer])
+            acc[4 * owner + layer] += dot_lhs_t(normed, g_pre)
+            g_normed = dot(g_pre, up_t[2 * owner + layer])
             prod = g_normed * xr
-            gain_acc[layer] += jnp.sum(prod.reshape(size // 8, 8, feats), 0)
+            gain_acc[2 * owner + layer] += jnp.sum(prod.reshape(size // 8, 8, feats), 0)
             mean = jnp.mean(prod * gain, -1, keepdims=True)
             g = g + r * (gain * g_normed - xr * mean)
-        xin[rows, :] = g
-
-    def state_copy(source, size, i, count=None):
+        place[...] = g
+
+    def state_copy(source, size, i, to, count=None):
         rows = rows_at(i * size, size if count is None else count)
         return pltpu.make_async_remote_copy(
             src_ref=source.at[rows],
             dst_ref=xin.at[rows],
             send_sem=st_send.at[i],
             recv_sem=st_recv.at[i],
-            device_id=(lax.rem(section + 1, sections), dp),
+            device_id=(to, dp),
             device_id_type=MESH,
         )
 
-    def cot_copy(size, i, count=None):
+    def cot_copy(size, i, to, count=None):
         rows = rows_at(i * size, size if count is None else count)
         return pltpu.make_async_remote_copy(
             src_ref=xin.at[rows],
             dst_ref=cin.at[rows],
             send_sem=ct_send.at[i],
             recv_sem=ct_recv.at[i],
-            device_id=(lax.rem(section + sections - 1, sections), dp),
+            device_id=(to, dp),
             device_id_type=MESH,
         )
+
+    up_one = lax.rem(section + 1, sections)
+    down_one = lax.rem(section + sections - 1, sections)
+    up_chip = lax.rem(section + 2, sections)
+    down_chip = jnp.where(section < 4, 1, section - 2)
 
     def shorter(copy, size, i, action):
         @pl.when(i < chunks - 1)
@@ -375,43 +434,43 @@
             action(copy(size, i, size - SPARE))
 
     def packed_state(size, i, count):
-        return state_copy(packed, size, i, count)
+        return state_copy(packed, size, i, 2 + lax.rem(i, 2), count)
 
     def packed_receive(size, i):
-        @pl.when(section == 2)
+        @pl.when(section < 4)
         def _():
             shorter(packed_state, size, i, lambda copy: copy.wait_recv())
 
-        @pl.when(section > 2)
+        @pl.when(section >= 4)
         def _():
-            state_copy(xout, size, i).wait_recv()
+            state_copy(xout, size, i, up_chip).wait_recv()
 
     def cot_part(size, i, count):
-        return cot_copy(size, i, count)
+        return cot_copy(size, i, down_chip, count)
 
     def cot_wait(size, i):
         shorter(cot_part, size, i, lambda copy: copy.wait_recv())
 
     def cot_do(size, i, action):
-        @pl.when(section == 2)
+        @pl.when(section < 4)
         def _():
             shorter(cot_part, size, i, action)
 
-        @pl.when(section > 2)
+        @pl.when(section >= 4)
         def _():
-            action(cot_copy(size, i))
+            action(cot_copy(size, i, down_chip))
 
     @pl.when(natural)
     def _():
         if packing:
-            lag = jnp.where(section == 0, ring - 1, ring - 3)
+            most = chunks if ring == chunks else ring - 1
+            lag = jnp.where(section == 0, most, most - 2)
         else:
             lag = jnp.minimum(ring - 1, 3 * (last - section))
 
         @pl.when(section > 0)
         def _():
             prepare_columns()
-            prepare_backward()
             if packing:
                 xout[2 * ROWS : WINDOW, :] = jnp.zeros((WINDOW - 2 * ROWS, feats), f32)
                 cin[total_packed - SPARE : total_packed, :] = jnp.zeros((SPARE, feats), f32)
@@ -424,17 +483,21 @@
                 def _():
                     input_copy(t).wait()
 
+                    @pl.when(t + NEAR < chunks)
+                    def _():
+                        input_copy(t + NEAR).start()
+
                 @pl.when(section > 0)
                 def _():
-                    state_copy(xout, ROWS, t).wait_recv()
+                    state_copy(xout, ROWS, t, up_one).wait_recv()
 
                 rows = rows_at(t * ROWS, ROWS)
                 saved = rows_at(lax.rem(t, ring) * ROWS, ROWS)
-                forward(rows, saved, tgt.at[saved])
+                forward(xin.at[rows], xout.at[rows], 0, saved, tgt.at[saved])
 
                 @pl.when(plain_next)
                 def _():
-                    state_copy(xout, ROWS, t).start()
+                    state_copy(xout, ROWS, t, up_one).start()
 
             if packing:
 
@@ -451,6 +514,9 @@
             @pl.when((section == 0) & (t == 3))
             def _():
                 prepare_columns()
+
+            @pl.when(t == jnp.minimum(lag, 4))
+            def _():
                 prepare_backward()
 
             k = t - lag
@@ -466,57 +532,51 @@
                 place = rows_at(lax.rem(k, NEAR) * ROWS, ROWS)
                 saved = rows_at(lax.rem(k, ring) * ROWS, ROWS)
 
-                @pl.when(plain_next)
-                def _():
-                    cot_copy(ROWS, k).wait_recv()
-                    spread[...] = cin[rows, :]
-
-                if packing:
-
-                    @pl.when(packs)
-                    def _():
-                        had = jnp.where(k == 0, -1, chunks_for(jnp.maximum(k - 1, 0)))
-                        for i in range(3):
-
-                            @pl.when(had + 1 + i <= chunks_for(k))
-                            def _():
-                                cot_wait(prows, had + 1 + i)
-
-                        spread[...] = unpack_rows(k)
-
-                else:
-
-                    @pl.when(section == last)
-                    def _():
-                        spread[...] = jnp.zeros_like(spread)
-
                 weight = jnp.concatenate(
                     [
                         jnp.broadcast_to(
-                            q_ref[pl.ds(k * (ROWS // LANES) + i, 1), :], (LANES, LANES)
+                            q_ref[0, pl.ds(k * (ROWS // LANES) + i, 1), :], (LANES, LANES)
                         ).T
                         for i in range(ROWS // LANES)
                     ],
                     axis=0,
                 )
                 diff = xout[rows, :] - near[place, :]
-                spread[...] += loss_part(ROWS, diff, weight)
+                spread[...] = loss_part(ROWS, diff, weight)
 
                 @pl.when(k + NEAR < chunks)
                 def _():
                     near_copy(k + NEAR).start()
 
-                backward(ROWS, rows, saved, tgt.at[saved], spread[...])
+                @pl.when(plain_next)
+                def _():
+                    cot_copy(ROWS, k, down_one).wait_recv()
+                    spread[...] += cin[rows, :]
+
+                if packing:
+
+                    @pl.when(packs)
+                    def _():
+                        had = jnp.where(k == 0, -1, chunks_for(jnp.maximum(k - 1, 0)))
+                        for i in range(3):
+
+                            @pl.when(had + 1 + i <= chunks_for(k))
+                            def _():
+                                cot_wait(prows, had + 1 + i)
+
+                        spread[...] += unpack_rows(k)
+
+                backward(ROWS, xin.at[rows], xin.at[rows], 0, saved, tgt.at[saved], spread[...])
 
                 @pl.when(section > 0)
                 def _():
-                    cot_copy(ROWS, k).start()
+                    cot_copy(ROWS, k, down_one).start()
 
         @pl.loop(0, chunks)
         def _(i):
             @pl.when(plain_next)
             def _():
-                state_copy(xout, ROWS, i).wait_send()
+                state_copy(xout, ROWS, i, up_one).wait_send()
 
             if packing:
 
@@ -526,141 +586,197 @@
 
             @pl.when(section > 0)
             def _():
-                cot_copy(ROWS, i).wait_send()
+                cot_copy(ROWS, i, down_one).wait_send()
 
     if packing:
 
         @pl.when(jnp.logical_not(natural))
         def _():
-            lag = jnp.minimum(2 * (last - section), min(ring_packed, qring.shape[0]) - 1)
+            turns = chunks // 2
+            final_chip = section >= sections - 2
+            lag = jnp.where(final_chip, 0, 1)
+            for i in range(5):
+                mate_weight(i).start()
             prepare_columns()
+            for i in range(5):
+                mate_weight(i).wait_send()
             prepare_backward()
-
-            @pl.when(section == 2)
+            prepare_mate()
+
+            @pl.when(section < 4)
             def _():
                 xin[total_packed - SPARE : total_packed, :] = jnp.zeros((SPARE, feats), f32)
 
-
-            @pl.loop(0, chunks + lag)
-            def _(t):
-                @pl.when(t < chunks)
+            def pack_target(j):
+                start, first, hits = pack_matrix(j)
+                packed[rows_at(j * prows, prows), :] = split_dot(
+                    dot, as_onehot(hits), tgt[rows_at(start, WINDOW), :]
+                )
+                return first, hits
+
+            def places(turn):
+                j = 2 * turn + core
+                slot = 2 * lax.rem(turn, 2)
+                rows, other = rows_at(j * prows, prows), rows_at(swapped(j) * prows, prows)
+                saved = [rows_at((slot + part) * ROWS, prows) for part in range(2)]
+                keep = [near.at[rows_at((slot + part) * prows, prows)] for part in range(2)]
+                return j, slot, rows, other, saved, keep
+
+            @pl.loop(0, turns + lag)
+            def _(turn):
+                @pl.when(turn < turns)
                 def _():
-                    @pl.when(t == 0)
+                    @pl.when(turn == 0)
                     def _():
                         target_copy(0).wait()
                         target_copy(1).wait()
 
-                    @pl.when(t + 2 < chunks)
+                    for i in range(2, 4):
+
+                        @pl.when(2 * turn + i < chunks)
+                        def _():
+                            target_copy(2 * turn + i).wait()
+
+                    j, slot, rows, other, saved, keep = places(turn)
+                    pack_target(swapped(j))
+                    pair_copy(swapped(j)).start()
+                    first, hits = pack_target(j)
+                    for part in range(2):
+                        owner = jnp.where(core == part, 0, 1)
+                        weight = jnp.zeros((prows, LANES), f32)
+                        for i, hit in enumerate(hits):
+                            weight += jnp.where(hit, q_ref[owner, pl.ds(first + i, 1), :], 0.0)
+                        qring[slot + part] = jnp.broadcast_to(
+                            jnp.sum(weight, -1, keepdims=True), (prows, LANES)
+                        )
+                    packed_receive(prows, j)
+                    forward(xin.at[rows], xout.at[other], core, saved[0], keep[0])
+                    forward(xout.at[other], xout.at[rows], 1 - core, saved[1], keep[1])
+
+                    @pl.when(jnp.logical_not(final_chip))
                     def _():
-                        target_copy(t + 2).wait()
-
-                    start, first, hits = pack_matrix(t)
-                    rows = rows_at(t * prows, prows)
-                    packed[rows, :] = split_dot(
-                        dot, as_onehot(hits), tgt[rows_at(start, WINDOW), :]
-                    )
-                    weight = jnp.zeros((prows, LANES), f32)
-                    for i, hit in enumerate(hits):
-                        weight += jnp.where(hit, q_ref[pl.ds(first + i, 1), :], 0.0)
-                    qring[lax.rem(t, sections)] = jnp.broadcast_to(
-                        jnp.sum(weight, -1, keepdims=True), (prows, LANES)
-                    )
-                    packed_receive(prows, t)
-                    saved = rows_at(lax.rem(t, ring) * ROWS, prows)
-                    kept = rows_at(lax.rem(t, ring_packed) * prows, prows)
-                    forward(rows, saved, near.at[kept])
-
-                    @pl.when(section < last)
-                    def _():
-                        state_copy(xout, prows, t).start()
-
-                k = t - lag
-
-                @pl.when(k >= 0)
+                        state_copy(xout, prows, j, up_chip).start()
+
+                @pl.when(turn >= lag)
                 def _():
-                    @pl.when(k == 0)
+                    @pl.when(turn == lag)
                     def _():
                         finish_weights()
 
-                    rows = rows_at(k * prows, prows)
-                    saved = rows_at(lax.rem(k, ring) * ROWS, prows)
-                    diff = xout[rows, :] - packed[rows, :]
-                    spread[0:prows, :] = loss_part(prows, diff, qring[lax.rem(k, sections)])
-
-                    @pl.when(section < last)
+                    j, slot, rows, other, saved, keep = places(turn - lag)
+                    part_rows = pl.ds(0, prows)
+                    pair_copy(j).wait_recv()
+
+                    def error(part, out):
+                        here = core == part
+                        target = jnp.where(here, packed[rows, :], cin[other, :])
+                        return loss_part(prows, out - target, qring[slot + part])
+
+                    spread[part_rows, :] = error(1, xout[rows, :])
+
+                    @pl.when(jnp.logical_not(final_chip))
                     def _():
-                        cot_copy(prows, k).wait_recv()
-                        spread[0:prows, :] += cin[rows, :]
-
-                    kept = rows_at(lax.rem(k, ring_packed) * prows, prows)
-                    backward(prows, rows, saved, near.at[kept], spread[0:prows, :])
-                    cot_do(prows, k, lambda copy: copy.start())
-
-            @pl.loop(0, chunks)
-            def _(i):
-                cot_do(prows, i, lambda copy: copy.wait_send())
-
-                @pl.when(section < last)
+                        cot_copy(prows, j, down_chip).wait_recv()
+                        spread[part_rows, :] += cin[rows, :]
+
+                    backward(
+                        prows,
+                        xout.at[other],
+                        spread.at[part_rows],
+                        1 - core,
+                        saved[1],
+                        keep[1],
+                        spread[part_rows, :],
+                    )
+                    g = error(0, xout[other, :]) + spread[part_rows, :]
+                    backward(prows, xin.at[rows], xin.at[rows], core, saved[0], keep[0], g)
+                    cot_do(prows, j, lambda copy: copy.start())
+
+            @pl.loop(0, turns)
+            def _(turn):
+                j = 2 * turn + core
+                cot_do(prows, j, lambda copy: copy.wait_send())
+                pair_copy(swapped(j)).wait_send()
+
+                @pl.when(jnp.logical_not(final_chip))
                 def _():
-                    state_copy(xout, prows, i).wait_send()
-
-    depth = min(4, groups)
-    width = groups // depth
-    y, z = lax.rem(dp, width), dp // width
-    ypart, zpart = PIECE // width, PIECE // groups
+                    state_copy(xout, prows, j, up_chip).wait_send()
+
+            for i in range(5):
+                mate_gradient(i).start()
+            for i in range(5):
+                mate_gradient(i).wait_recv()
+                if i < 4:
+                    acc[i] += xin[columns - (4 - i) * feats : columns - (3 - i) * feats, :]
+                else:
+                    gain_acc[0:2] += gain_land[...]
+            for i in range(5):
+                mate_gradient(i).wait_send()
+
+    bits = groups.bit_length() - 1
     halves = feats // PIECE
     pieces = range(4 * halves)
     matrix = [m for m in (3, 1, 2, 0) for _ in range(halves)]
     first = [PIECE * (p % halves) for p in pieces]
-    ysum = near
-
-    def y_copy(p, step):
-        to = lax.rem(y + step, width)
-        i = p * width + step
+
+    def bit_order(p):
+        order = list(range(bits))
+        if bits > 1 and p % 4 == 3:
+            order[0], order[1] = order[1], order[0]
+        return order
+
+    def bit_value(bit):
+        return lax.rem(dp // 2**bit, 2)
+
+    def kept_start(p, step):
+        start = 0
+        for i in range(step):
+            start = start + bit_value(bit_order(p)[i]) * (PIECE >> (i + 1))
+        return start
+
+    def across(p, step):
+        bit = bit_order(p)[step]
+        return (section, dp + (1 - 2 * bit_value(bit)) * 2**bit)
+
+    def reduce_copy(p, step):
+        size = PIECE >> (step + 1)
+        away = 1 - bit_value(bit_order(p)[step])
+        start = kept_start(p, step) + away * size
+        if step == 0:
+            source = acc.at[matrix[p], rows_at(first[p] + start, size, 8)]
+        else:
+            source = near.at[rows_at(p * PIECE + start, size, 8)]
         return pltpu.make_async_remote_copy(
-            src_ref=acc.at[matrix[p], rows_at(first[p] + to * ypart, ypart)],
-            dst_ref=ybuf.at[p * (width - 1) + step - 1],
-            send_sem=y_send.at[i],
-            recv_sem=y_recv.at[i],
-            device_id=(section, z * width + to),
+            src_ref=source,
+            dst_ref=land.at[p, pl.ds(PIECE - (PIECE >> step), size)],
+            send_sem=rs_send.at[p * bits + step],
+            recv_sem=rs_recv.at[p * bits + step],
+            device_id=across(p, step),
             device_id_type=MESH,
         )
 
-    def z_copy(p, step):
-        to = lax.rem(z + step, depth)
-        i = p * depth + step
-        return pltpu.make_async_remote_copy(
-            src_ref=ysum.at[rows_at(p * ypart + to * zpart, zpart)],
-            dst_ref=zbuf.at[p * (depth - 1) + step - 1],
-            send_sem=z_send.at[i],
-            recv_sem=z_recv.at[i],
-            device_id=(section, to * width + y),
-            device_id_type=MESH,
-        )
-
-    def z_back(p, step):
-        to = lax.rem(z + step, depth)
-        i = p * depth + step
-        rows = rows_at(first[p] + y * ypart + z * zpart, zpart)
+    def reduce_add(p, step):
+        size = PIECE >> (step + 1)
+        start = kept_start(p, step + 1)
+        if step == 0:
+            own = acc[matrix[p], rows_at(first[p] + start, size, 8), :]
+        else:
+            own = near[rows_at(p * PIECE + start, size, 8), :]
+        own = own + land[p, PIECE - (PIECE >> step) : PIECE - (PIECE >> (step + 1)), :]
+        if step == bits - 1:
+            final[matrix[p], rows_at(first[p] + start, size, 8), :] = own
+        else:
+            near[rows_at(p * PIECE + start, size, 8), :] = own
+        return own
+
+    def gather_copy(p, step):
+        rows = rows_at(first[p] + kept_start(p, step + 1), PIECE >> (step + 1), 8)
         return pltpu.make_async_remote_copy(
             src_ref=final.at[matrix[p], rows],
             dst_ref=final.at[matrix[p], rows],
-            send_sem=za_send.at[i],
-            recv_sem=za_recv.at[i],
-            device_id=(section, to * width + y),
-            device_id_type=MESH,
-        )
-
-    def y_back(p, step):
-        to = lax.rem(y + step, width)
-        i = p * width + step
-        rows = rows_at(first[p] + y * ypart, ypart)
-        return pltpu.make_async_remote_copy(
-            src_ref=final.at[matrix[p], rows],
-            dst_ref=final.at[matrix[p], rows],
-            send_sem=ya_send.at[i],
-            recv_sem=ya_recv.at[i],
-            device_id=(section, z * width + to),
+            send_sem=ag_send.at[p * bits + step],
+            recv_sem=ag_recv.at[p * bits + step],
+            device_id=across(p, step),
             device_id_type=MESH,
         )
 
@@ -691,26 +807,17 @@
         )
 
     for p in pieces:
-        for step in range(1, width):
-            y_copy(p, step).start()
-    for p in pieces:
-        own = acc[matrix[p], rows_at(first[p] + y * ypart, ypart), :]
-        for step in range(1, width):
-            y_copy(p, step).wait_recv()
-            own = own + ybuf[p * (width - 1) + step - 1]
-        ysum[p * ypart : (p + 1) * ypart, :] = own
-        for step in range(1, depth):
-            z_copy(p, step).start()
+        reduce_copy(p, 0).start()
     squares = jnp.zeros((1, 1), f32)
-    for p in pieces:
-        own = ysum[rows_at(p * ypart + z * zpart, zpart), :]
-        for step in range(1, depth):
-            z_copy(p, step).wait_recv()
-            own = own + zbuf[p * (depth - 1) + step - 1]
-        final[matrix[p], rows_at(first[p] + y * ypart + z * zpart, zpart), :] = own
-        squares = squares + jnp.sum(own * own, axis=(0, 1), keepdims=True)
-        for step in range(1, depth):
-            z_back(p, step).start()
+    for step in range(bits):
+        for p in pieces:
+            reduce_copy(p, step).wait_recv()
+            own = reduce_add(p, step)
+            if step < bits - 1:
+                reduce_copy(p, step + 1).start()
+            else:
+                gather_copy(p, step).start()
+                squares = squares + jnp.sum(own * own, axis=(0, 1), keepdims=True)
     loss = jnp.sum(loss_acc[...], axis=(0, 1), keepdims=True)
     wide_row = lax.broadcasted_iota(jnp.int32, (8, feats), 0)
     small[dp] = jnp.where(
@@ -724,11 +831,10 @@
     )
     for step in range(1, groups):
         small_copy(step).start()
-    for p in pieces:
-        for step in range(1, depth):
-            z_back(p, step).wait_recv()
-        for step in range(1, width):
-            y_back(p, step).start()
+    for step in range(bits - 1, 0, -1):
+        for p in pieces:
+            gather_copy(p, step).wait_recv()
+            gather_copy(p, step - 1).start()
     for step in range(1, groups):
         small_copy(step).wait_recv()
     total = small[0]
@@ -739,8 +845,7 @@
     for step in range(1, sections):
         tiny_copy(step).start()
     for p in pieces:
-        for step in range(1, width):
-            y_back(p, step).wait_recv()
+        gather_copy(p, 0).wait_recv()
         out_copy(p).start()
     for step in range(1, sections):
         tiny_copy(step).wait_recv()
@@ -761,12 +866,9 @@
         tiny_copy(step).wait_send()
     for p in pieces:
         out_copy(p).wait()
-        for step in range(1, width):
-            y_copy(p, step).wait_send()
-            y_back(p, step).wait_send()
-        for step in range(1, depth):
-            z_copy(p, step).wait_send()
-            z_back(p, step).wait_send()
+        for step in range(bits):
+            reduce_copy(p, step).wait_send()
+            gather_copy(p, step).wait_send()
 
 
 def rollout(packing, sections, groups, inputs, target, lengths, lat_index, land, w_up, w_down, gains):
@@ -776,16 +878,13 @@
     grid_rows = columns // LANES
     packed_bytes = 4 * chunks * prows * feats
     ring = min((SAVE_BYTES - packed_bytes) // (8 * ROWS * feats), chunks)
-    depth = min(4, groups)
-    width = groups // depth
+    bits = groups.bit_length() - 1
     pieces = 4 * feats // PIECE
     hbm = pl.BlockSpec(memory_space=pl.ANY)
     vmem = pl.BlockSpec(memory_space=pltpu.VMEM)
     dma = pltpu.SemaphoreType.DMA
     wide = pltpu.VMEM((columns, feats), f32)
-    lows = pltpu.VMEM((2, feats, feats), bf16)
-    grads = pltpu.VMEM((4, feats, feats), f32)
-    square = pltpu.VMEM((2, feats, feats), f32)
+    lows = pltpu.VMEM((4, feats, feats), bf16)
     flat = lambda array: array.reshape(grid_rows, LANES)
     return pl.pallas_call(
         functools.partial(rollout_kernel, sections, groups, packing),
@@ -811,23 +910,20 @@
             lows,
             lows,
             pltpu.VMEM((grid_rows, LANES), f32),
-            pltpu.VMEM((grid_rows, LANES), f32),
+            pltpu.VMEM((2, grid_rows, LANES), f32),
             pltpu.VMEM((8, LANES), f32),
             pltpu.VMEM((8, LANES), f32),
             pltpu.VMEM((8, feats), f32),
-            pltpu.VMEM((2, 8, feats), f32),
+            pltpu.VMEM((4, 8, feats), f32),
             pltpu.VMEM((groups, 8, LANES), f32),
             pltpu.VMEM((ROWS, feats), f32),
             pltpu.VMEM((grid_rows, LANES), jnp.int32),
             pltpu.VMEM((grid_rows, LANES), jnp.int32),
             pltpu.VMEM((grid_rows, LANES), jnp.int32),
-            pltpu.VMEM((2, feats), f32),
-            square,
-            square,
-            grads,
-            grads,
-            pltpu.VMEM((max(pieces * (width - 1), 1), PIECE // width, feats), f32),
-            pltpu.VMEM((pieces * (depth - 1), PIECE // groups, feats), f32),
+            pltpu.VMEM((2, 2, feats), f32),
+            pltpu.VMEM((8, feats, feats), f32),
+            pltpu.VMEM((2, 8, feats), f32),
+            pltpu.VMEM((pieces, PIECE, feats), f32),
             pltpu.VMEM((groups, 8, feats), f32),
             pltpu.VMEM((sections, 8, LANES), f32),
             dma((chunks,)),
@@ -838,20 +934,20 @@
             dma((chunks,)),
             dma((groups,)),
             dma((groups,)),
-            dma((pieces * width,)),
-            dma((pieces * width,)),
-            dma((pieces * depth,)),
-            dma((pieces * depth,)),
-            dma((pieces * depth,)),
-            dma((pieces * depth,)),
-            dma((pieces * width,)),
-            dma((pieces * width,)),
+            dma((pieces * bits,)),
+            dma((pieces * bits,)),
+            dma((pieces * bits,)),
+            dma((pieces * bits,)),
             dma((groups,)),
             dma((groups,)),
             dma((sections,)),
             dma((sections,)),
             dma((pieces,)),
             dma((6,)),
+            dma((10,)),
+            dma((10,)),
+            dma((chunks,)),
+            dma((chunks,)),
         ],
         compiler_params=pltpu.CompilerParams(
             collective_id=0 if packing else 1,

time: 122 us -> 117 us (0.959)
  Pallas kernels: 120 us -> 115 us
    pallas_call x1, Pallas kernels: 116 us -> 111 us  [rollout(): pl.pallas_call(functools.partial(rollout_kernel, sections, groups, packin...]
where the time goes in v6:
time: 117 us
  Pallas kernels  115 us (98%)
  between operations  1.55 us (1%)
    pallas_call x1, Pallas kernels, rollout(): pl.pallas_call(functools.partial(rollout_kernel, sections, groups, packin...  111 us
    pallas_call x1, Pallas kernels, update(): pl.pallas_call(update_kernel, in_specs=[hbm] * 11, out_specs=(vmem,) * 3...  3.92 us

profile of v6, /device:TPU:0, one launch (start us, length us, event | category | flops | bytes accessed | tf_op | source)
XLA Modules:
  0.0 117.1 jit_solution(8997916122709378969)
XLA Ops:
  0.6 0.0 copy-start
  0.7 0.0 copy-start.1
  0.7 0.0 copy-start.2
  0.7 0.0 copy-start.3
  0.7 0.0 copy-start.4
  0.7 111.4 %rollout_packed.1 = (f32[4,256,256]{2,1,0:T(8,128)}, f32[8,256]{1,0:T(8,128)S(1)}, s32[1,1]{1,0:T(1,128)}) custom-call(f32[8192,256]{1,0:T(8,128)} %inputs_ref.1, f32[8192,256]{1,0:T(8,128)} %bitcast.29, s32[64,128]{1,0:T(8,128)} %bitcast.41, s32[64,128]{1,0:T(8,128)} %bitcast.43, s32[64,128]{1,0:T(8,128)} %bitcast.45, f32[2,256,256]{2,1,0:T(8,128)} %bitcast.31, ...), custom_call_target="tpu_custom_call" | custom-call | tf_op jit(solution)/shard_map/rollout_packed/pallas_call | solution.py:889
  112.7 0.0 copy-done
  112.7 0.0 copy-done.1
  112.7 0.0 copy-done.2
  112.7 0.0 copy-done.3
  112.8 0.0 copy-done.4
  112.8 0.2 conditional.1
  113.0 3.9 %update.1 = (f32[1,1]{1,0:T(1,128)}, f32[1,1]{1,0:T(1,128)}, f32[1,1]{1,0:T(1,128)}, f32[2,256,256]{2,1,0:T(8,128)}, f32[2,256,256]{2,1,0:T(8,128)}, /*index=5*/...) custom-call(f32[4,256,256]{2,1,0:T(8,128)} %get-tuple-element.62.gra, ...), custom_call_target="tpu_custom_call" | custom-call | tf_op jit(solution)/shard_map/update/pallas_call | solution.py:1063
Async XLA Ops:
  0.6 112.1 %copy-start = (f32[1,2,256,256]{3,2,1,0:T(8,128)S(1)}, f32[1,2,256,256]{3,2,1,0:T(8,128)}, u32[]{:S(2)}) copy-start(f32[1,2,256,256]{3,2,1,0:T(8,128)} %param.21) | copy-start | bytes 1572868
  0.7 112.1 %copy-start.1 = (s32[8192]{0:T(1024)S(1)}, s32[8192]{0:T(1024)}, u32[]{:S(2)}) copy-start(s32[8192]{0:T(1024)} %param.18) | copy-start | bytes 98308
  0.7 112.1 %copy-start.2 = (s32[8192]{0:T(1024)S(1)}, s32[8192]{0:T(1024)}, u32[]{:S(2)}) copy-start(s32[8192]{0:T(1024)} %param.19) | copy-start | bytes 98308
  0.7 112.1 %copy-start.3 = (s32[8192]{0:T(1024)S(1)}, s32[8192]{0:T(1024)}, u32[]{:S(2)}) copy-start(s32[8192]{0:T(1024)} %param.20) | copy-start | bytes 98308
  0.7 112.1 %copy-start.4 = (f32[1,2,256]{2,1,0:T(2,128)S(1)}, f32[1,2,256]{2,1,0:T(2,128)}, u32[]{:S(2)}) copy-start(f32[1,2,256]{2,1,0:T(2,128)} %param.23) | copy-start | bytes 6148

commit v7 on v6

--- a/solution.py
+++ b/solution.py
@@ -26,8 +26,9 @@
 ROWS = 512
 SPARE = 80
 WINDOW = 1536
-SAVE_BYTES = 18 * 1024 * 1024
-NEAR = 4
+SAVE_BYTES = 17 * 1024 * 1024
+SLOTS = 10
+NEAR = 3
 
 
 def dot(a, b):
@@ -236,7 +237,7 @@
 
     def pair_copy(j):
         return pltpu.make_async_remote_copy(
-            src_ref=packed.at[rows_at(j * prows, prows)],
+            src_ref=packed.at[slot_rows(j, prows)],
             dst_ref=cin.at[rows_at(swapped(j) * prows, prows)],
             send_sem=pair_send.at[j],
             recv_sem=pair_recv.at[j],
@@ -244,6 +245,9 @@
             device_id_type=MESH,
         )
 
+    def slot_rows(j, count):
+        return rows_at(lax.rem(j, SLOTS) * prows, count)
+
     def swapped(j):
         return j + 1 - 2 * lax.rem(j, 2)
 
@@ -255,7 +259,9 @@
         return jnp.clip(ROWS * (j - 1) + shift, 0, columns - WINDOW)
 
     def expand_start(k):
-        return jnp.clip(live_rows * k - 272, 0, total_packed - expand)
+        end = live_rows * k + expand - 288
+        end = jnp.where(k >= 11, jnp.minimum(end, prows * (k + 1)), end)
+        return jnp.clip(end - expand, 0, total_packed - expand)
 
     def chunks_for(k):
         return (expand_start(k) + expand - 1) // prows
@@ -308,7 +314,7 @@
                 ready = ROWS * (j + 2 if j < 7 else j + 3)
                 missed |= member & ((place < start) | (place >= min(start + WINDOW, ready)))
             row_chunk = lax.broadcasted_iota(jnp.int32, (grid_rows, LANES), 0) // (ROWS // LANES)
-            row_start = jnp.clip(live_rows * row_chunk - 272, 0, total_packed - expand)
+            row_start = expand_start(row_chunk)
             missed |= beyond & ((rank_i < row_start) | (rank_i >= row_start + expand))
             misses = jnp.sum(missed.astype(f32), axis=(0, 1), keepdims=True)
         wbuf[dp] = jnp.where(tile_row < 4, local_weight, misses)
@@ -434,7 +440,14 @@
             action(copy(size, i, size - SPARE))
 
     def packed_state(size, i, count):
-        return state_copy(packed, size, i, 2 + lax.rem(i, 2), count)
+        return pltpu.make_async_remote_copy(
+            src_ref=packed.at[slot_rows(i, count)],
+            dst_ref=xin.at[rows_at(i * size, count)],
+            send_sem=st_send.at[i],
+            recv_sem=st_recv.at[i],
+            device_id=(2 + lax.rem(i, 2), dp),
+            device_id_type=MESH,
+        )
 
     def packed_receive(size, i):
         @pl.when(section < 4)
@@ -506,7 +519,12 @@
                 @pl.when(packs & (t >= 1) & (t != 8) & (j < chunks))
                 def _():
                     start, _, hits = pack_matrix(j)
-                    packed[rows_at(j * prows, prows), :] = split_dot(
+
+                    @pl.when(j >= SLOTS)
+                    def _():
+                        shorter(packed_state, prows, j - SLOTS, lambda copy: copy.wait_send())
+
+                    packed[slot_rows(j, prows), :] = split_dot(
                         dot, as_onehot(hits), xout[rows_at(start, WINDOW), :]
                     )
                     shorter(packed_state, prows, j, lambda copy: copy.start())
@@ -580,7 +598,7 @@
 
             if packing:
 
-                @pl.when(packs)
+                @pl.when(packs & (i + SLOTS >= chunks))
                 def _():
                     shorter(packed_state, prows, i, lambda copy: copy.wait_send())
 
@@ -609,7 +627,7 @@
 
             def pack_target(j):
                 start, first, hits = pack_matrix(j)
-                packed[rows_at(j * prows, prows), :] = split_dot(
+                packed[slot_rows(j, prows), :] = split_dot(
                     dot, as_onehot(hits), tgt[rows_at(start, WINDOW), :]
                 )
                 return first, hits
@@ -638,6 +656,11 @@
                             target_copy(2 * turn + i).wait()
 
                     j, slot, rows, other, saved, keep = places(turn)
+
+                    @pl.when(swapped(j) >= SLOTS)
+                    def _():
+                        pair_copy(swapped(j) - SLOTS).wait_send()
+
                     pack_target(swapped(j))
                     pair_copy(swapped(j)).start()
                     first, hits = pack_target(j)
@@ -669,7 +692,7 @@
 
                     def error(part, out):
                         here = core == part
-                        target = jnp.where(here, packed[rows, :], cin[other, :])
+                        target = jnp.where(here, packed[slot_rows(j, prows), :], cin[other, :])
                         return loss_part(prows, out - target, qring[slot + part])
 
                     spread[part_rows, :] = error(1, xout[rows, :])
@@ -696,7 +719,10 @@
             def _(turn):
                 j = 2 * turn + core
                 cot_do(prows, j, lambda copy: copy.wait_send())
-                pair_copy(swapped(j)).wait_send()
+
+                @pl.when(swapped(j) + SLOTS >= chunks)
+                def _():
+                    pair_copy(swapped(j)).wait_send()
 
                 @pl.when(jnp.logical_not(final_chip))
                 def _():
@@ -721,7 +747,7 @@
 
     def bit_order(p):
         order = list(range(bits))
-        if bits > 1 and p % 4 == 3:
+        if bits > 1 and p % 2 == 0:
             order[0], order[1] = order[1], order[0]
         return order
 
@@ -876,7 +902,7 @@
     chunks = columns // ROWS
     prows = ROWS * (sections - 2) // sections + 16
     grid_rows = columns // LANES
-    packed_bytes = 4 * chunks * prows * feats
+    packed_bytes = 4 * SLOTS * prows * feats
     ring = min((SAVE_BYTES - packed_bytes) // (8 * ROWS * feats), chunks)
     bits = groups.bit_length() - 1
     pieces = 4 * feats // PIECE
@@ -900,8 +926,8 @@
             wide,
             wide,
             wide,
-            pltpu.VMEM((chunks * prows if packing else 8, feats), f32),
-            pltpu.VMEM((NEAR * ROWS, feats), f32),
+            pltpu.VMEM((SLOTS * prows if packing else 8, feats), f32),
+            pltpu.VMEM((max(NEAR * ROWS, 4 * prows), feats), f32),
             pltpu.VMEM((2, ring * ROWS, feats), bf16),
             pltpu.VMEM((2, ring * ROWS, feats), bf16),
             pltpu.VMEM((sections, prows, LANES), f32),

time: 117 us -> 112 us (0.957)
  Pallas kernels: 115 us -> 110 us
    pallas_call x1, Pallas kernels: 111 us -> 106 us  [rollout(): pl.pallas_call(functools.partial(rollout_kernel, sections, groups, packin...]
where the time goes in v7:
time: 112 us
  Pallas kernels  110 us (98%)
  between operations  1.55 us (1%)
    pallas_call x1, Pallas kernels, rollout(): pl.pallas_call(functools.partial(rollout_kernel, sections, groups, packin...  106 us
    pallas_call x1, Pallas kernels, update(): pl.pallas_call(update_kernel, in_specs=[hbm] * 11, out_specs=(vmem,) * 3...  3.92 us

profile of v7, /device:TPU:0, one launch (start us, length us, event | category | flops | bytes accessed | tf_op | source)
XLA Modules:
  0.0 111.7 jit_solution(7595957694615665585)
XLA Ops:
  0.6 0.0 copy-start
  0.7 0.0 copy-start.1
  0.7 0.0 copy-start.2
  0.7 0.0 copy-start.3
  0.7 0.0 copy-start.4
  0.7 106.0 %rollout_packed.1 = (f32[4,256,256]{2,1,0:T(8,128)}, f32[8,256]{1,0:T(8,128)S(1)}, s32[1,1]{1,0:T(1,128)}) custom-call(f32[8192,256]{1,0:T(8,128)} %inputs_ref.1, f32[8192,256]{1,0:T(8,128)} %bitcast.29, s32[64,128]{1,0:T(8,128)} %bitcast.41, s32[64,128]{1,0:T(8,128)} %bitcast.43, s32[64,128]{1,0:T(8,128)} %bitcast.45, f32[2,256,256]{2,1,0:T(8,128)} %bitcast.31, ...), custom_call_target="tpu_custom_call" | custom-call | tf_op jit(solution)/shard_map/rollout_packed/pallas_call | solution.py:915
  107.4 0.0 copy-done
  107.4 0.0 copy-done.1
  107.4 0.0 copy-done.2
  107.4 0.0 copy-done.3
  107.4 0.0 copy-done.4
  107.4 0.2 conditional.1
  107.6 3.9 %update.1 = (f32[1,1]{1,0:T(1,128)}, f32[1,1]{1,0:T(1,128)}, f32[1,1]{1,0:T(1,128)}, f32[2,256,256]{2,1,0:T(8,128)}, f32[2,256,256]{2,1,0:T(8,128)}, /*index=5*/...) custom-call(f32[4,256,256]{2,1,0:T(8,128)} %get-tuple-element.62.gra, ...), custom_call_target="tpu_custom_call" | custom-call | tf_op jit(solution)/shard_map/update/pallas_call | solution.py:1089
Async XLA Ops:
  0.6 106.7 %copy-start = (f32[1,2,256,256]{3,2,1,0:T(8,128)S(1)}, f32[1,2,256,256]{3,2,1,0:T(8,128)}, u32[]{:S(2)}) copy-start(f32[1,2,256,256]{3,2,1,0:T(8,128)} %param.21) | copy-start | bytes 1572868
  0.7 106.7 %copy-start.1 = (s32[8192]{0:T(1024)S(1)}, s32[8192]{0:T(1024)}, u32[]{:S(2)}) copy-start(s32[8192]{0:T(1024)} %param.18) | copy-start | bytes 98308
  0.7 106.7 %copy-start.2 = (s32[8192]{0:T(1024)S(1)}, s32[8192]{0:T(1024)}, u32[]{:S(2)}) copy-start(s32[8192]{0:T(1024)} %param.19) | copy-start | bytes 98308
  0.7 106.7 %copy-start.3 = (s32[8192]{0:T(1024)S(1)}, s32[8192]{0:T(1024)}, u32[]{:S(2)}) copy-start(s32[8192]{0:T(1024)} %param.20) | copy-start | bytes 98308
  0.7 106.7 %copy-start.4 = (f32[1,2,256]{2,1,0:T(2,128)S(1)}, f32[1,2,256]{2,1,0:T(2,128)}, u32[]{:S(2)}) copy-start(f32[1,2,256]{2,1,0:T(2,128)} %param.23) | copy-start | bytes 6148

commit v8 on v7

--- a/solution.py
+++ b/solution.py
@@ -747,8 +747,8 @@
 
     def bit_order(p):
         order = list(range(bits))
-        if bits > 1 and p % 2 == 0:
-            order[0], order[1] = order[1], order[0]
+        if p % 2 == 0:
+            order.insert(0, order.pop(min(2 - p % 4 // 2, bits - 1)))
         return order
 
     def bit_value(bit):

time: 112 us -> 111 us (level)
    pallas_call x1, Pallas kernels: 106 us -> 105 us  [rollout(): pl.pallas_call(functools.partial(rollout_kernel, sections, groups, packin...]
where the time goes in v8:
time: 111 us
  Pallas kernels  109 us (98%)
  between operations  1.55 us (1%)
    pallas_call x1, Pallas kernels, rollout(): pl.pallas_call(functools.partial(rollout_kernel, sections, groups, packin...  105 us
    pallas_call x1, Pallas kernels, update(): pl.pallas_call(update_kernel, in_specs=[hbm] * 11, out_specs=(vmem,) * 3...  3.92 us

profile of v8, /device:TPU:0, one launch (start us, length us, event | category | flops | bytes accessed | tf_op | source)
XLA Modules:
  0.0 110.6 jit_solution(15079837861229371714)
XLA Ops:
  0.6 0.0 copy-start
  0.7 0.0 copy-start.1
  0.7 0.0 copy-start.2
  0.7 0.0 copy-start.3
  0.7 0.0 copy-start.4
  0.7 104.9 %rollout_packed.1 = (f32[4,256,256]{2,1,0:T(8,128)}, f32[8,256]{1,0:T(8,128)S(1)}, s32[1,1]{1,0:T(1,128)}) custom-call(f32[8192,256]{1,0:T(8,128)} %inputs_ref.1, f32[8192,256]{1,0:T(8,128)} %bitcast.29, s32[64,128]{1,0:T(8,128)} %bitcast.41, s32[64,128]{1,0:T(8,128)} %bitcast.43, s32[64,128]{1,0:T(8,128)} %bitcast.45, f32[2,256,256]{2,1,0:T(8,128)} %bitcast.31, ...), custom_call_target="tpu_custom_call" | custom-call | tf_op jit(solution)/shard_map/rollout_packed/pallas_call | solution.py:915
  106.2 0.0 copy-done
  106.2 0.0 copy-done.1
  106.2 0.0 copy-done.2
  106.3 0.0 copy-done.3
  106.3 0.0 copy-done.4
  106.3 0.2 conditional.1
  106.5 3.9 %update.1 = (f32[1,1]{1,0:T(1,128)}, f32[1,1]{1,0:T(1,128)}, f32[1,1]{1,0:T(1,128)}, f32[2,256,256]{2,1,0:T(8,128)}, f32[2,256,256]{2,1,0:T(8,128)}, /*index=5*/...) custom-call(f32[4,256,256]{2,1,0:T(8,128)} %get-tuple-element.62.gra, ...), custom_call_target="tpu_custom_call" | custom-call | tf_op jit(solution)/shard_map/update/pallas_call | solution.py:1089
Async XLA Ops:
  0.6 105.6 %copy-start = (f32[1,2,256,256]{3,2,1,0:T(8,128)S(1)}, f32[1,2,256,256]{3,2,1,0:T(8,128)}, u32[]{:S(2)}) copy-start(f32[1,2,256,256]{3,2,1,0:T(8,128)} %param.21) | copy-start | bytes 1572868
  0.7 105.6 %copy-start.1 = (s32[8192]{0:T(1024)S(1)}, s32[8192]{0:T(1024)}, u32[]{:S(2)}) copy-start(s32[8192]{0:T(1024)} %param.18) | copy-start | bytes 98308
  0.7 105.6 %copy-start.2 = (s32[8192]{0:T(1024)S(1)}, s32[8192]{0:T(1024)}, u32[]{:S(2)}) copy-start(s32[8192]{0:T(1024)} %param.19) | copy-start | bytes 98308
  0.7 105.6 %copy-start.3 = (s32[8192]{0:T(1024)S(1)}, s32[8192]{0:T(1024)}, u32[]{:S(2)}) copy-start(s32[8192]{0:T(1024)} %param.20) | copy-start | bytes 98308
  0.7 105.6 %copy-start.4 = (f32[1,2,256]{2,1,0:T(2,128)S(1)}, f32[1,2,256]{2,1,0:T(2,128)}, u32[]{:S(2)}) copy-start(f32[1,2,256]{2,1,0:T(2,128)} %param.23) | copy-start | bytes 6148

commit v9 on v8

--- a/solution.py
+++ b/solution.py
@@ -590,22 +590,6 @@
                 def _():
                     cot_copy(ROWS, k, down_one).start()
 
-        @pl.loop(0, chunks)
-        def _(i):
-            @pl.when(plain_next)
-            def _():
-                state_copy(xout, ROWS, i, up_one).wait_send()
-
-            if packing:
-
-                @pl.when(packs & (i + SLOTS >= chunks))
-                def _():
-                    shorter(packed_state, prows, i, lambda copy: copy.wait_send())
-
-            @pl.when(section > 0)
-            def _():
-                cot_copy(ROWS, i, down_one).wait_send()
-
     if packing:
 
         @pl.when(jnp.logical_not(natural))
@@ -714,19 +698,6 @@
                     g = error(0, xout[other, :]) + spread[part_rows, :]
                     backward(prows, xin.at[rows], xin.at[rows], core, saved[0], keep[0], g)
                     cot_do(prows, j, lambda copy: copy.start())
-
-            @pl.loop(0, turns)
-            def _(turn):
-                j = 2 * turn + core
-                cot_do(prows, j, lambda copy: copy.wait_send())
-
-                @pl.when(swapped(j) + SLOTS >= chunks)
-                def _():
-                    pair_copy(swapped(j)).wait_send()
-
-                @pl.when(jnp.logical_not(final_chip))
-                def _():
-                    state_copy(xout, prows, j, up_chip).wait_send()
 
             for i in range(5):
                 mate_gradient(i).start()
@@ -884,6 +855,41 @@
     for row, number in ((2, clip), (3, whole[0:1, 0:1]), (4, weight_ref[0:1, 0:1]), (5, norm)):
         stats = jnp.where(wide_row == row, number, stats)
     stat_ref[...] = stats
+
+    @pl.when(natural)
+    def _():
+        @pl.loop(0, chunks)
+        def _(i):
+            @pl.when(plain_next)
+            def _():
+                state_copy(xout, ROWS, i, up_one).wait_send()
+
+            if packing:
+
+                @pl.when(packs & (i + SLOTS >= chunks))
+                def _():
+                    shorter(packed_state, prows, i, lambda copy: copy.wait_send())
+
+            @pl.when(section > 0)
+            def _():
+                cot_copy(ROWS, i, down_one).wait_send()
+
+    if packing:
+
+        @pl.when(jnp.logical_not(natural))
+        def _():
+            @pl.loop(0, chunks // 2)
+            def _(turn):
+                j = 2 * turn + core
+                cot_do(prows, j, lambda copy: copy.wait_send())
+
+                @pl.when(swapped(j) + SLOTS >= chunks)
+                def _():
+                    pair_copy(swapped(j)).wait_send()
+
+                @pl.when(section < sections - 2)
+                def _():
+                    state_copy(xout, prows, j, up_chip).wait_send()
 
     for step in range(1, groups):
         weight_copy(step).wait_send()

time: 111 us -> 110 us (level)
  no operation moved by 1% of the time
where the time goes in v9:
time: 110 us
  Pallas kernels  108 us (98%)
  between operations  1.55 us (1%)
    pallas_call x1, Pallas kernels, rollout(): pl.pallas_call(functools.partial(rollout_kernel, sections, groups, packin...  104 us
    pallas_call x1, Pallas kernels, update(): pl.pallas_call(update_kernel, in_specs=[hbm] * 11, out_specs=(vmem,) * 3...  3.92 us

profile of v9, /device:TPU:0, one launch (start us, length us, event | category | flops | bytes accessed | tf_op | source)
XLA Modules:
  0.0 109.8 jit_solution(538237937624857025)
XLA Ops:
  0.6 0.0 copy-start
  0.7 0.0 copy-start.1
  0.7 0.0 copy-start.2
  0.7 0.0 copy-start.3
  0.7 0.0 copy-start.4
  0.7 104.1 %rollout_packed.1 = (f32[4,256,256]{2,1,0:T(8,128)}, f32[8,256]{1,0:T(8,128)S(1)}, s32[1,1]{1,0:T(1,128)}) custom-call(f32[8192,256]{1,0:T(8,128)} %inputs_ref.1, f32[8192,256]{1,0:T(8,128)} %bitcast.29, s32[64,128]{1,0:T(8,128)} %bitcast.41, s32[64,128]{1,0:T(8,128)} %bitcast.43, s32[64,128]{1,0:T(8,128)} %bitcast.45, f32[2,256,256]{2,1,0:T(8,128)} %bitcast.31, ...), custom_call_target="tpu_custom_call" | custom-call | tf_op jit(solution)/shard_map/rollout_packed/pallas_call | solution.py:921
  105.5 0.0 copy-done
  105.5 0.0 copy-done.1
  105.5 0.0 copy-done.2
  105.5 0.0 copy-done.3
  105.5 0.0 copy-done.4
  105.5 0.2 conditional.1
  105.8 3.9 %update.1 = (f32[1,1]{1,0:T(1,128)}, f32[1,1]{1,0:T(1,128)}, f32[1,1]{1,0:T(1,128)}, f32[2,256,256]{2,1,0:T(8,128)}, f32[2,256,256]{2,1,0:T(8,128)}, /*index=5*/...) custom-call(f32[4,256,256]{2,1,0:T(8,128)} %get-tuple-element.62.gra, ...), custom_call_target="tpu_custom_call" | custom-call | tf_op jit(solution)/shard_map/update/pallas_call | solution.py:1095
Async XLA Ops:
  0.6 104.8 %copy-start = (f32[1,2,256,256]{3,2,1,0:T(8,128)S(1)}, f32[1,2,256,256]{3,2,1,0:T(8,128)}, u32[]{:S(2)}) copy-start(f32[1,2,256,256]{3,2,1,0:T(8,128)} %param.21) | copy-start | bytes 1572868
  0.7 104.8 %copy-start.1 = (s32[8192]{0:T(1024)S(1)}, s32[8192]{0:T(1024)}, u32[]{:S(2)}) copy-start(s32[8192]{0:T(1024)} %param.18) | copy-start | bytes 98308
  0.7 104.8 %copy-start.2 = (s32[8192]{0:T(1024)S(1)}, s32[8192]{0:T(1024)}, u32[]{:S(2)}) copy-start(s32[8192]{0:T(1024)} %param.19) | copy-start | bytes 98308
  0.7 104.8 %copy-start.3 = (s32[8192]{0:T(1024)S(1)}, s32[8192]{0:T(1024)}, u32[]{:S(2)}) copy-start(s32[8192]{0:T(1024)} %param.20) | copy-start | bytes 98308
  0.7 104.8 %copy-start.4 = (f32[1,2,256]{2,1,0:T(2,128)S(1)}, f32[1,2,256]{2,1,0:T(2,128)}, u32[]{:S(2)}) copy-start(f32[1,2,256]{2,1,0:T(2,128)} %param.23) | copy-start | bytes 6148

commit v10 on v9

--- a/solution.py
+++ b/solution.py
@@ -74,6 +74,7 @@
     down_lo,
     down_t,
     rank_ref,
+    area_ref,
     q_ref,
     scale_ref,
     weight_ref,
@@ -282,10 +283,7 @@
         area = jnp.cos(latitude) * (1.0 + land_ref[...].astype(f32))
         q_ref[0] = area * (section < length).astype(f32)
         q_ref[1] = area * (mate < length).astype(f32)
-        local_weight = jnp.sum(
-            area * jnp.minimum(length, sections).astype(f32), axis=(0, 1), keepdims=True
-        )
-        misses = jnp.zeros((1, 1), f32)
+        area_ref[...] = area
         if packing:
             beyond = length > 2
             flag = beyond.astype(bf16)
@@ -301,6 +299,16 @@
             )
             rank = jnp.where(beyond, within + before, -1e6)
             rank_ref[...] = rank
+
+    def prepare_totals():
+        length = len_ref[...]
+        local_weight = jnp.sum(
+            area_ref[...] * jnp.minimum(length, sections).astype(f32), axis=(0, 1), keepdims=True
+        )
+        misses = jnp.zeros((1, 1), f32)
+        if packing:
+            beyond = length > 2
+            rank = rank_ref[...]
             place = (
                 lax.broadcasted_iota(jnp.int32, (grid_rows, LANES), 0) * LANES
                 + lax.broadcasted_iota(jnp.int32, (grid_rows, LANES), 1)
@@ -484,6 +492,8 @@
         @pl.when(section > 0)
         def _():
             prepare_columns()
+            if not packing:
+                prepare_totals()
             if packing:
                 xout[2 * ROWS : WINDOW, :] = jnp.zeros((WINDOW - 2 * ROWS, feats), f32)
                 cin[total_packed - SPARE : total_packed, :] = jnp.zeros((SPARE, feats), f32)
@@ -532,6 +542,14 @@
             @pl.when((section == 0) & (t == 3))
             def _():
                 prepare_columns()
+                if not packing:
+                    prepare_totals()
+
+            if packing:
+
+                @pl.when(t == 3)
+                def _():
+                    prepare_totals()
 
             @pl.when(t == jnp.minimum(lag, 4))
             def _():
@@ -600,6 +618,7 @@
             for i in range(5):
                 mate_weight(i).start()
             prepare_columns()
+            prepare_totals()
             for i in range(5):
                 mate_weight(i).wait_send()
             prepare_backward()
@@ -941,6 +960,7 @@
             lows,
             lows,
             lows,
+            pltpu.VMEM((grid_rows, LANES), f32),
             pltpu.VMEM((grid_rows, LANES), f32),
             pltpu.VMEM((2, grid_rows, LANES), f32),
             pltpu.VMEM((8, LANES), f32),
@@ -1135,10 +1155,9 @@
     operands = (inputs, targets[0], lengths, lat_index, land) + state[:3]
     packed = rollout(True, sections, groups, *operands)
 
-    grads, stats, unused = lax.cond(
-        packed[2].reshape(()) > 0,
-        lambda: rollout(False, sections, groups, *operands),
-        lambda: packed,
+    grads, stats, unused = lax.switch(
+        packed[2].reshape(()),
+        (lambda: packed, lambda: rollout(False, sections, groups, *operands)),
     )
     new = update(grads, stats, *state)
     return tuple(a.reshape(()) for a in new[:3]) + tuple(a[None] for a in new[3:])

time: 110 us -> 110 us (level)
  no operation moved by 1% of the time
where the time goes in v10:
time: 110 us
  Pallas kernels  108 us (98%)
  between operations  1.55 us (1%)
    pallas_call x1, Pallas kernels, rollout(): pl.pallas_call(functools.partial(rollout_kernel, sections, groups, packin...  104 us
    pallas_call x1, Pallas kernels, update(): pl.pallas_call(update_kernel, in_specs=[hbm] * 11, out_specs=(vmem,) * 3...  3.92 us

profile of v10, /device:TPU:0, one launch (start us, length us, event | category | flops | bytes accessed | tf_op | source)
XLA Modules:
  0.0 109.5 jit_solution(13028663813291156673)
XLA Ops:
  0.6 0.0 copy-start
  0.7 0.0 copy-start.1
  0.7 0.0 copy-start.2
  0.7 0.0 copy-start.3
  0.7 0.0 copy-start.4
  0.7 103.8 %rollout_packed.1 = (f32[4,256,256]{2,1,0:T(8,128)}, f32[8,256]{1,0:T(8,128)S(1)}, s32[1,1]{1,0:T(1,128)}) custom-call(f32[8192,256]{1,0:T(8,128)} %inputs_ref.1, f32[8192,256]{1,0:T(8,128)} %bitcast.29, s32[64,128]{1,0:T(8,128)} %bitcast.41, s32[64,128]{1,0:T(8,128)} %bitcast.43, s32[64,128]{1,0:T(8,128)} %bitcast.45, f32[2,256,256]{2,1,0:T(8,128)} %bitcast.31, ...), custom_call_target="tpu_custom_call" | custom-call | tf_op jit(solution)/shard_map/rollout_packed/pallas_call | solution.py:940
  105.1 0.0 copy-done
  105.1 0.0 copy-done.1
  105.1 0.0 copy-done.2
  105.1 0.0 copy-done.3
  105.2 0.0 copy-done.4
  105.2 0.2 conditional.1
  105.4 3.9 %update.1 = (f32[1,1]{1,0:T(1,128)}, f32[1,1]{1,0:T(1,128)}, f32[1,1]{1,0:T(1,128)}, f32[2,256,256]{2,1,0:T(8,128)}, f32[2,256,256]{2,1,0:T(8,128)}, /*index=5*/...) custom-call(f32[4,256,256]{2,1,0:T(8,128)} %get-tuple-element.62.gra, ...), custom_call_target="tpu_custom_call" | custom-call | tf_op jit(solution)/shard_map/update/pallas_call | solution.py:1115
Async XLA Ops:
  0.6 104.5 %copy-start = (f32[1,2,256,256]{3,2,1,0:T(8,128)S(1)}, f32[1,2,256,256]{3,2,1,0:T(8,128)}, u32[]{:S(2)}) copy-start(f32[1,2,256,256]{3,2,1,0:T(8,128)} %param.21) | copy-start | bytes 1572868
  0.7 104.5 %copy-start.1 = (s32[8192]{0:T(1024)S(1)}, s32[8192]{0:T(1024)}, u32[]{:S(2)}) copy-start(s32[8192]{0:T(1024)} %param.18) | copy-start | bytes 98308
  0.7 104.5 %copy-start.2 = (s32[8192]{0:T(1024)S(1)}, s32[8192]{0:T(1024)}, u32[]{:S(2)}) copy-start(s32[8192]{0:T(1024)} %param.19) | copy-start | bytes 98308
  0.7 104.5 %copy-start.3 = (s32[8192]{0:T(1024)S(1)}, s32[8192]{0:T(1024)}, u32[]{:S(2)}) copy-start(s32[8192]{0:T(1024)} %param.20) | copy-start | bytes 98308
  0.7 104.5 %copy-start.4 = (f32[1,2,256]{2,1,0:T(2,128)S(1)}, f32[1,2,256]{2,1,0:T(2,128)}, u32[]{:S(2)}) copy-start(f32[1,2,256]{2,1,0:T(2,128)} %param.23) | copy-start | bytes 6148
